TPU v7x, 32 devices: a whole 2x2x4 slice. The times are simulated.
32 devices in a mesh: ens: 2 (over y), comp: 4 (over z), lat: 2 (over x), lon: 2 (over core).
Axes of the slice: x: 2, y: 2, z: 4, core: 2. Of those that a mesh axis runs over, the one named last changes fastest.
Arguments:
- spectrum: float32 [2304, 16, 256], P(('ens', 'comp'), 'lat', 'lon'), parts along dimension 0, may hold values from 0 to 2
- sea_mask: int32 [16, 256], P('lat', 'lon'), may hold values 0 or 1
- depth_class: int32 [16, 256], P('lat', 'lon'), may hold values from 0 to 15
- current_class: int32 [16, 256], P('lat', 'lon'), may hold values from 0 to 15
- speed_table: float32 [16, 32], replicated, may hold values from 0.1 to 0.5
- current_table: float32 [16, 2], replicated, may hold values from -0.14 to 0.14
- coupling: float32 [1152], replicated, may hold values from 0.05 to 0.5
- quad_index: int32 [2, 1152, 4], replicated, may hold values from 0 to 1151, as said below
- quad_weight: float32 [2, 1152, 4], replicated, may hold values from 0 to 1, as said below
Outputs:
- spectrum_out: float32 [2304, 16, 256], P(('ens', 'comp'), 'lat', 'lon'), parts along dimension 0
There are 2 independent parts, one for each index of `ens`. A program takes and returns all parts, laid end to end along the dimension named above; an argument that names none is the same for every part. Nothing has to cross between parts.
Inputs may be any that keep to these rules, and one draw needn't show every extreme that they name: `quad_index`: for each side (0 plus, 1 minus) and component k the four entries are distinct components: two adjacent frequencies crossed with two adjacent directions, directions counted modulo 36; a component's number is its frequency times 36 plus its direction. `quad_weight`: the four weights of each side and component are non-negative and sum to one.
All inputs are finite; a program needn't handle non-finite values. No bound on the sum of `sea_mask` on one device may be relied on, other than what follows from the above.
Results may differ from a plain program's by a relative error of at most 0.002.
Values sent between devices are 32-bit elements; how exact they have to be, the bound alone decides.
No kernel may reach another device: no remote copies, remote signals or barrier semaphores. Data moves between devices by JAX's collectives and lax.ppermute only.
A program may use at most 64 MiB of HBM per device.

v0:
```python
import math

import jax
import jax.numpy as jnp
from jax import lax
from jax.sharding import PartitionSpec as P

NDIR = 36
SUBSTEPS = 4


plus_factor = 0.4096
minus_factor = 3.160494
cross_factor = 2.007843


def with_halo(block, sides, width):
    for axis, dim in sides:
        count = lax.axis_size(axis)
        forward = [(i, i + 1) for i in range(count - 1)]
        forward.append((count - 1, 0))
        backward = [(target, source) for source, target in forward]
        low = lax.ppermute(
            lax.slice_in_dim(block, block.shape[dim] - width, None, axis=dim), axis, forward
        )
        high = lax.ppermute(lax.slice_in_dim(block, 0, width, axis=dim), axis, backward)
        block = jnp.concatenate([low, block, high], axis=dim)
    return block


def minmod(former, latter):
    return jnp.maximum(0.0, jnp.minimum(former, latter)) + jnp.minimum(
        0.0, jnp.maximum(former, latter)
    )


def part_of(array, start, length, axis):
    return lax.slice_in_dim(array, start, start + length, axis=axis)


def face_flux(energy, cour, wet_cells, axis):
    length = energy.shape[axis]
    differences = part_of(energy, 1, length - 1, axis) - part_of(energy, 0, length - 1, axis)
    slopes = minmod(
        part_of(differences, 1, length - 2, axis), part_of(differences, 0, length - 2, axis)
    )
    face_count = length - 3
    face_speed = (
        0.5
        * (part_of(cour, 1, face_count, axis) + part_of(cour, 2, face_count, axis))
        * (part_of(wet_cells, 1, face_count, axis) * part_of(wet_cells, 2, face_count, axis))
    )
    upwind_left = part_of(energy, 1, face_count, axis) + 0.5 * (1.0 - face_speed) * part_of(
        slopes, 0, face_count, axis
    )
    upwind_right = part_of(energy, 2, face_count, axis) - 0.5 * (1.0 + face_speed) * part_of(
        slopes, 1, face_count, axis
    )
    return jnp.maximum(face_speed, 0.0) * upwind_left + jnp.minimum(face_speed, 0.0) * upwind_right


def advance(energy, cour_x, cour_y, wet_cells):
    flux_lon = face_flux(energy[:, 2:-2, :], cour_x[:, 2:-2, :], wet_cells[:, 2:-2, :], 2)
    flux_lat = face_flux(energy[:, :, 2:-2], cour_y[:, :, 2:-2], wet_cells[:, :, 2:-2], 1)
    return (
        energy[:, 2:-2, 2:-2]
        - (flux_lon[:, :, 1:] - flux_lon[:, :, :-1])
        - (flux_lat[:, 1:, :] - flux_lat[:, :-1, :])
    )


def courant(comp_ids, depth_grid, current_grid, speed_table, current_table):
    n_depth, n_freq = speed_table.shape
    n_current = current_table.shape[0]
    depth_hot = (depth_grid[None] == jnp.arange(n_depth, dtype=jnp.int32)[:, None, None]).astype(
        jnp.float32
    )
    current_hot = (
        current_grid[None] == jnp.arange(n_current, dtype=jnp.int32)[:, None, None]
    ).astype(jnp.float32)
    freq_hot = ((comp_ids // NDIR)[:, None] == jnp.arange(n_freq, dtype=jnp.int32)[None, :]).astype(
        jnp.float32
    )
    comp_speed = jnp.dot(freq_hot, speed_table.T, precision=lax.Precision.HIGHEST)
    speeds = jnp.einsum("kn,nhw->khw", comp_speed, depth_hot, precision=lax.Precision.HIGHEST)
    current_uv = jnp.einsum(
        "nc,nhw->chw", current_table, current_hot, precision=lax.Precision.HIGHEST
    )
    angles = 2.0 * math.pi / NDIR * (comp_ids % NDIR).astype(jnp.float32)
    cour_x = speeds * jnp.cos(angles)[:, None, None] + current_uv[0]
    cour_y = speeds * jnp.sin(angles)[:, None, None] + current_uv[1]
    return (cour_x, cour_y)


def dense_kernel(table_index, table_weight):
    comp_total = table_index.shape[0]
    columns = jnp.arange(comp_total, dtype=jnp.int32)[None, :]
    weights = table_weight.astype(jnp.bfloat16)
    kernel = jnp.where(columns == table_index[:, 3:4], weights[:, 3:4], jnp.zeros((), jnp.bfloat16))
    for corner in (2, 1, 0):
        kernel = jnp.where(
            columns == table_index[:, corner : corner + 1], weights[:, corner : corner + 1], kernel
        )
    return kernel


def interact(energy, kernel_plus, kernel_minus, coupling):
    energy_low = energy.astype(jnp.bfloat16)
    plus_side = jnp.dot(kernel_plus, energy_low, preferred_element_type=jnp.float32)
    minus_side = jnp.dot(kernel_minus, energy_low, preferred_element_type=jnp.float32)
    source = coupling[:, None] * (
        energy * energy * (plus_factor * plus_side + minus_factor * minus_side)
        - cross_factor * energy * plus_side * minus_side
    )
    source_low = source.astype(jnp.bfloat16)
    contract = (((0,), (0,)), ((), ()))
    net_gain = (
        lax.dot_general(kernel_plus, source_low, contract, preferred_element_type=jnp.float32)
        + lax.dot_general(kernel_minus, source_low, contract, preferred_element_type=jnp.float32)
        - 2.0 * source
    )
    return energy + net_gain / (1.0 + jnp.abs(net_gain))


def window(array, offset):
    return array[:, offset : array.shape[1] - offset, offset : array.shape[2] - offset]


def local(
    spectrum,
    sea_mask,
    depth_class,
    current_class,
    speed_table,
    current_table,
    coupling,
    quad_index,
    quad_weight,
):
    comps_local, lat_rows, lon_cols = spectrum.shape
    n_comp = lax.axis_size("comp")
    n_lat = lax.axis_size("lat")
    deep_rim = 2 * SUBSTEPS
    stacked = jnp.stack([sea_mask, depth_class, current_class])
    padded = with_halo(stacked, (("lat", 1), ("lon", 2)), deep_rim)
    row_global = (
        lax.axis_index("lat") * lat_rows
        - deep_rim
        + jnp.arange(lat_rows + 2 * deep_rim, dtype=jnp.int32)
    )
    inside = ((row_global >= 0) & (row_global < lat_rows * n_lat)).astype(jnp.float32)[:, None]
    wet_rim = (padded[0].astype(jnp.float32) * inside)[None]
    comp_ids = lax.axis_index("comp") * comps_local + jnp.arange(comps_local, dtype=jnp.int32)
    cour_x, cour_y = courant(comp_ids, padded[1], padded[2], speed_table, current_table)
    energy = spectrum * sea_mask.astype(jnp.float32)[None]
    inner_rows = inside[deep_rim - 2 : deep_rim + lat_rows + 2]
    offset = deep_rim - 2
    for substep in range(SUBSTEPS):
        rimmed = with_halo(energy, (("lat", 1), ("lon", 2)), 2) * inner_rows[None]
        energy = advance(
            rimmed, window(cour_x, offset), window(cour_y, offset), window(wet_rim, offset)
        )
    kernel_plus = dense_kernel(quad_index[0], quad_weight[0])
    kernel_minus = dense_kernel(quad_index[1], quad_weight[1])
    cell_count = lat_rows * lon_cols
    outgoing = energy.reshape(comps_local, n_comp, cell_count // n_comp)
    pieces = lax.all_to_all(outgoing, "comp", split_axis=1, concat_axis=0, tiled=True)
    point_grid = pieces.reshape(pieces.shape[0], pieces.shape[2])
    arrived = interact(point_grid, kernel_plus, kernel_minus, coupling).reshape(pieces.shape)
    returned = lax.all_to_all(arrived, "comp", split_axis=0, concat_axis=1, tiled=True)
    return returned.reshape(comps_local, lat_rows, lon_cols)


def solution(mesh):
    placed = (
        P(("ens", "comp"), "lat", "lon"),
        P("lat", "lon"),
        P("lat", "lon"),
        P("lat", "lon"),
        P(),
        P(),
        P(),
        P(),
        P(),
    )
    return jax.shard_map(
        local,
        mesh=mesh,
        in_specs=placed,
        out_specs=P(("ens", "comp"), "lat", "lon"),
        check_vma=False,
    )
```

profile of v0, /device:TPU:0, one launch (start us, length us, event | category | flops | bytes accessed | tf_op | source)
XLA Modules:
  0.0 197.4 jit_solution(13081938902043382700)
XLA Ops:
  0.0 0.7 pad_add_fusion.2
  0.7 2.9 %collective-permute-start.4 = (s32[3,8,128]{2,1,0:T(8,128)S(1)}, s32[3,8,128]{2,1,0:T(8,128)S(1)}, u32[]{:S(2)}, u32[]{:S(2)}) collective-permute-start(s32[3,8,128]{2,1,0:T(8,128)S(1)} %pad_add_fusion.2), channel_id=1, source_target_pairs={{0,2},{2,0},{1,3},{3,1},{4,6},{6,4},{5,7},{7,5},{8,10},{10,8},{9,1... | collective-permute-start | bytes 36872 | tf_op jit(solution)/shard_map/ppermute | solution.py:23
  3.7 0.7 convert_element_type.41
  4.4 1.7 copy.13
  6.5 2.1 %collective-permute-start = (f32[288,2,128]{0,2,1:T(8,128)S(1)}, f32[288,2,128]{0,2,1:T(8,128)S(1)}, u32[]{:S(2)}, u32[]{:S(2)}) collective-permute-start(f32[288,2,128]{0,2,1:T(8,128)S(1)} %get-tuple-element.41), channel_id=1, source_target_pairs={{0,2},{2,0},{1,3},{3,1},{4,6},{6,4},{5,7},{7,5},{8,10},{10,8},{9,1... | collective-permute-start | bytes 884744 | tf_op jit(solution)/shard_map/ppermute | solution.py:23
  9.1 0.5 collective-permute-start.7
  9.7 0.6 collective-permute-done.6
  10.9 3.2 %multiply_add_fusion.1 = (f32[288,24,144]{0,2,1:T(8,128)S(1)}, f32[288,24,144]{0,2,1:T(8,128)S(1)}) fusion(f32[24,144]{1,0:T(8,128)S(1)} %get-tuple-element.62, f32[288]{0:T(512)S(1)} %get-tuple-element.64, f32[24,144]{1,0:T(8,128)S(1)} %get-tuple-element.61, f32[288]{0:T(512)S(1)} %get-tuple-element.63, f32[288,16,1]{0,1,2:T(8,128)S(1)} %convolution_bitcast_fusion.1, ...), kind=kOutput, calls=%fused_computation.9 | convolution fusion | flops 195139584 | bytes 8024832 | tf_op jit(solution)/shard_map/kn,nhw->khw/dot_general | solution.py:85
  14.3 4.3 %collective-permute-done = f32[288,2,128]{0,2,1:T(8,128)S(1)} collective-permute-done((f32[288,2,128]{0,2,1:T(8,128)S(1)}, f32[288,2,128]{0,2,1:T(8,128)S(1)}, u32[]{:S(2)}, u32[]{:S(2)}) %collective-permute-start) | collective-permute-done | bytes 294944 | tf_op jit(solution)/shard_map/ppermute | solution.py:23
  18.6 7.0 %collective-permute-done.1 = f32[288,2,128]{0,2,1:T(8,128)S(1)} collective-permute-done((f32[288,2,128]{0,2,1:T(8,128)S(1)}, f32[288,2,128]{0,2,1:T(8,128)S(1)}, u32[]{:S(2)}, u32[]{:S(2)}) %collective-permute-start.1) | collective-permute-done | bytes 294944 | tf_op jit(solution)/shard_map/ppermute | solution.py:26
  25.6 0.5 collective-permute-start.3
  26.2 0.6 collective-permute-done.2
  27.0 0.3 maximum_multiply_fusion
  27.8 0.4 minimum_add_fusion.7
  28.2 0.3 minimum_add_fusion.3
  28.5 1.4 fusion.47
  30.0 1.6 fusion.26
  31.6 0.4 fusion.57
  32.1 1.8 collective-permute-start.8
  33.8 0.3 collective-permute-start.9
  34.2 9.9 %collective-permute-done.8 = f32[288,2,128]{0,2,1:T(8,128)S(1)} collective-permute-done((f32[288,2,128]{0,2,1:T(8,128)S(1)}, f32[288,2,128]{0,2,1:T(8,128)S(1)}, u32[]{:S(2)}, u32[]{:S(2)}) %collective-permute-start.8) | collective-permute-done | bytes 294944 | tf_op jit(solution)/shard_map/ppermute | solution.py:23
  44.1 7.9 %collective-permute-done.9 = f32[288,2,128]{0,2,1:T(8,128)S(1)} collective-permute-done((f32[288,2,128]{0,2,1:T(8,128)S(1)}, f32[288,2,128]{0,2,1:T(8,128)S(1)}, u32[]{:S(2)}, u32[]{:S(2)}) %collective-permute-start.9) | collective-permute-done | bytes 294944 | tf_op jit(solution)/shard_map/ppermute | solution.py:26
  52.0 0.5 collective-permute-start.11
  52.5 0.7 collective-permute-done.10
  53.4 0.3 maximum_multiply_fusion.1
  54.2 0.4 minimum_add_fusion.6
  54.6 0.3 minimum_add_fusion.2
  54.9 1.0 fusion.42
  55.9 0.9 fusion.21
  56.8 0.4 fusion.55
  57.3 1.8 collective-permute-start.12
  59.1 0.3 collective-permute-start.13
  59.4 9.9 %collective-permute-done.12 = f32[288,2,128]{0,2,1:T(8,128)S(1)} collective-permute-done((f32[288,2,128]{0,2,1:T(8,128)S(1)}, f32[288,2,128]{0,2,1:T(8,128)S(1)}, u32[]{:S(2)}, u32[]{:S(2)}) %collective-permute-start.12) | collective-permute-done | bytes 294944 | tf_op jit(solution)/shard_map/ppermute | solution.py:23
  69.3 7.9 %collective-permute-done.13 = f32[288,2,128]{0,2,1:T(8,128)S(1)} collective-permute-done((f32[288,2,128]{0,2,1:T(8,128)S(1)}, f32[288,2,128]{0,2,1:T(8,128)S(1)}, u32[]{:S(2)}, u32[]{:S(2)}) %collective-permute-start.13) | collective-permute-done | bytes 294944 | tf_op jit(solution)/shard_map/ppermute | solution.py:26
  77.3 0.5 collective-permute-start.15
  77.8 0.7 collective-permute-done.14
  78.6 0.3 maximum_multiply_fusion.2
  79.4 0.4 minimum_add_fusion.5
  79.8 1.0 fusion.37
  80.8 0.3 minimum_add_fusion.1
  81.2 0.9 fusion.16
  82.0 0.4 fusion.53
  82.5 1.8 collective-permute-start.16
  84.6 9.9 %collective-permute-done.16 = f32[288,2,128]{0,2,1:T(8,128)S(1)} collective-permute-done((f32[288,2,128]{0,2,1:T(8,128)S(1)}, f32[288,2,128]{0,2,1:T(8,128)S(1)}, u32[]{:S(2)}, u32[]{:S(2)}) %collective-permute-start.16) | collective-permute-done | bytes 294944 | tf_op jit(solution)/shard_map/ppermute | solution.py:23
  94.5 7.9 %collective-permute-done.17 = f32[288,2,128]{0,2,1:T(8,128)S(1)} collective-permute-done((f32[288,2,128]{0,2,1:T(8,128)S(1)}, f32[288,2,128]{0,2,1:T(8,128)S(1)}, u32[]{:S(2)}, u32[]{:S(2)}) %collective-permute-start.17) | collective-permute-done | bytes 294944 | tf_op jit(solution)/shard_map/ppermute | solution.py:26
  102.5 0.5 collective-permute-start.19
  103.0 0.7 collective-permute-done.18
  103.9 0.3 maximum_multiply_fusion.3
  104.6 0.4 minimum_add_fusion.4
  105.0 1.0 fusion.32
  106.1 0.5 minimum_add_fusion
  106.6 0.9 fusion.11
  107.5 0.4 fusion.51
  107.9 1.5 copy.14
  109.4 5.2 %all-to-all-start = ((f32[288,4,256]{2,0,1:T(8,128)}), f32[288,4,256]{2,0,1:T(8,128)S(1)}, u32[]{:S(2)}, u32[]{:S(2)}) async-start(f32[288,4,256]{2,0,1:T(8,128)} %copy.14), calls=%async_computation | async-start | bytes 2359296 | tf_op jit(solution)/shard_map/all_to_all | solution.py:167
  114.9 28.8 %all-to-all-done = f32[288,4,256]{2,0,1:T(8,128)S(1)} async-done(((f32[288,4,256]{2,0,1:T(8,128)}), f32[288,4,256]{2,0,1:T(8,128)S(1)}, u32[]{:S(2)}, u32[]{:S(2)}) %all-to-all-start) | async-done | bytes 1179680 | tf_op jit(solution)/shard_map/all_to_all | solution.py:167
  143.7 4.3 %fusion.72 = f32[1152,256]{1,0:T(8,128)S(1)} fusion(bf16[1152,256]{1,0:T(8,128)(2,1)S(1)} %bitcast_convert_fusion, s32[1152]{0:T(1024)S(1)} %get-tuple-element.55, s32[1152]{0:T(1024)S(1)} %get-tuple-element.54, s32[1152]{0:T(1024)S(1)} %get-tuple-element.53, s32[1152]{0:T(1024)S(1)} %get-tuple-element.56, bf16[1152]{0:T(1024)(128)(2,1)S(1)} %get-tuple-element.59, ...), kind=kOutput, calls=%fused_computation.132 | convolution fusion | flops 690094080 | bytes 1797120 | tf_op jit(solution)/shard_map/dot_general | solution.py:109
  148.1 4.6 %fusion.61 = f32[1152,256]{1,0:T(8,128)S(1)} fusion(f32[288,4,256]{2,0,1:T(8,128)S(1)} %all-to-all-done, f32[1152,256]{1,0:T(8,128)S(1)} %fusion.72, bf16[1152,256]{1,0:T(8,128)(2,1)S(1)} %bitcast_convert_fusion, s32[1152]{0:T(1024)S(1)} %get-tuple-element.6, s32[1152]{0:T(1024)S(1)} %get-tuple-element.7, s32[1152]{0:T(1024)S(1)} %get-tuple-element.8, ...), kind=kOutput, calls=%fused_computation.126 | convolution fusion | flops 693043200 | bytes 4161024 | tf_op jit(solution)/shard_map/dot_general | solution.py:110
  152.6 3.4 %fusion.70 = f32[1152,256]{1,0:T(8,128)S(1)} fusion(s32[1152]{0:T(1024)S(1)} %get-tuple-element.55, s32[1152]{0:T(1024)S(1)} %get-tuple-element.54, s32[1152]{0:T(1024)S(1)} %get-tuple-element.53, s32[1152]{0:T(1024)S(1)} %get-tuple-element.56, bf16[1152]{0:T(1024)(128)(2,1)S(1)} %get-tuple-element.59, bf16[1152]{0:T(1024)(128)(2,1)S(1)} %get-tuple-element.58, ...), kind=kOutput, calls=%fused_computation.131 | convolution fusion | flops 690388992 | bytes 2386944 | tf_op jit(solution)/shard_map/dot_general | solution.py:118
  156.0 3.6 %fusion.64 = f32[1152,1,256]{2,0,1:T(8,128)S(1)} fusion(f32[1152,256]{1,0:T(8,128)S(1)} %fusion.70, f32[288,4,256]{2,0,1:T(8,128)S(1)} %all-to-all-done, f32[1152,256]{1,0:T(8,128)S(1)} %fusion.61, s32[1152]{0:T(1024)S(1)} %get-tuple-element.6, s32[1152]{0:T(1024)S(1)} %get-tuple-element.7, s32[1152]{0:T(1024)S(1)} %get-tuple-element.8, ...), kind=kOutput, calls=%fused_computation.129 | convolution fusion | flops 692453376 | bytes 4746240 | tf_op jit(solution)/shard_map/dot_general | solution.py:119
  159.6 4.9 %copy.15 = f32[1152,1,256]{2,1,0:T(1,128)S(1)} copy(f32[1152,1,256]{2,0,1:T(8,128)S(1)} %fusion.64) | data formatting | bytes 2359296 | tf_op jit(solution)/shard_map/reshape | solution.py:169
  164.5 30.6 %all_to_all.30 = f32[1152,1,256]{2,1,0:T(1,128)S(1)} all-to-all(f32[1152,1,256]{2,1,0:T(1,128)S(1)} %copy.15), channel_id=1, replica_groups=mesh['ens'=2,'comp'=4,'lat'=2,'lon'=2] {'comp'}, dimensions={0} | all-to-all | bytes 2359296 | tf_op jit(solution)/shard_map/all_to_all | solution.py:170
  195.1 0.8 copy.16
  195.9 1.5 reshape.71
  (71 shorter events, 5.2 us)
Async XLA Ops:
  0.0 8.6 %copy-start = (f32[16,32]{1,0:T(8,128)S(1)}, f32[16,32]{1,0:T(8,128)}, u32[]{:S(2)}) copy-start(f32[16,32]{1,0:T(8,128)} %param.13) | copy-start | bytes 6148
  0.7 8.2 %collective-permute-start.4 = (s32[3,8,128]{2,1,0:T(8,128)S(1)}, s32[3,8,128]{2,1,0:T(8,128)S(1)}, u32[]{:S(2)}, u32[]{:S(2)}) collective-permute-start(s32[3,8,128]{2,1,0:T(8,128)S(1)} %pad_add_fusion.2), channel_id=1, source_target_pairs={{0,2},{2,0},{1,3},{3,1},{4,6},{6,4},{5,7},{7,5},{8,10},{10,8},{9,1... | collective-permute-start | bytes 36872 | tf_op jit(solution)/shard_map/ppermute | solution.py:23
  3.7 5.3 %collective-permute-start.5 = (s32[3,8,128]{2,1,0:T(8,128)S(1)}, s32[3,8,128]{2,1,0:T(8,128)S(1)}, u32[]{:S(2)}, u32[]{:S(2)}) collective-permute-start(s32[3,8,128]{2,1,0:T(8,128)S(1)} %pad_add_fusion.2), channel_id=1, source_target_pairs={{2,0},{0,2},{3,1},{1,3},{6,4},{4,6},{7,5},{5,7},{10,8},{8,10},{11,... | collective-permute-start | bytes 36872 | tf_op jit(solution)/shard_map/ppermute | solution.py:26
  6.1 2.8 %copy-start.2 = (s32[8,128]{1,0:T(8,128)S(1)}, s32[8,128]{1,0:T(8,128)}, u32[]{:S(2)}) copy-start(s32[8,128]{1,0:T(8,128)} %param.10) | copy-start | bytes 12292
  6.2 2.8 %copy-start.3 = (s32[8,128]{1,0:T(8,128)S(1)}, s32[8,128]{1,0:T(8,128)}, u32[]{:S(2)}) copy-start(s32[8,128]{1,0:T(8,128)} %param.12) | copy-start | bytes 12292
  6.2 2.8 %copy-start.4 = (s32[8,128]{1,0:T(8,128)S(1)}, s32[8,128]{1,0:T(8,128)}, u32[]{:S(2)}) copy-start(s32[8,128]{1,0:T(8,128)} %param.11) | copy-start | bytes 12292
  6.4 4.2 %copy-start.8 = (f32[16,2]{0,1:T(2,128)S(1)}, f32[16,2]{0,1:T(2,128)}, u32[]{:S(2)}) copy-start(f32[16,2]{0,1:T(2,128)} %param.14) | copy-start | bytes 388
  6.5 12.1 %collective-permute-start = (f32[288,2,128]{0,2,1:T(8,128)S(1)}, f32[288,2,128]{0,2,1:T(8,128)S(1)}, u32[]{:S(2)}, u32[]{:S(2)}) collective-permute-start(f32[288,2,128]{0,2,1:T(8,128)S(1)} %get-tuple-element.41), channel_id=1, source_target_pairs={{0,2},{2,0},{1,3},{3,1},{4,6},{6,4},{5,7},{7,5},{8,10},{10,8},{9,1... | collective-permute-start | bytes 884744 | tf_op jit(solution)/shard_map/ppermute | solution.py:23
  8.5 17.0 %collective-permute-start.1 = (f32[288,2,128]{0,2,1:T(8,128)S(1)}, f32[288,2,128]{0,2,1:T(8,128)S(1)}, u32[]{:S(2)}, u32[]{:S(2)}) collective-permute-start(f32[288,2,128]{0,2,1:T(8,128)S(1)} %get-tuple-element.42), channel_id=1, source_target_pairs={{2,0},{0,2},{3,1},{1,3},{6,4},{4,6},{7,5},{5,7},{10,8},{8,10},{11,... | collective-permute-start | bytes 884744 | tf_op jit(solution)/shard_map/ppermute | solution.py:26
  9.1 1.2 collective-permute-start.6
  9.1 1.4 collective-permute-start.7
  25.6 1.3 collective-permute-start.2
  25.6 1.4 collective-permute-start.3
  32.1 12.0 %collective-permute-start.8 = (f32[288,2,128]{0,2,1:T(8,128)S(1)}, f32[288,2,128]{0,2,1:T(8,128)S(1)}, u32[]{:S(2)}, u32[]{:S(2)}) collective-permute-start(f32[288,2,128]{0,2,1:T(8,128)S(1)} %get-tuple-element.39), channel_id=1, source_target_pairs={{0,2},{2,0},{1,3},{3,1},{4,6},{6,4},{5,7},{7,5},{8,10},{10,8},{9,1... | collective-permute-start | bytes 884744 | tf_op jit(solution)/shard_map/ppermute | solution.py:23
  33.8 18.1 %collective-permute-start.9 = (f32[288,2,128]{0,2,1:T(8,128)S(1)}, f32[288,2,128]{0,2,1:T(8,128)S(1)}, u32[]{:S(2)}, u32[]{:S(2)}) collective-permute-start(f32[288,2,128]{0,2,1:T(8,128)S(1)} %get-tuple-element.40), channel_id=1, source_target_pairs={{2,0},{0,2},{3,1},{1,3},{6,4},{4,6},{7,5},{5,7},{10,8},{8,10},{11,... | collective-permute-start | bytes 884744 | tf_op jit(solution)/shard_map/ppermute | solution.py:26
  52.0 1.3 collective-permute-start.10
  52.0 1.4 collective-permute-start.11
  57.3 12.0 %collective-permute-start.12 = (f32[288,2,128]{0,2,1:T(8,128)S(1)}, f32[288,2,128]{0,2,1:T(8,128)S(1)}, u32[]{:S(2)}, u32[]{:S(2)}) collective-permute-start(f32[288,2,128]{0,2,1:T(8,128)S(1)} %get-tuple-element.37), channel_id=1, source_target_pairs={{0,2},{2,0},{1,3},{3,1},{4,6},{6,4},{5,7},{7,5},{8,10},{10,8},{9,1... | collective-permute-start | bytes 884744 | tf_op jit(solution)/shard_map/ppermute | solution.py:23
  59.1 18.1 %collective-permute-start.13 = (f32[288,2,128]{0,2,1:T(8,128)S(1)}, f32[288,2,128]{0,2,1:T(8,128)S(1)}, u32[]{:S(2)}, u32[]{:S(2)}) collective-permute-start(f32[288,2,128]{0,2,1:T(8,128)S(1)} %get-tuple-element.38), channel_id=1, source_target_pairs={{2,0},{0,2},{3,1},{1,3},{6,4},{4,6},{7,5},{5,7},{10,8},{8,10},{11,... | collective-permute-start | bytes 884744 | tf_op jit(solution)/shard_map/ppermute | solution.py:26
  77.2 1.3 collective-permute-start.14
  77.3 1.4 collective-permute-start.15
  82.5 12.0 %collective-permute-start.16 = (f32[288,2,128]{0,2,1:T(8,128)S(1)}, f32[288,2,128]{0,2,1:T(8,128)S(1)}, u32[]{:S(2)}, u32[]{:S(2)}) collective-permute-start(f32[288,2,128]{0,2,1:T(8,128)S(1)} %get-tuple-element.35), channel_id=1, source_target_pairs={{0,2},{2,0},{1,3},{3,1},{4,6},{6,4},{5,7},{7,5},{8,10},{10,8},{9,1... | collective-permute-start | bytes 884744 | tf_op jit(solution)/shard_map/ppermute | solution.py:23
  84.3 18.1 %collective-permute-start.17 = (f32[288,2,128]{0,2,1:T(8,128)S(1)}, f32[288,2,128]{0,2,1:T(8,128)S(1)}, u32[]{:S(2)}, u32[]{:S(2)}) collective-permute-start(f32[288,2,128]{0,2,1:T(8,128)S(1)} %get-tuple-element.36), channel_id=1, source_target_pairs={{2,0},{0,2},{3,1},{1,3},{6,4},{4,6},{7,5},{5,7},{10,8},{8,10},{11,... | collective-permute-start | bytes 884744 | tf_op jit(solution)/shard_map/ppermute | solution.py:26
  102.4 1.3 collective-permute-start.18
  102.5 1.4 collective-permute-start.19
  109.4 5.2 %copy-start.5 = (f32[2,1152,4]{1,2,0:T(4,128)S(1)}, f32[2,1152,4]{1,2,0:T(4,128)}, u32[]{:S(2)}) copy-start(f32[2,1152,4]{1,2,0:T(4,128)} %param.17) | copy-start | bytes 110596
  109.4 5.4 %copy-start.6 = (s32[2,1152,4]{1,2,0:T(4,128)S(1)}, s32[2,1152,4]{1,2,0:T(4,128)}, u32[]{:S(2)}) copy-start(s32[2,1152,4]{1,2,0:T(4,128)} %param.16) | copy-start | bytes 110596
  109.4 34.3 %all-to-all-start = ((f32[288,4,256]{2,0,1:T(8,128)}), f32[288,4,256]{2,0,1:T(8,128)S(1)}, u32[]{:S(2)}, u32[]{:S(2)}) async-start(f32[288,4,256]{2,0,1:T(8,128)} %copy.14), calls=%async_computation | async-start | bytes 2359296 | tf_op jit(solution)/shard_map/all_to_all | solution.py:167
  143.7 4.4 %copy-start.7 = (f32[1152]{0:T(1024)S(1)}, f32[1152]{0:T(1024)}, u32[]{:S(2)}) copy-start(f32[1152]{0:T(1024)} %param.15) | copy-start | bytes 13828
  195.1 2.3 %copy-start.1 = (f32[16,32]{1,0:T(8,128)S(1)}, f32[16,32]{1,0:T(8,128)}, u32[]{:S(2)}) copy-start(f32[16,32]{1,0:T(8,128)} %param.13) | copy-start | bytes 6148
where the time goes:
time: 198 us; the launch traced here: 197 us
  waiting for transfers between devices  97.5 us (49%)
  blocking collectives  30.6 us (15%)
  matrix products  19.6 us (10%)
  starting transfers between devices  19.4 us (10%)
  other arithmetic  18.7 us (9%)
  local copies, waits for them, and re-layouts  11 us (6%)
    ppermute x10, waiting for transfers between devices, with_halo(): lax.ppermute(lax.slice_in_dim(block, block.shape[dim] - width, None, axis...  37.3 us
    ppermute x10, waiting for transfers between devices, with_halo(): lax.ppermute(lax.slice_in_dim(block, 0, width, axis=dim), axis, backward)  31.4 us
    all_to_all x1, blocking collectives, local(): lax.all_to_all(arrived, 'comp', split_axis=0, concat_axis=1, tiled=True)  30.6 us
    all_to_all x1, waiting for transfers between devices, local(): lax.all_to_all(outgoing, 'comp', split_axis=1, concat_axis=0, tiled=True)  28.8 us
    ppermute x10, starting transfers between devices, with_halo(): lax.ppermute(lax.slice_in_dim(block, block.shape[dim] - width, None, axis...  10.6 us
    add x8, other arithmetic, face_flux(): jnp.maximum(face_speed, 0.0) * upwind_left  8.76 us
    all_to_all x1, starting transfers between devices, local(): lax.all_to_all(outgoing, 'comp', split_axis=1, concat_axis=0, tiled=True)  5.22 us
    reshape x1, local copies, waits for them, and re-layouts, local(): interact(point_grid, kernel_plus, kernel_minus, coupling)  4.89 us
  transfers between devices with their start and end apart: 21, of which 19 were waited for; matrix products, arithmetic and copies ran while one was open for 4% of the time, Pallas kernels for 0%

commit v1 on v0

v1 whole, which is shorter than its diff:
```python
import functools
import math

import jax
import jax.numpy as jnp
from jax import lax
from jax.experimental import pallas as pl
from jax.experimental.pallas import tpu as pltpu
from jax.sharding import PartitionSpec as P

NDIR = 36
SUBSTEPS = 4
RIM = 2 * SUBSTEPS
GROUP = 16
CHUNKS = 3

plus_factor = 0.4096
minus_factor = 3.160494
cross_factor = 2.007843

VMEM_LIMIT = 16 * 1024 * 1024
whole = pl.BlockSpec(memory_space=pltpu.VMEM)
scalars = pl.BlockSpec(memory_space=pltpu.SMEM)


def params():
    return pltpu.CompilerParams(vmem_limit_bytes=VMEM_LIMIT)


def cost(micros):
    return pl.CostEstimate(flops=0, bytes_accessed=int(micros * 3.5e6), transcendentals=0)


def chunk_sizes(total):
    groups = total // GROUP
    count = min(CHUNKS, groups)
    return [GROUP * (groups // count + (i < groups % count)) for i in range(count)]


class Window:
    def __init__(self, n_lat, rows):
        self.pair = n_lat == 2
        self.rows = rows
        self.size = 2 * rows + 4 if self.pair else 3 * rows

    def own(self, lat):
        return jnp.where(lat == 0, 2, 2 + self.rows) if self.pair else self.rows

    def received(self, lat):
        if self.pair:
            return [jnp.where(lat == 0, 2 + self.rows, 2)]
        return [0, 2 * self.rows]

    def zeros(self, lat):
        if not self.pair:
            return []
        first = jnp.where(lat == 0, 0, 2 + 2 * self.rows)
        return [first, first + 1]

    def steps(self, lat, substep):
        shrink = 2 * (substep + 1)
        if self.pair:
            return jnp.where(lat == 0, 2, 2 + shrink), 2 * self.rows - shrink
        return shrink, 3 * self.rows - 2 * shrink


def faces_kernel(window, n_lon, place, own, lon_fields, lat_fields, out, fields):
    lat = place[0]
    rows, lanes = own.shape[1], own.shape[2]
    for row in window.zeros(lat):
        fields[row] = jnp.zeros((3, n_lon * lanes), jnp.float32)
    sources = [(window.own(lat), [own] + lon_fields)]
    for offset, blocks in zip(window.received(lat), lat_fields):
        sources.append((offset, blocks))
    for offset, blocks in sources:
        for d, block in enumerate(blocks):
            for f in range(3):
                for row in range(rows):
                    fields[offset + row, f : f + 1, d * lanes : (d + 1) * lanes] = block[f, row : row + 1, :]
    width = n_lon * lanes
    n_class = out.shape[2] // 6
    classes = lax.broadcasted_iota(jnp.int32, (n_class, width), 0).astype(jnp.float32)

    def hots(row):
        wet = fields[row, 0:1, :]
        hot_depth = (classes == fields[row, 1:2, :]).astype(jnp.float32)
        hot_current = (classes == fields[row, 2:3, :]).astype(jnp.float32)
        return wet, jnp.concatenate([hot_depth, hot_current], axis=0)

    def step(row, _):
        wet, hot = hots(row)
        wet_next, hot_next = hots(row + 1)
        east_wet = 0.5 * wet * pltpu.roll(wet, width - 1, 1)
        east = ((hot + pltpu.roll(hot, width - 1, 1)) * east_wet).astype(jnp.bfloat16)
        north = ((hot + hot_next) * (0.5 * wet * wet_next)).astype(jnp.bfloat16)
        span = 2 * n_class
        for copy in range(3):
            out[row, 0, copy * span : (copy + 1) * span, :] = east
            out[row, 1, copy * span : (copy + 1) * span, :] = north
        return 0

    lax.fori_loop(0, window.size - 1, step, 0)
    out[window.size - 1] = jnp.zeros(out.shape[1:], jnp.bfloat16)


def median_zero(a, b):
    return jnp.maximum(jnp.minimum(a, b), jnp.minimum(jnp.maximum(a, b), 0.0))


def flux(u, c, low, high, slope_low, slope_high):
    rising = u > 0.0
    return u * jnp.where(rising, low, high) + c * jnp.where(rising, slope_low, slope_high)


def prop_scratch(window, size, width):
    small = pltpu.VMEM((window.size, GROUP, width), jnp.float32)
    big = pltpu.VMEM((window.size, size, width), jnp.float32)
    return [small, small, big, big, big, big]


def propagate_kernel(
    window, n_lon, n_comp, split, start, head, place, tables, faces, wet, mine, lon_in, lat_in, *refs
):
    outs = refs[:-6]
    energy, other, east_u, east_c, north_u, north_c = refs[-6:]
    lat, comp = place[0], place[1]
    rows, lanes = window.rows, mine.shape[1]
    width = n_lon * lanes
    count = east_u.shape[1]

    def speeds(row, _):
        for which, u_ref, c_ref in ((0, east_u, east_c), (1, north_u, north_c)):
            u = jnp.dot(tables[which], faces[row, which], preferred_element_type=jnp.float32)
            size = jnp.abs(u)
            u_ref[row] = u
            c_ref[row] = 0.5 * size * (1.0 - size)
        return 0

    lax.fori_loop(0, window.size, speeds, 0, unroll=True)

    own = window.own(lat)

    def group(g, _):
        first = pl.multiple_of(g * GROUP, GROUP)
        here = pl.ds(first, GROUP)
        for row in window.zeros(lat):
            energy[row] = jnp.zeros((GROUP, width), jnp.float32)
            other[row] = jnp.zeros((GROUP, width), jnp.float32)
        sources = [(own, [(mine, start)] + [(ref, 3 + start) for ref in lon_in])]
        for offset, blocks in zip(window.received(lat), lat_in):
            sources.append((offset, [(ref, head) for ref in blocks]))
        for offset, blocks in sources:
            for d, (ref, lead) in enumerate(blocks):
                for row in range(rows):
                    at = pl.ds((lead + first) * rows + row, GROUP, stride=rows)
                    sea = wet[offset + row, 0:1, d * lanes : (d + 1) * lanes]
                    energy[offset + row, :, d * lanes : (d + 1) * lanes] = ref[at, :] * sea

        for substep in range(SUBSTEPS):
            base, length = window.steps(lat, substep)
            old, new = (energy, other) if substep % 2 == 0 else (other, energy)
            prior = [old[base + i] for i in (-2, -1, 0, 1)]
            gap = [b - a for a, b in zip(prior, prior[1:])]
            slope_prior, slope_here = median_zero(gap[1], gap[0]), median_zero(gap[2], gap[1])
            south = flux(
                north_u[base - 1, here], north_c[base - 1, here], prior[1], prior[2], slope_prior, slope_here
            )

            def row_step(i, carry):
                south, this, after, gap_after, slope_this = carry
                row = base + i
                beyond = old[row + 2]
                gap_beyond = beyond - after
                slope_after = median_zero(gap_beyond, gap_after)
                north = flux(north_u[row, here], north_c[row, here], this, after, slope_this, slope_after)
                east_cell = pltpu.roll(this, width - 1, 1)
                gap_east = east_cell - this
                gap_west = pltpu.roll(gap_east, 1, 1)
                slope = median_zero(gap_east, gap_west)
                slope_east = pltpu.roll(slope, width - 1, 1)
                east = flux(east_u[row, here], east_c[row, here], this, east_cell, slope, slope_east)
                west = pltpu.roll(east, 1, 1)
                new[row] = this - (east - west) - (north - south)
                return north, after, beyond, gap_beyond, slope_after

            lax.fori_loop(0, length, row_step, (south, prior[2], prior[3], gap[2], slope_here), unroll=True)

        if split:
            share = rows // n_comp
            for r in range(n_comp):
                base = own + lax.rem(comp + r, n_comp) * share
                for d in range(n_lon):
                    for k in range(share):
                        outs[r][d, k, here, :] = energy[base + k, :, d * lanes : (d + 1) * lanes]
        else:
            for row in range(rows):
                for d in range(n_lon):
                    outs[0][row, d, here, :] = energy[own + row, :, d * lanes : (d + 1) * lanes]
        return 0

    lax.fori_loop(0, count // GROUP, group, 0)


def matrix_kernel(index_cols, weight_cols, index_rows, weight_rows, out, out_t):
    height, total = out.shape[1], out.shape[2]
    base = pl.program_id(1) * height

    def step(i, _):
        at = pl.ds(pl.multiple_of(i * GROUP, GROUP), GROUP)
        cols = lax.broadcasted_iota(jnp.int32, (GROUP, total), 1)
        index, weight = index_cols[0, at, :], weight_cols[0, at, :]
        made = jnp.zeros((GROUP, total), jnp.float32)
        for corner in range(4):
            made = jnp.where(cols == index[:, corner : corner + 1], weight[:, corner : corner + 1], made)
        out[0, at, :] = made.astype(jnp.bfloat16)
        rows = base + i * GROUP + lax.broadcasted_iota(jnp.int32, (GROUP, total), 0)
        made = jnp.zeros((GROUP, total), jnp.float32)
        for corner in range(4):
            made = jnp.where(
                rows == index_rows[0, corner : corner + 1, :], weight_rows[0, corner : corner + 1, :], made
            )
        out_t[0, at, :] = made.astype(jnp.bfloat16)
        return 0

    lax.fori_loop(0, height // GROUP, step, 0, unroll=3)


def forward_kernel(sizes, n_lon, matrix, coupling, *refs):
    pieces = refs[:-4]
    energy_out, source_out, source_low_out, low = refs[-4:]
    step = pl.program_id(0)
    block = matrix.shape[1]
    half = block // n_lon
    per_chunk = len(pieces) // len(sizes)
    share, lanes = pieces[0].shape[1], pieces[0].shape[3]

    @pl.when(step == 0)
    def _():
        for s in range(per_chunk - n_lon + 1):
            for d in range(n_lon):
                at = (s * n_lon + d) * half
                for i, size in enumerate(sizes):
                    group = pieces[i * per_chunk : (i + 1) * per_chunk]
                    for k in range(share):
                        part = group[s][0, k] if d == 0 else group[d - n_lon][s, k]
                        energy_out[at : at + size, k * lanes : (k + 1) * lanes] = part
                        low[at : at + size, k * lanes : (k + 1) * lanes] = part.astype(jnp.bfloat16)
                    at += size

    here = pl.ds(pl.multiple_of(step * block, GROUP), block)
    energy = energy_out[here, :]
    plus_side = jnp.dot(matrix[0], low[...], preferred_element_type=jnp.float32)
    minus_side = jnp.dot(matrix[1], low[...], preferred_element_type=jnp.float32)
    source = coupling[...] * (
        energy * energy * (plus_factor * plus_side + minus_factor * minus_side)
        - cross_factor * energy * plus_side * minus_side
    )
    source_out[...] = source
    source_low_out[...] = source.astype(jnp.bfloat16)


def backward_kernel(matrix_t, source_low, energy, source, out):
    gain = (
        jnp.dot(matrix_t[0], source_low[...], preferred_element_type=jnp.float32)
        + jnp.dot(matrix_t[1], source_low[...], preferred_element_type=jnp.float32)
        - 2.0 * source[...]
    )
    result = energy[...] + gain / (1.0 + jnp.abs(gain))
    lanes = out.shape[2]
    for k in range(out.shape[0]):
        out[k] = result[:, k * lanes : (k + 1) * lanes]


def gather_kernel(n_lon, rows, place, *refs):
    pieces, out = refs[:-1], refs[-1]
    comp, lon = place[1], place[2]
    n_comp = len(pieces)
    share = rows // n_comp
    half = pieces[0].shape[1] // n_lon
    for r, piece in enumerate(pieces):
        for k in range(share):
            row = lax.rem(comp + r, n_comp) * share + k
            for d in range(n_lon):
                first = lax.rem(lon + n_lon - d, n_lon) * half
                for i in range(0, half, GROUP):
                    at = pl.ds((first + i) * rows + row, GROUP, stride=rows)
                    out[at, :] = piece[k, d * half + i : d * half + i + GROUP, :]


def turned(array, axis, position):
    return jnp.roll(jnp.flip(array, axis), position + 1, axis)


def local(
    spectrum,
    sea_mask,
    depth_class,
    current_class,
    speed_table,
    current_table,
    coupling,
    quad_index,
    quad_weight,
):
    comps_local, rows, lanes = spectrum.shape
    n_comp, n_lat, n_lon = (lax.axis_size(a) for a in ("comp", "lat", "lon"))
    comp, lat, lon = (lax.axis_index(a) for a in ("comp", "lat", "lon"))
    place = jnp.stack([lat, comp, lon]).astype(jnp.int32)
    half_own = comps_local // n_lon
    half = -(-half_own // GROUP) * GROUP
    sizes = chunk_sizes(half)
    starts = [sum(sizes[:i]) for i in range(len(sizes))]
    window = Window(n_lat, rows)
    width = n_lon * lanes
    split = rows % n_comp == 0

    flat = spectrum.reshape(comps_local * rows, lanes)
    fields = jnp.stack([sea_mask, depth_class, current_class]).astype(jnp.float32)
    fields_flat = fields.reshape(3 * rows, lanes)
    parts = []
    for d in range(n_lon):
        owner = lax.rem(lon + d, n_lon)
        part = lax.dynamic_slice_in_dim(flat, owner * half_own * rows, half_own * rows, 0)
        parts.append(jnp.pad(part, ((0, (half - half_own) * rows), (0, 0))))
    lon_in = []
    for d in range(n_lon - 1, 0, -1):
        lon_in.append(
            lax.ppermute(
                jnp.concatenate([fields_flat, parts[d]]), "lon", [(i, (i + d) % n_lon) for i in range(n_lon)]
            )
        )
    if window.pair:
        moves = [[(0, 1), (1, 0)]]
    else:
        moves = [[(i, i + 1) for i in range(n_lat - 1)], [(i + 1, i) for i in range(n_lat - 1)]]
    lat_in = []
    for i, (start, size) in enumerate(zip(starts, sizes)):
        of_chunk = []
        for move in moves:
            blocks = []
            for d in [0] + list(range(n_lon - 1, 0, -1)):
                block = lax.slice_in_dim(parts[d], start * rows, (start + size) * rows, axis=0)
                if i == 0:
                    block = jnp.concatenate([fields_flat, block])
                pairs = [
                    (a * n_lon + b, to * n_lon + (b + d) % n_lon) for a, to in move for b in range(n_lon)
                ]
                blocks.append(lax.ppermute(block, ("lat", "lon"), pairs))
            of_chunk.append(blocks)
        lat_in.append(of_chunk)

    n_class = speed_table.shape[0]
    head_block = pl.BlockSpec((3, rows, lanes), lambda i: (0, 0, 0))
    lon_heads = [a.reshape(-1, rows, lanes) for a in lon_in]
    lat_heads = [[a.reshape(-1, rows, lanes) for a in blocks] for blocks in lat_in[0]]
    faces, window_fields = pl.pallas_call(
        functools.partial(faces_kernel, window, n_lon),
        grid=(1,),
        out_shape=(
            jax.ShapeDtypeStruct((window.size, 2, 6 * n_class, width), jnp.bfloat16),
            jax.ShapeDtypeStruct((window.size, 3, width), jnp.float32),
        ),
        in_specs=[
            scalars,
            head_block,
            [head_block] * len(lon_heads),
            [[head_block] * len(blocks) for blocks in lat_heads],
        ],
        out_specs=(whole, whole),
        compiler_params=params(),
        cost_estimate=cost(2),
    )(place, fields, lon_heads, lat_heads)

    ids = comp * comps_local + lon * half_own + jnp.arange(half, dtype=jnp.int32)
    freq_hot = ((ids // NDIR)[:, None] == jnp.arange(speed_table.shape[1], dtype=jnp.int32)[None, :]).astype(
        jnp.float32
    )
    speed = jnp.dot(freq_hot, speed_table.T, precision=lax.Precision.HIGHEST)
    angles = 2.0 * math.pi / NDIR * (ids % NDIR).astype(jnp.float32)
    tables = []
    for which, turn in ((0, jnp.cos(angles)), (1, jnp.sin(angles))):
        currents = jnp.broadcast_to(current_table[:, which][None], (half, n_class))
        left = jnp.concatenate([speed * turn[:, None], currents], axis=1)
        levels = []
        for _ in range(3):
            level = lax.reduce_precision(left, 8, 7)
            levels.append(level)
            left = left - level
        tables.append(jnp.concatenate(levels, axis=1).astype(jnp.bfloat16))
    tables = jnp.stack(tables)

    def arranged(array):
        array = array.reshape(array.shape[0], n_comp, n_lon, half_own, array.shape[-1])
        if split:
            array = turned(array, 1, comp)
        return turned(array, 2, lon)

    def position(index):
        of_comp, rest = index // comps_local, index % comps_local
        if split:
            of_comp = lax.rem(comp + n_comp - of_comp, n_comp)
        of_lon = lax.rem(lon + n_lon - rest // half_own, n_lon)
        return (of_comp * n_lon + of_lon) * half + rest % half_own

    padding = ((0, 0), (0, 0), (0, 0), (0, half - half_own), (0, 0))
    total = n_comp * n_lon * half
    block = n_lon * half
    index = jnp.pad(arranged(position(quad_index)), padding, constant_values=-1).reshape(2, total, 4)
    weight = jnp.pad(arranged(quad_weight), padding).reshape(2, total, 4)
    strength = jnp.pad(arranged(coupling[None, :, None]), padding).reshape(total, 1)
    by_rows = pl.BlockSpec((1, block, 4), lambda s, i: (s, i, 0))
    by_cols = pl.BlockSpec((1, 4, total), lambda s, i: (s, 0, 0))
    by_block = pl.BlockSpec((1, block, total), lambda s, i: (s, i, 0))
    matrix, matrix_t = pl.pallas_call(
        matrix_kernel,
        grid=(2, n_comp),
        out_shape=(jax.ShapeDtypeStruct((2, total, total), jnp.bfloat16),) * 2,
        in_specs=[by_rows, by_rows, by_cols, by_cols],
        out_specs=(by_block, by_block),
        compiler_params=params(),
        cost_estimate=cost(10),
    )(index, weight, jnp.swapaxes(index, 1, 2), jnp.swapaxes(weight, 1, 2))

    if split:
        share, span = rows // n_comp, lanes
    else:
        groups = n_comp // rows
        share, span = 1, lanes // groups
    arrived = []
    for i, (start, size) in enumerate(zip(starts, sizes)):
        table = lax.slice_in_dim(tables, start, start + size, axis=1)
        if split:
            shapes = [jax.ShapeDtypeStruct((n_lon, share, size, lanes), jnp.float32)] * n_comp
        else:
            shapes = [jax.ShapeDtypeStruct((rows, n_lon, size, lanes), jnp.float32)]
        big = pltpu.VMEM((window.size, size, width), jnp.float32)
        pieces = pl.pallas_call(
            functools.partial(
                propagate_kernel, window, n_lon, n_comp, split, start, 3 if i == 0 else 0
            ),
            out_shape=shapes,
            in_specs=[
                scalars,
                whole,
                whole,
                whole,
                whole,
                [whole] * len(lon_in),
                [[whole] * len(blocks) for blocks in lat_in[i]],
            ],
            out_specs=[whole] * len(shapes),
            scratch_shapes=prop_scratch(window, size, width),
            compiler_params=params(),
            cost_estimate=cost(7),
        )(
            place,
            table,
            faces,
            window_fields,
            parts[0],
            lon_in,
            lat_in[i],
        )
        if split:
            moved = [pieces[0]]
            for r in range(1, n_comp):
                moved.append(lax.ppermute(pieces[r], "comp", [(a, (a + r) % n_comp) for a in range(n_comp)]))
        else:
            energy = pieces[0].reshape(rows, n_lon, size, groups, span)
            energy = jnp.transpose(energy, (0, 3, 1, 2, 4)).reshape(n_comp, n_lon, 1, size, span)
            energy = lax.all_to_all(energy, "comp", split_axis=0, concat_axis=0, tiled=True)
            moved = [energy[s] for s in range(n_comp)]
        crossed = []
        for d in range(1, n_lon):
            pairs = [(b, (b + d) % n_lon) for b in range(n_lon)]
            crossed.append(lax.ppermute(jnp.stack([piece[d] for piece in moved]), "lon", pairs))
        arrived += moved + crossed

    cells = share * span
    energy, source, source_low = pl.pallas_call(
        functools.partial(forward_kernel, sizes, n_lon),
        grid=(n_comp,),
        out_shape=(
            jax.ShapeDtypeStruct((total, cells), jnp.float32),
            jax.ShapeDtypeStruct((total, cells), jnp.float32),
            jax.ShapeDtypeStruct((total, cells), jnp.bfloat16),
        ),
        in_specs=[
            pl.BlockSpec((2, block, total), lambda s: (0, s, 0)),
            pl.BlockSpec((block, 1), lambda s: (s, 0)),
        ]
        + [whole] * len(arrived),
        out_specs=(
            pl.BlockSpec((total, cells), lambda s: (0, 0)),
            pl.BlockSpec((block, cells), lambda s: (s, 0)),
            pl.BlockSpec((block, cells), lambda s: (s, 0)),
        ),
        scratch_shapes=[pltpu.VMEM((total, cells), jnp.bfloat16)],
        compiler_params=params(),
        cost_estimate=cost(4),
    )(matrix, strength, *arrived)

    back = []
    for s in range(n_comp):
        back.append(
            pl.pallas_call(
                backward_kernel,
                grid=(1,),
                out_shape=jax.ShapeDtypeStruct((share, block, span), jnp.float32),
                in_specs=[
                    pl.BlockSpec((2, block, total), lambda i, s=s: (0, s, 0)),
                    pl.BlockSpec((total, cells), lambda i: (0, 0)),
                    pl.BlockSpec((block, cells), lambda i, s=s: (s, 0)),
                    pl.BlockSpec((block, cells), lambda i, s=s: (s, 0)),
                ],
                out_specs=pl.BlockSpec((share, block, span), lambda i: (0, 0, 0)),
                compiler_params=params(),
                cost_estimate=cost(0.6),
            )(matrix_t, source_low, energy, source)
        )

    if split:
        home = [back[0]]
        for r in range(1, n_comp):
            home.append(lax.ppermute(back[r], "comp", [(a, (a - r) % n_comp) for a in range(n_comp)]))
        if half == half_own:
            out = pl.pallas_call(
                functools.partial(gather_kernel, n_lon, rows),
                out_shape=jax.ShapeDtypeStruct((comps_local * rows, lanes), jnp.float32),
                in_specs=[scalars] + [whole] * n_comp,
                out_specs=whole,
                compiler_params=params(),
                cost_estimate=cost(2),
            )(place, *home)
            return out.reshape(comps_local, rows, lanes)
        home = jnp.stack(home).reshape(n_comp, share, n_lon, half, lanes)[:, :, :, :half_own]
        home = jnp.roll(home, comp, 0)
        home = turned(home, 2, lon)
        return jnp.transpose(home, (2, 3, 0, 1, 4)).reshape(comps_local, rows, lanes)
    home = lax.all_to_all(jnp.concatenate(back), "comp", split_axis=0, concat_axis=0, tiled=True)
    home = home.reshape(rows, groups, n_lon, half, span)[:, :, :, :half_own]
    home = turned(home, 2, lon)
    return jnp.transpose(home, (2, 3, 0, 1, 4)).reshape(comps_local, rows, lanes)


def solution(mesh):
    placed = (
        P(("ens", "comp"), "lat", "lon"),
        P("lat", "lon"),
        P("lat", "lon"),
        P("lat", "lon"),
        P(),
        P(),
        P(),
        P(),
        P(),
    )
    return jax.shard_map(
        local,
        mesh=mesh,
        in_specs=placed,
        out_specs=P(("ens", "comp"), "lat", "lon"),
        check_vma=False,
    )
```

time: 198 us -> 128 us (0.65)
  waiting for transfers between devices: 97.5 us -> 40.8 us
  Pallas kernels: 0 us -> 40 us
  blocking collectives: 30.6 us -> 0 us
  matrix products: 19.6 us -> 0.2 us
  other arithmetic: 18.7 us -> 4.69 us
  starting transfers between devices: 19.4 us -> 26.4 us
  local copies, waits for them, and re-layouts: 11 us -> 14.5 us
    pallas_call x0 -> x11, Pallas kernels: none -> 40 us  [the longest x3 18.7 us: local(): pl.pallas_call(functools.partial(propagate_kernel, window, n_lon, n_comp,...]
    all_to_all x1 -> x0, blocking collectives: 30.6 us -> none  [local(): lax.all_to_all(arrived, 'comp', split_axis=0, concat_axis=1, tiled=True)]
    all_to_all x1 -> x0, waiting for transfers between devices: 28.8 us -> none  [local(): lax.all_to_all(outgoing, 'comp', split_axis=1, concat_axis=0, tiled=True)]
    ppermute x20 -> x22, waiting for transfers between devices: 68.7 us -> 40.8 us  [the longest x3 25.3 us: local(): lax.ppermute(back[r], 'comp', [(a, (a - r) % n_comp) for a in range(n_com...]
    dot_general x7 -> x1, matrix products: 19.6 us -> 0.2 us  [local(): speed = jnp.dot(freq_hot, speed_table.T, precision=lax.Precision.HIGHEST)]
    ppermute x20 -> x22, starting transfers between devices: 14.2 us -> 26.4 us  [the longest x9 14.2 us: local(): lax.ppermute(pieces[r], 'comp', [(a, (a + r) % n_comp) for a in range(n_c...]
    add x16 -> x1, other arithmetic: 11.8 us -> 0.2 us  [position(): return (of_comp * n_lon + of_lon) * half + rest % half_own]
    reshape x3 -> x7, local copies, waits for them, and re-layouts: 7.84 us -> 1.66 us  [the longest x2 0.54 us: local(): jnp.pad(arranged(position(quad_index)), padding, constant_values=-1)]
  transfers between devices with their start and end apart: 21 -> 22, of which waited for: 19 -> 5; matrix products, arithmetic and copies ran while one was open for 4% -> 10% of each run, Pallas kernels for 0% -> 25%
where the time goes in v1:
time: 128 us; the launch traced here: 127 us
  waiting for transfers between devices  40.8 us (32%)
  Pallas kernels  40 us (31%)
  starting transfers between devices  26.4 us (21%)
  local copies, waits for them, and re-layouts  14.5 us (11%)
  other arithmetic  4.69 us (4%)
    ppermute x3, waiting for transfers between devices, local(): lax.ppermute(back[r], 'comp', [(a, (a - r) % n_comp) for a in range(n_com...  25.3 us
    pallas_call x3, Pallas kernels, local(): pl.pallas_call(functools.partial(propagate_kernel, window, n_lon, n_comp,...  18.7 us
    ppermute x9, starting transfers between devices, local(): lax.ppermute(pieces[r], 'comp', [(a, (a + r) % n_comp) for a in range(n_c...  14.2 us
    pallas_call x1, Pallas kernels, local(): pl.pallas_call(matrix_kernel, grid=(2, n_comp), out_shape=(jax.ShapeDtype...  10.8 us
    ppermute x6, waiting for transfers between devices, local(): blocks.append(lax.ppermute(block, ('lat', 'lon'), pairs))  10.6 us
    ppermute x6, starting transfers between devices, local(): blocks.append(lax.ppermute(block, ('lat', 'lon'), pairs))  8.26 us
    ppermute x9, waiting for transfers between devices, local(): lax.ppermute(pieces[r], 'comp', [(a, (a + r) % n_comp) for a in range(n_c...  4.92 us
    pallas_call x1, Pallas kernels, local(): pl.pallas_call(functools.partial(forward_kernel, sizes, n_lon), grid=(n_c...  4.2 us
  transfers between devices with their start and end apart: 22, of which 5 were waited for; matrix products, arithmetic and copies ran while one was open for 10% of the time, Pallas kernels for 25%

profile of v1, /device:TPU:0, one launch (start us, length us, event | category | flops | bytes accessed | tf_op | source)
XLA Modules:
  0.0 127.2 jit_solution(1701499476070510298)
XLA Ops:
  0.0 2.4 %constant_dynamic-slice_fusion = (f32[384,128]{1,0:T(8,128)}, f32[384,128]{1,0:T(8,128)}, f32[384,128]{1,0:T(8,128)}, f32[384,128]{1,0:T(8,128)}, f32[384,128]{1,0:T(8,128)S(1)}, /*index=5*/f32[384,128]{1,0:T(8,128)S(1)}) fusion(f32[2304,128]{1,0:T(8,128)} %bitcast.47, s32[]{:T(128)S(6)} %add.140, s32[]{:T(128)S(6)} %add.139, s32[]{:T(128)S(6)} %add.138, ...), kind=kLoop, calls=%fused_computation.70 | loop fusion | bytes 2359320 | tf_op jit(solution)/shard_map/slice | solution.py:342
  2.4 2.4 %collective-permute-start.14 = (f32[384,128]{1,0:T(8,128)}, f32[384,128]{1,0:T(8,128)}, u32[]{:S(2)}, u32[]{:S(2)}) collective-permute-start(f32[384,128]{1,0:T(8,128)} %get-tuple-element.43), channel_id=1, source_target_pairs={{0,3},{1,2},{2,1},{3,0},{4,7},{5,6},{6,5},{7,4},{8,11},{9,10},{10,... | collective-permute-start | bytes 589832 | tf_op jit(solution)/shard_map/ppermute | solution.py:348
  4.8 0.6 collective-permute-start.13
  5.4 0.8 pad_maximum_fusion.1
  6.2 1.5 %collective-permute-start.2 = (f32[408,128]{1,0:T(8,128)}, f32[408,128]{1,0:T(8,128)S(1)}, u32[]{:S(2)}, u32[]{:S(2)}) collective-permute-start(f32[408,128]{1,0:T(8,128)} %get-tuple-element.62), channel_id=1, source_target_pairs={{0,3},{1,2},{2,1},{3,0},{4,7},{5,6},{6,5},{7,4},{8,11},{9,10},{10,... | collective-permute-start | bytes 626696 | tf_op jit(solution)/shard_map/ppermute | solution.py:348
  7.7 0.3 collective-permute-start.1
  8.1 0.2 collective-permute-start
  8.4 0.3 copy-done.27
  9.1 0.2 fusion.13
  9.3 0.2 reshape.311
  9.6 0.2 rev.25
  9.8 0.1 fusion.7
  10.0 0.1 reshape.312
  10.1 0.2 broadcast_multiply_fusion.1
  10.3 0.1 pad_maximum_fusion.7
  10.8 0.2 reshape.313
  10.9 0.6 rev.26
  11.8 7.3 %collective-permute-done.2.lat_in_0__1_ = f32[408,128]{1,0:T(8,128)S(1)} collective-permute-done((f32[408,128]{1,0:T(8,128)}, f32[408,128]{1,0:T(8,128)S(1)}, u32[]{:S(2)}, u32[]{:S(2)}) %collective-permute-start.2) | collective-permute-done | bytes 208928 | tf_op jit(solution)/shard_map/ppermute | solution.py:348
  19.1 2.1 %collective-permute-start.8 = (f32[384,128]{1,0:T(8,128)}, f32[384,128]{1,0:T(8,128)S(1)}, u32[]{:S(2)}, u32[]{:S(2)}) collective-permute-start(f32[384,128]{1,0:T(8,128)} %get-tuple-element.45), channel_id=1, source_target_pairs={{0,3},{1,2},{2,1},{3,0},{4,7},{5,6},{6,5},{7,4},{8,11},{9,10},{10,... | collective-permute-start | bytes 589832 | tf_op jit(solution)/shard_map/ppermute | solution.py:348
  21.2 3.3 %collective-permute-done.1.lat_in_0__0_ = f32[408,128]{1,0:T(8,128)S(1)} collective-permute-done((f32[408,128]{1,0:T(8,128)}, f32[408,128]{1,0:T(8,128)S(1)}, u32[]{:S(2)}, u32[]{:S(2)}) %collective-permute-start.1) | collective-permute-done | bytes 208928 | tf_op jit(solution)/shard_map/ppermute | solution.py:348
  24.5 0.7 copy-done.1
  25.1 1.5 %collective-permute-start.7 = (f32[384,128]{1,0:T(8,128)}, f32[384,128]{1,0:T(8,128)S(1)}, u32[]{:S(2)}, u32[]{:S(2)}) collective-permute-start(f32[384,128]{1,0:T(8,128)} %get-tuple-element.46), channel_id=1, source_target_pairs={{0,2},{1,3},{2,0},{3,1},{4,6},{5,7},{6,4},{7,5},{8,10},{9,11},{10,... | collective-permute-start | bytes 589832 | tf_op jit(solution)/shard_map/ppermute | solution.py:348
  26.6 0.9 copy-done.2
  27.6 2.2 %shard_map.92 = (bf16[20,2,96,256]{3,2,1,0:T(8,128)(2,1)S(1)}, f32[20,3,256]{2,1,0:T(4,128)S(1)}) custom-call(s32[3]{0:T(128)S(1)} %pad_add_fusion.place, f32[3,8,128]{2,1,0:T(8,128)S(1)} %get-tuple-element.65.own, f32[147,8,128]{2,1,0:T(8,128)S(1)} %bitcast.42, f32[51,8,128]{2,1,0:T(8,128)S(1)} %bitcast.44, f32[51,8,128]{2,1,0:T(8,128)S(1)} %bitcast.43), custom_call_target="tpu_custom_call" | custom-call | bytes 7000000 | tf_op jit(solution)/shard_map/pallas_call | solution.py:356
  29.8 6.7 %shard_map.95 = (f32[2,2,48,128]{3,2,1,0:T(8,128)S(1)}, f32[2,2,48,128]{3,2,1,0:T(8,128)}, f32[2,2,48,128]{3,2,1,0:T(8,128)S(1)}, f32[2,2,48,128]{3,2,1,0:T(8,128)S(1)}) custom-call(s32[3]{0:T(128)S(1)} %pad_add_fusion.place, bf16[2,48,96]{2,1,0:T(8,128)(2,1)S(1)} %get-tuple-element.51.tables, bf16[20,2,96,256]{3,2,1,0:T(8,128)(2,1)S(1)} %get-tuple-element.26.faces, ...), custom_call_target="tpu_custom_call" | custom-call | bytes 24500000 | tf_op jit(solution)/shard_map/pallas_call | solution.py:437
  36.5 0.6 copy-done.4
  37.2 1.6 %collective-permute-start.15 = (f32[2,2,48,128]{3,2,1,0:T(8,128)}, f32[2,2,48,128]{3,2,1,0:T(8,128)}, u32[]{:S(2)}, u32[]{:S(2)}) collective-permute-start(f32[2,2,48,128]{3,2,1,0:T(8,128)} %get-tuple-element.37), channel_id=1, source_target_pairs={{0,4},{4,8},{8,12},{12,0},{1,5},{5,9},{9,13},{13,1},{2,6},{6,10},{... | collective-permute-start | bytes 294920 | tf_op jit(solution)/shard_map/ppermute | solution.py:467
  38.8 6.3 %shard_map.94 = (f32[2,2,48,128]{3,2,1,0:T(8,128)S(1)}, f32[2,2,48,128]{3,2,1,0:T(8,128)}, f32[2,2,48,128]{3,2,1,0:T(8,128)}, f32[2,2,48,128]{3,2,1,0:T(8,128)}) custom-call(s32[3]{0:T(128)S(1)} %pad_add_fusion.place, bf16[2,48,96]{2,1,0:T(8,128)(2,1)S(1)} %get-tuple-element.52.tables, bf16[20,2,96,256]{3,2,1,0:T(8,128)(2,1)S(1)} %get-tuple-element.26.faces, ...), custom_call_target="tpu_custom_call" | custom-call | bytes 24500000 | tf_op jit(solution)/shard_map/pallas_call | solution.py:437
  45.1 0.6 copy-done.7
  45.7 1.6 %collective-permute-start.9 = (f32[2,2,48,128]{3,2,1,0:T(8,128)}, f32[2,2,48,128]{3,2,1,0:T(8,128)}, u32[]{:S(2)}, u32[]{:S(2)}) collective-permute-start(f32[2,2,48,128]{3,2,1,0:T(8,128)} %get-tuple-element.33), channel_id=1, source_target_pairs={{0,4},{4,8},{8,12},{12,0},{1,5},{5,9},{9,13},{13,1},{2,6},{6,10},{... | collective-permute-start | bytes 294920 | tf_op jit(solution)/shard_map/ppermute | solution.py:467
  47.3 1.2 collective-permute-start.10
  48.6 2.7 %collective-permute-start.11 = (f32[2,2,48,128]{3,2,1,0:T(8,128)}, f32[2,2,48,128]{3,2,1,0:T(8,128)}, u32[]{:S(2)}, u32[]{:S(2)}) collective-permute-start(f32[2,2,48,128]{3,2,1,0:T(8,128)} %get-tuple-element.35), channel_id=1, source_target_pairs={{0,12},{4,0},{8,4},{12,8},{1,13},{5,1},{9,5},{13,9},{2,14},{6,2},{... | collective-permute-start | bytes 294920 | tf_op jit(solution)/shard_map/ppermute | solution.py:467
  51.3 0.7 fusion.6
  52.0 1.5 %rev.27 = f32[2,4,2,144,4]{3,2,1,4,0:T(2,128)} reverse(f32[2,4,2,144,4]{3,2,1,4,0:T(2,128)} %fusion.6), dimensions={2} | reverse | bytes 73728 | tf_op jit(solution)/shard_map/jit(_flip)/rev | solution.py:291
  53.5 0.9 copy-done.3
  54.4 5.6 %shard_map.93 = (f32[2,2,48,128]{3,2,1,0:T(8,128)S(1)}, f32[2,2,48,128]{3,2,1,0:T(8,128)S(1)}, f32[2,2,48,128]{3,2,1,0:T(8,128)S(1)}, f32[2,2,48,128]{3,2,1,0:T(8,128)S(1)}) custom-call(s32[3]{0:T(128)S(1)} %pad_add_fusion.place, bf16[2,48,96]{2,1,0:T(8,128)(2,1)S(1)} %get-tuple-element.53.tables, bf16[20,2,96,256]{3,2,1,0:T(8,128)(2,1)S(1)} %get-tuple-element.26.faces, ...), custom_call_target="tpu_custom_call" | custom-call | bytes 24500000 | tf_op jit(solution)/shard_map/pallas_call | solution.py:437
  60.2 1.0 collective-permute-start.4
  61.2 0.8 slice.101
  62.0 2.8 %collective-permute-start.5 = (f32[2,2,48,128]{3,2,1,0:T(8,128)S(1)}, f32[2,2,48,128]{3,2,1,0:T(8,128)S(1)}, u32[]{:S(2)}, u32[]{:S(2)}) collective-permute-start(f32[2,2,48,128]{3,2,1,0:T(8,128)S(1)} %get-tuple-element.31), channel_id=1, source_target_pairs={{0,12},{4,0},{8,4},{12,8},{1,13},{5,1},{9,5},{13,9},{2,14},{6,2},{... | collective-permute-start | bytes 294920 | tf_op jit(solution)/shard_map/ppermute | solution.py:467
  64.8 0.8 slice.97
  65.6 2.1 %collective-permute-start.16 = (f32[2,2,48,128]{3,2,1,0:T(8,128)S(1)}, f32[2,2,48,128]{3,2,1,0:T(8,128)S(1)}, u32[]{:S(2)}, u32[]{:S(2)}) collective-permute-start(f32[2,2,48,128]{3,2,1,0:T(8,128)S(1)} %copy-done.17), channel_id=1, source_target_pairs={{0,8},{4,12},{8,0},{12,4},{1,9},{5,13},{9,1},{13,5},{2,10},{6,14},... | collective-permute-start | bytes 294920 | tf_op jit(solution)/shard_map/ppermute | solution.py:467
  67.7 0.8 slice.98
  68.5 1.1 collective-permute-start.17
  69.6 0.8 slice.99
  70.4 0.7 pad_maximum_fusion.4
  71.1 4.9 %collective-permute-done.16.refs_12_ = f32[2,2,48,128]{3,2,1,0:T(8,128)S(1)} collective-permute-done((f32[2,2,48,128]{3,2,1,0:T(8,128)S(1)}, f32[2,2,48,128]{3,2,1,0:T(8,128)S(1)}, u32[]{:S(2)}, u32[]{:S(2)}) %collective-permute-start.16) | collective-permute-done | bytes 98336 | tf_op jit(solution)/shard_map/ppermute | solution.py:467
  76.1 0.7 pad_maximum_fusion.5
  76.8 0.5 collective-permute-start.18
  77.3 0.7 pad_maximum_fusion.3
  78.2 0.1 reshape.314
  78.3 0.3 reshape.321.coupling
  78.6 0.4 copy.20.weight_cols
  79.0 0.4 copy.19.index_cols
  79.5 10.8 %shard_map.91 = (bf16[2,1152,1152]{2,1,0:T(8,128)(2,1)S(1)}, bf16[2,1152,1152]{2,1,0:T(8,128)(2,1)S(1)}) custom-call(s32[2,1152,4]{2,1,0:T(8,128)S(1)} %copy.19.index_cols, f32[2,1152,4]{2,1,0:T(8,128)S(1)} %copy.20.weight_cols, s32[2,4,1152]{2,1,0:T(4,128)S(1)} %bitcast.45, f32[2,4,1152]{2,1,0:T(4,128)S(1)} %bitcast.46), custom_call_target="tpu_custom_call" | custom-call | bytes 35000000 | tf_op jit(solution)/shard_map/pallas_call | solution.py:414
  90.3 4.2 %shard_map.96 = (f32[1152,256]{1,0:T(8,128)S(1)}, f32[1152,256]{1,0:T(8,128)S(1)}, bf16[1152,256]{1,0:T(8,128)(2,1)S(1)}) custom-call(bf16[2,1152,1152]{2,1,0:T(8,128)(2,1)S(1)} %get-tuple-element.25.matrix, f32[1152,1]{1,0:T(8,128)S(1)} %reshape.321.coupling, f32[2,2,48,128]{3,2,1,0:T(8,128)S(1)} %copy-done.11, ...), custom_call_target="tpu_custom_call" | custom-call | bytes 14000000 | tf_op jit(solution)/shard_map/pallas_call | solution.py:480
  94.5 0.6 shard_map.100
  95.1 0.6 shard_map.99
  95.7 0.6 shard_map.98
  96.2 2.3 %collective-permute-start.19 = (f32[2,288,128]{2,1,0:T(8,128)S(1)}, f32[2,288,128]{2,1,0:T(8,128)S(1)}, u32[]{:S(2)}, u32[]{:S(2)}) collective-permute-start(f32[2,288,128]{2,1,0:T(8,128)S(1)} %shard_map.98), channel_id=1, source_target_pairs={{0,12},{4,0},{8,4},{12,8},{1,13},{5,1},{9,5},{13,9},{2,14},{6,2},{... | collective-permute-start | bytes 884744 | tf_op jit(solution)/shard_map/ppermute | solution.py:525
  98.5 0.9 collective-permute-start.20
  99.4 0.6 shard_map.97.refs_0_
  100.0 6.0 %collective-permute-done.19.refs_1_ = f32[2,288,128]{2,1,0:T(8,128)S(1)} collective-permute-done((f32[2,288,128]{2,1,0:T(8,128)S(1)}, f32[2,288,128]{2,1,0:T(8,128)S(1)}, u32[]{:S(2)}, u32[]{:S(2)}) %collective-permute-start.19) | collective-permute-done | bytes 294944 | tf_op jit(solution)/shard_map/ppermute | solution.py:525
  106.0 19.3 %collective-permute-done.20.refs_2_ = f32[2,288,128]{2,1,0:T(8,128)S(1)} collective-permute-done((f32[2,288,128]{2,1,0:T(8,128)S(1)}, f32[2,288,128]{2,1,0:T(8,128)S(1)}, u32[]{:S(2)}, u32[]{:S(2)}) %collective-permute-start.20) | collective-permute-done | bytes 294944 | tf_op jit(solution)/shard_map/ppermute | solution.py:525
  125.3 1.9 %shard_map.101 = f32[2304,128]{1,0:T(8,128)} custom-call(s32[3]{0:T(128)S(1)} %pad_add_fusion.place, f32[2,288,128]{2,1,0:T(8,128)S(1)} %shard_map.97.refs_0_, f32[2,288,128]{2,1,0:T(8,128)S(1)} %collective-permute-done.19.refs_1_, f32[2,288,128]{2,1,0:T(8,128)S(1)} %collective-permute-done.20.refs_2_, f32[2,288,128]{2,1,0:T(8,128)S(1)} %collective-permute-done.21.refs_3_), custom_call_target="tpu_custom_call" | custom-call | bytes 7000000 | tf_op jit(solution)/shard_map/pallas_call | solution.py:527
  (103 shorter events, 1.6 us)
Async XLA Ops:
  0.0 10.1 %copy-start = (f32[16,32]{1,0:T(8,128)S(1)}, f32[16,32]{1,0:T(8,128)}, u32[]{:S(2)}) copy-start(f32[16,32]{1,0:T(8,128)} %param.13) | copy-start | bytes 6148
  0.0 5.4 %copy-start.24 = (s32[8,128]{1,0:T(8,128)S(1)}, s32[8,128]{1,0:T(8,128)}, u32[]{:S(2)}) copy-start(s32[8,128]{1,0:T(8,128)} %param.12) | copy-start | bytes 12292
  0.0 5.4 %copy-start.25 = (s32[8,128]{1,0:T(8,128)S(1)}, s32[8,128]{1,0:T(8,128)}, u32[]{:S(2)}) copy-start(s32[8,128]{1,0:T(8,128)} %param.11) | copy-start | bytes 12292
  0.0 5.4 %copy-start.26 = (s32[8,128]{1,0:T(8,128)S(1)}, s32[8,128]{1,0:T(8,128)}, u32[]{:S(2)}) copy-start(s32[8,128]{1,0:T(8,128)} %param.10) | copy-start | bytes 12292
  0.0 7.9 %copy-start.18 = (f32[288,8,128]{2,1,0:T(8,128)S(1)}, f32[288,8,128]{2,1,0:T(8,128)}, u32[]{:S(2)}) copy-start(f32[288,8,128]{2,1,0:T(8,128)} %param.9) | copy-start | bytes 3538948
  2.4 27.4 %collective-permute-start.14 = (f32[384,128]{1,0:T(8,128)}, f32[384,128]{1,0:T(8,128)}, u32[]{:S(2)}, u32[]{:S(2)}) collective-permute-start(f32[384,128]{1,0:T(8,128)} %get-tuple-element.43), channel_id=1, source_target_pairs={{0,3},{1,2},{2,1},{3,0},{4,7},{5,6},{6,5},{7,4},{8,11},{9,10},{10,... | collective-permute-start | bytes 589832 | tf_op jit(solution)/shard_map/ppermute | solution.py:348
  4.8 25.0 %collective-permute-start.13 = (f32[384,128]{1,0:T(8,128)}, f32[384,128]{1,0:T(8,128)}, u32[]{:S(2)}, u32[]{:S(2)}) collective-permute-start(f32[384,128]{1,0:T(8,128)} %get-tuple-element.44), channel_id=1, source_target_pairs={{0,2},{1,3},{2,0},{3,1},{4,6},{5,7},{6,4},{7,5},{8,10},{9,11},{10,... | collective-permute-start | bytes 589832 | tf_op jit(solution)/shard_map/ppermute | solution.py:348
  6.2 12.9 %collective-permute-start.2 = (f32[408,128]{1,0:T(8,128)}, f32[408,128]{1,0:T(8,128)S(1)}, u32[]{:S(2)}, u32[]{:S(2)}) collective-permute-start(f32[408,128]{1,0:T(8,128)} %get-tuple-element.62), channel_id=1, source_target_pairs={{0,3},{1,2},{2,1},{3,0},{4,7},{5,6},{6,5},{7,4},{8,11},{9,10},{10,... | collective-permute-start | bytes 626696 | tf_op jit(solution)/shard_map/ppermute | solution.py:348
  7.7 16.8 %collective-permute-start.1 = (f32[408,128]{1,0:T(8,128)}, f32[408,128]{1,0:T(8,128)S(1)}, u32[]{:S(2)}, u32[]{:S(2)}) collective-permute-start(f32[408,128]{1,0:T(8,128)} %get-tuple-element.63), channel_id=1, source_target_pairs={{0,2},{1,3},{2,0},{3,1},{4,6},{5,7},{6,4},{7,5},{8,10},{9,11},{10,... | collective-permute-start | bytes 626696 | tf_op jit(solution)/shard_map/ppermute | solution.py:348
  8.0 0.7 copy-start.27
  8.0 0.8 copy-start.23
  8.0 1.1 copy-start.22
  8.1 2.7 %copy-start.21 = (f32[2,1152,4]{1,2,0:T(4,128)S(1)}, f32[2,1152,4]{1,2,0:T(4,128)}, u32[]{:S(2)}) copy-start(f32[2,1152,4]{1,2,0:T(4,128)} %param.17) | copy-start | bytes 110596
  8.1 18.5 %collective-permute-start = (f32[1176,128]{1,0:T(8,128)S(1)}, f32[1176,128]{1,0:T(8,128)S(1)}, u32[]{:S(2)}, u32[]{:S(2)}) collective-permute-start(f32[1176,128]{1,0:T(8,128)S(1)} %pad_maximum_fusion), channel_id=1, source_target_pairs={{0,1},{1,0},{2,3},{3,2},{4,5},{5,4},{6,7},{7,6},{8,9},{9,8},{10,11... | collective-permute-start | bytes 1806344 | tf_op jit(solution)/shard_map/ppermute | solution.py:328
  19.1 19.7 %collective-permute-start.8 = (f32[384,128]{1,0:T(8,128)}, f32[384,128]{1,0:T(8,128)S(1)}, u32[]{:S(2)}, u32[]{:S(2)}) collective-permute-start(f32[384,128]{1,0:T(8,128)} %get-tuple-element.45), channel_id=1, source_target_pairs={{0,3},{1,2},{2,1},{3,0},{4,7},{5,6},{6,5},{7,4},{8,11},{9,10},{10,... | collective-permute-start | bytes 589832 | tf_op jit(solution)/shard_map/ppermute | solution.py:348
  24.5 0.7 copy-start.1
  25.1 13.6 %collective-permute-start.7 = (f32[384,128]{1,0:T(8,128)}, f32[384,128]{1,0:T(8,128)S(1)}, u32[]{:S(2)}, u32[]{:S(2)}) collective-permute-start(f32[384,128]{1,0:T(8,128)} %get-tuple-element.46), channel_id=1, source_target_pairs={{0,2},{1,3},{2,0},{3,1},{4,6},{5,7},{6,4},{7,5},{8,10},{9,11},{10,... | collective-permute-start | bytes 589832 | tf_op jit(solution)/shard_map/ppermute | solution.py:348
  26.6 0.9 copy-start.2
  36.5 0.6 copy-start.4
  37.2 7.9 %copy-start.14 = (f32[2,2,48,128]{3,2,1,0:T(8,128)}, f32[2,2,48,128]{3,2,1,0:T(8,128)S(1)}, u32[]{:S(2)}) copy-start(f32[2,2,48,128]{3,2,1,0:T(8,128)S(1)} %get-tuple-element.39) | copy-start | bytes 294916
  37.2 7.9 %copy-start.16 = (f32[2,2,48,128]{3,2,1,0:T(8,128)}, f32[2,2,48,128]{3,2,1,0:T(8,128)S(1)}, u32[]{:S(2)}) copy-start(f32[2,2,48,128]{3,2,1,0:T(8,128)S(1)} %get-tuple-element.38) | copy-start | bytes 294916
  37.2 23.0 %collective-permute-start.15 = (f32[2,2,48,128]{3,2,1,0:T(8,128)}, f32[2,2,48,128]{3,2,1,0:T(8,128)}, u32[]{:S(2)}, u32[]{:S(2)}) collective-permute-start(f32[2,2,48,128]{3,2,1,0:T(8,128)} %get-tuple-element.37), channel_id=1, source_target_pairs={{0,4},{4,8},{8,12},{12,0},{1,5},{5,9},{9,13},{13,1},{2,6},{6,10},{... | collective-permute-start | bytes 294920 | tf_op jit(solution)/shard_map/ppermute | solution.py:467
  38.8 12.5 %copy-start.20 = (f32[2,4,2,144,4]{3,2,1,4,0:T(2,128)S(1)}, f32[2,4,2,144,4]{3,2,1,4,0:T(2,128)}, u32[]{:S(2)}) copy-start(f32[2,4,2,144,4]{3,2,1,4,0:T(2,128)} %rev.26) | copy-start | bytes 110596
  45.1 0.6 copy-start.7
  45.7 16.2 %collective-permute-start.9 = (f32[2,2,48,128]{3,2,1,0:T(8,128)}, f32[2,2,48,128]{3,2,1,0:T(8,128)}, u32[]{:S(2)}, u32[]{:S(2)}) collective-permute-start(f32[2,2,48,128]{3,2,1,0:T(8,128)} %get-tuple-element.33), channel_id=1, source_target_pairs={{0,4},{4,8},{8,12},{12,0},{1,5},{5,9},{9,13},{13,1},{2,6},{6,10},{... | collective-permute-start | bytes 294920 | tf_op jit(solution)/shard_map/ppermute | solution.py:467
  47.3 18.3 %collective-permute-start.10 = (f32[2,2,48,128]{3,2,1,0:T(8,128)}, f32[2,2,48,128]{3,2,1,0:T(8,128)}, u32[]{:S(2)}, u32[]{:S(2)}) collective-permute-start(f32[2,2,48,128]{3,2,1,0:T(8,128)} %get-tuple-element.34), channel_id=1, source_target_pairs={{0,8},{4,12},{8,0},{12,4},{1,9},{5,13},{9,1},{13,5},{2,10},{6,14},... | collective-permute-start | bytes 294920 | tf_op jit(solution)/shard_map/ppermute | solution.py:467
  48.6 19.9 %collective-permute-start.11 = (f32[2,2,48,128]{3,2,1,0:T(8,128)}, f32[2,2,48,128]{3,2,1,0:T(8,128)}, u32[]{:S(2)}, u32[]{:S(2)}) collective-permute-start(f32[2,2,48,128]{3,2,1,0:T(8,128)} %get-tuple-element.35), channel_id=1, source_target_pairs={{0,12},{4,0},{8,4},{12,8},{1,13},{5,1},{9,5},{13,9},{2,14},{6,2},{... | collective-permute-start | bytes 294920 | tf_op jit(solution)/shard_map/ppermute | solution.py:467
  53.5 0.9 copy-start.3
  54.4 5.7 %copy-start.5 = (f32[2,2,48,128]{3,2,1,0:T(8,128)S(1)}, f32[2,2,48,128]{3,2,1,0:T(8,128)}, u32[]{:S(2)}) copy-start(f32[2,2,48,128]{3,2,1,0:T(8,128)} %copy-done.4) | copy-start | bytes 294916
  54.4 5.7 %copy-start.8 = (f32[2,2,48,128]{3,2,1,0:T(8,128)S(1)}, f32[2,2,48,128]{3,2,1,0:T(8,128)}, u32[]{:S(2)}) copy-start(f32[2,2,48,128]{3,2,1,0:T(8,128)} %copy-done.7) | copy-start | bytes 294916
  54.4 11.2 %copy-start.17 = (f32[2,2,48,128]{3,2,1,0:T(8,128)S(1)}, f32[2,2,48,128]{3,2,1,0:T(8,128)}, u32[]{:S(2)}) copy-start(f32[2,2,48,128]{3,2,1,0:T(8,128)} %copy-done.16) | copy-start | bytes 294916
  54.4 14.1 %copy-start.15 = (f32[2,2,48,128]{3,2,1,0:T(8,128)S(1)}, f32[2,2,48,128]{3,2,1,0:T(8,128)}, u32[]{:S(2)}) copy-start(f32[2,2,48,128]{3,2,1,0:T(8,128)} %copy-done.14) | copy-start | bytes 294916
  60.0 18.0 %copy-start.10 = (f32[2,2,48,128]{3,2,1,0:T(8,128)}, f32[2,2,48,128]{3,2,1,0:T(8,128)S(1)}, u32[]{:S(2)}) copy-start(f32[2,2,48,128]{3,2,1,0:T(8,128)S(1)} %get-tuple-element.28.refs_0_) | copy-start | bytes 294916
  60.0 18.0 %copy-start.19 = (f32[2,4,2,144,4]{3,2,1,4,0:T(2,128)S(1)}, f32[2,4,2,144,4]{3,2,1,4,0:T(2,128)}, u32[]{:S(2)}) copy-start(f32[2,4,2,144,4]{3,2,1,4,0:T(2,128)} %rev.27) | copy-start | bytes 110596
  60.1 17.2 %collective-permute-start.3 = (f32[2,2,48,128]{3,2,1,0:T(8,128)S(1)}, f32[2,2,48,128]{3,2,1,0:T(8,128)S(1)}, u32[]{:S(2)}, u32[]{:S(2)}) collective-permute-start(f32[2,2,48,128]{3,2,1,0:T(8,128)S(1)} %get-tuple-element.29), channel_id=1, source_target_pairs={{0,4},{4,8},{8,12},{12,0},{1,5},{5,9},{9,13},{13,1},{2,6},{6,10},{... | collective-permute-start | bytes 294920 | tf_op jit(solution)/shard_map/ppermute | solution.py:467
  60.2 17.1 %collective-permute-start.4 = (f32[2,2,48,128]{3,2,1,0:T(8,128)S(1)}, f32[2,2,48,128]{3,2,1,0:T(8,128)S(1)}, u32[]{:S(2)}, u32[]{:S(2)}) collective-permute-start(f32[2,2,48,128]{3,2,1,0:T(8,128)S(1)} %get-tuple-element.30), channel_id=1, source_target_pairs={{0,8},{4,12},{8,0},{12,4},{1,9},{5,13},{9,1},{13,5},{2,10},{6,14},... | collective-permute-start | bytes 294920 | tf_op jit(solution)/shard_map/ppermute | solution.py:467
  62.0 15.3 %collective-permute-start.5 = (f32[2,2,48,128]{3,2,1,0:T(8,128)S(1)}, f32[2,2,48,128]{3,2,1,0:T(8,128)S(1)}, u32[]{:S(2)}, u32[]{:S(2)}) collective-permute-start(f32[2,2,48,128]{3,2,1,0:T(8,128)S(1)} %get-tuple-element.31), channel_id=1, source_target_pairs={{0,12},{4,0},{8,4},{12,8},{1,13},{5,1},{9,5},{13,9},{2,14},{6,2},{... | collective-permute-start | bytes 294920 | tf_op jit(solution)/shard_map/ppermute | solution.py:467
  65.6 10.4 %collective-permute-start.16 = (f32[2,2,48,128]{3,2,1,0:T(8,128)S(1)}, f32[2,2,48,128]{3,2,1,0:T(8,128)S(1)}, u32[]{:S(2)}, u32[]{:S(2)}) collective-permute-start(f32[2,2,48,128]{3,2,1,0:T(8,128)S(1)} %copy-done.17), channel_id=1, source_target_pairs={{0,8},{4,12},{8,0},{12,4},{1,9},{5,13},{9,1},{13,5},{2,10},{6,14},... | collective-permute-start | bytes 294920 | tf_op jit(solution)/shard_map/ppermute | solution.py:467
  68.5 7.5 %collective-permute-start.17 = (f32[2,2,48,128]{3,2,1,0:T(8,128)S(1)}, f32[2,2,48,128]{3,2,1,0:T(8,128)S(1)}, u32[]{:S(2)}, u32[]{:S(2)}) collective-permute-start(f32[2,2,48,128]{3,2,1,0:T(8,128)S(1)} %copy-done.15), channel_id=1, source_target_pairs={{0,12},{4,0},{8,4},{12,8},{1,13},{5,1},{9,5},{13,9},{2,14},{6,2},{... | collective-permute-start | bytes 294920 | tf_op jit(solution)/shard_map/ppermute | solution.py:467
  76.0 14.2 %collective-permute-start.12 = (f32[4,2,48,128]{3,2,1,0:T(8,128)}, f32[4,2,48,128]{3,2,1,0:T(8,128)}, u32[]{:S(2)}, u32[]{:S(2)}) collective-permute-start(f32[4,2,48,128]{3,2,1,0:T(8,128)} %pad_maximum_fusion.4), channel_id=1, source_target_pairs={{0,1},{1,0},{2,3},{3,2},{4,5},{5,4},{6,7},{7,6},{8,9},{9,8},{10,11... | collective-permute-start | bytes 589832 | tf_op jit(solution)/shard_map/ppermute | solution.py:476
  76.1 2.3 %copy-start.12 = (f32[2,2,48,128]{3,2,1,0:T(8,128)}, f32[2,2,48,128]{3,2,1,0:T(8,128)S(1)}, u32[]{:S(2)}) copy-start(f32[2,2,48,128]{3,2,1,0:T(8,128)S(1)} %collective-permute-done.17.refs_13_) | copy-start | bytes 294916
  76.8 13.5 %collective-permute-start.18 = (f32[4,2,48,128]{3,2,1,0:T(8,128)}, f32[4,2,48,128]{3,2,1,0:T(8,128)}, u32[]{:S(2)}, u32[]{:S(2)}) collective-permute-start(f32[4,2,48,128]{3,2,1,0:T(8,128)} %pad_maximum_fusion.5), channel_id=1, source_target_pairs={{0,1},{1,0},{2,3},{3,2},{4,5},{5,4},{6,7},{7,6},{8,9},{9,8},{10,11... | collective-permute-start | bytes 589832 | tf_op jit(solution)/shard_map/ppermute | solution.py:476
  78.0 12.2 %collective-permute-start.6 = (f32[4,2,48,128]{3,2,1,0:T(8,128)}, f32[4,2,48,128]{3,2,1,0:T(8,128)}, u32[]{:S(2)}, u32[]{:S(2)}) collective-permute-start(f32[4,2,48,128]{3,2,1,0:T(8,128)} %pad_maximum_fusion.3), channel_id=1, source_target_pairs={{0,1},{1,0},{2,3},{3,2},{4,5},{5,4},{6,7},{7,6},{8,9},{9,8},{10,11... | collective-permute-start | bytes 589832 | tf_op jit(solution)/shard_map/ppermute | solution.py:476
  79.4 10.8 %copy-start.6 = (f32[2,2,48,128]{3,2,1,0:T(8,128)S(1)}, f32[2,2,48,128]{3,2,1,0:T(8,128)}, u32[]{:S(2)}) copy-start(f32[2,2,48,128]{3,2,1,0:T(8,128)} %copy-done.4) | copy-start | bytes 294916
  79.4 10.8 %copy-start.9 = (f32[2,2,48,128]{3,2,1,0:T(8,128)S(1)}, f32[2,2,48,128]{3,2,1,0:T(8,128)}, u32[]{:S(2)}) copy-start(f32[2,2,48,128]{3,2,1,0:T(8,128)} %copy-done.7) | copy-start | bytes 294916
  79.5 10.8 %copy-start.11 = (f32[2,2,48,128]{3,2,1,0:T(8,128)S(1)}, f32[2,2,48,128]{3,2,1,0:T(8,128)}, u32[]{:S(2)}) copy-start(f32[2,2,48,128]{3,2,1,0:T(8,128)} %copy-done.10) | copy-start | bytes 294916
  79.5 10.8 %copy-start.13 = (f32[2,2,48,128]{3,2,1,0:T(8,128)S(1)}, f32[2,2,48,128]{3,2,1,0:T(8,128)}, u32[]{:S(2)}) copy-start(f32[2,2,48,128]{3,2,1,0:T(8,128)} %copy-done.12) | copy-start | bytes 294916
  96.2 9.8 %collective-permute-start.19 = (f32[2,288,128]{2,1,0:T(8,128)S(1)}, f32[2,288,128]{2,1,0:T(8,128)S(1)}, u32[]{:S(2)}, u32[]{:S(2)}) collective-permute-start(f32[2,288,128]{2,1,0:T(8,128)S(1)} %shard_map.98), channel_id=1, source_target_pairs={{0,12},{4,0},{8,4},{12,8},{1,13},{5,1},{9,5},{13,9},{2,14},{6,2},{... | collective-permute-start | bytes 884744 | tf_op jit(solution)/shard_map/ppermute | solution.py:525
  98.5 26.8 %collective-permute-start.20 = (f32[2,288,128]{2,1,0:T(8,128)S(1)}, f32[2,288,128]{2,1,0:T(8,128)S(1)}, u32[]{:S(2)}, u32[]{:S(2)}) collective-permute-start(f32[2,288,128]{2,1,0:T(8,128)S(1)} %shard_map.99), channel_id=1, source_target_pairs={{0,8},{4,12},{8,0},{12,4},{1,9},{5,13},{9,1},{13,5},{2,10},{6,14},... | collective-permute-start | bytes 884744 | tf_op jit(solution)/shard_map/ppermute | solution.py:525
  99.4 25.9 %collective-permute-start.21 = (f32[2,288,128]{2,1,0:T(8,128)S(1)}, f32[2,288,128]{2,1,0:T(8,128)S(1)}, u32[]{:S(2)}, u32[]{:S(2)}) collective-permute-start(f32[2,288,128]{2,1,0:T(8,128)S(1)} %shard_map.100), channel_id=1, source_target_pairs={{0,4},{4,8},{8,12},{12,0},{1,5},{5,9},{9,13},{13,1},{2,6},{6,10},{... | collective-permute-start | bytes 884744 | tf_op jit(solution)/shard_map/ppermute | solution.py:525

commit v2 on v1

v2 whole, which is shorter than its diff:
```python
import functools
import math

import jax
import jax.numpy as jnp
from jax import lax
from jax.experimental import pallas as pl
from jax.experimental.pallas import tpu as pltpu
from jax.sharding import PartitionSpec as P

NDIR = 36
SUBSTEPS = 4
RIM = 2 * SUBSTEPS
GROUP = 16
CHUNKS = 3

plus_factor = 0.4096
minus_factor = 3.160494
cross_factor = 2.007843

VMEM_LIMIT = 16 * 1024 * 1024
whole = pl.BlockSpec(memory_space=pltpu.VMEM)
anywhere = pl.BlockSpec(memory_space=pl.ANY)
scalars = pl.BlockSpec(memory_space=pltpu.SMEM)


def params():
    return pltpu.CompilerParams(vmem_limit_bytes=VMEM_LIMIT)


def cost(micros):
    return pl.CostEstimate(flops=0, bytes_accessed=int(micros * 3.5e6), transcendentals=0)


def chunk_sizes(total):
    groups = total // GROUP
    count = min(CHUNKS, groups)
    return [GROUP * (groups // count + (i < groups % count)) for i in range(count)]


class Window:
    def __init__(self, n_lat, rows):
        self.pair = n_lat == 2
        self.rows = rows
        self.size = 2 * rows + 4 if self.pair else 3 * rows

    def own(self, lat):
        return jnp.where(lat == 0, 2, 2 + self.rows) if self.pair else self.rows

    def received(self, lat):
        if self.pair:
            return [jnp.where(lat == 0, 2 + self.rows, 2)]
        return [0, 2 * self.rows]

    def zeros(self, lat):
        if not self.pair:
            return []
        first = jnp.where(lat == 0, 0, 2 + 2 * self.rows)
        return [first, first + 1]

    def steps(self, lat, substep):
        shrink = 2 * (substep + 1)
        if self.pair:
            return jnp.where(lat == 0, 2, 2 + shrink), 2 * self.rows - shrink
        return shrink, 3 * self.rows - 2 * shrink


def faces_kernel(window, n_lon, place, own, received, after, out, fields):
    lat = place[0]
    rows, lanes = own[0].shape[0] // 3, own[0].shape[1]
    for row in window.zeros(lat):
        fields[row] = jnp.zeros((3, n_lon * lanes), jnp.float32)
    sources = [(window.own(lat), [(ref, 0) for ref in own])]
    for offset, ref in zip(window.received(lat), received):
        sources.append((offset, [(ref, 3 * d) for d in range(n_lon)]))
    for offset, blocks in sources:
        for d, (ref, lead) in enumerate(blocks):
            for f in range(3):
                for row in range(rows):
                    at = (lead + f) * rows + row
                    fields[offset + row, f : f + 1, d * lanes : (d + 1) * lanes] = ref[at : at + 1, :]
    width = n_lon * lanes
    n_class = out.shape[2] // 6
    classes = lax.broadcasted_iota(jnp.int32, (n_class, width), 0).astype(jnp.float32)

    def hots(row):
        wet = fields[row, 0:1, :]
        hot_depth = (classes == fields[row, 1:2, :]).astype(jnp.float32)
        hot_current = (classes == fields[row, 2:3, :]).astype(jnp.float32)
        return wet, jnp.concatenate([hot_depth, hot_current], axis=0)

    def step(row, _):
        wet, hot = hots(row)
        wet_next, hot_next = hots(row + 1)
        east_wet = 0.5 * wet * pltpu.roll(wet, width - 1, 1)
        east = ((hot + pltpu.roll(hot, width - 1, 1)) * east_wet).astype(jnp.bfloat16)
        north = ((hot + hot_next) * (0.5 * wet * wet_next)).astype(jnp.bfloat16)
        span = 2 * n_class
        for copy in range(3):
            out[row, 0, copy * span : (copy + 1) * span, :] = east
            out[row, 1, copy * span : (copy + 1) * span, :] = north
        return 0

    lax.fori_loop(0, window.size - 1, step, 0)
    out[window.size - 1] = jnp.zeros(out.shape[1:], jnp.bfloat16)


def pack_kernel(start, half, rows, place, own_in, head, after, out, sems):
    lead = sum(ref.shape[0] for ref in head)
    length = (out.shape[0] - lead) // len(own_in)
    first = pl.multiple_of((place[2] * half + start) * rows, 8)
    copies = []
    for d, ref in enumerate(own_in):
        to = out.at[pl.ds(lead + d * length, length)]
        copies.append(pltpu.make_async_copy(ref.at[pl.ds(first, length)], to, sems.at[d]))
        copies[-1].start()
    for i, ref in enumerate(head):
        out[i * ref.shape[0] : (i + 1) * ref.shape[0], :] = ref[...]
    for copy in copies:
        copy.wait()


def cross_pack_kernel(d, pieces, after, out, sems):
    copies = []
    for s, ref in enumerate(pieces):
        copies.append(pltpu.make_async_copy(ref.at[d], out.at[s], sems.at[s]))
        copies[-1].start()
    for copy in copies:
        copy.wait()


def gate_kernel(*refs):
    pass


def median_zero(a, b):
    return jnp.maximum(jnp.minimum(a, b), jnp.minimum(jnp.maximum(a, b), 0.0))


def flux(u, c, low, high, slope_low, slope_high):
    rising = u > 0.0
    return u * jnp.where(rising, low, high) + c * jnp.where(rising, slope_low, slope_high)


def propagate_scratch(window, size, lanes, n_lon):
    width = n_lon * lanes
    energy = pltpu.VMEM((window.size, GROUP, width), jnp.float32)
    speed = pltpu.VMEM((window.size, size, width), jnp.float32)
    block = pltpu.VMEM((size * window.rows, lanes), jnp.float32)
    return [energy, energy, speed, speed, speed, speed] + [block] * n_lon + [pltpu.SemaphoreType.DMA((n_lon,))]


def propagate_kernel(
    window, n_lon, n_comp, split, start, half, head, place, tables, faces, wet, own_in, lat_in, after, *refs
):
    outs, scratch = refs[: -7 - n_lon], refs[-7 - n_lon :]
    energy, other, east_u, east_c, north_u, north_c = scratch[:6]
    own_blocks, sems = scratch[6:-1], scratch[-1]
    lat, comp, lon = place[0], place[1], place[2]
    rows, lanes = window.rows, wet.shape[2] // n_lon
    width = n_lon * lanes
    count = east_u.shape[1]
    copies = []
    for d in range(n_lon):
        first = pl.multiple_of((lon * half + start) * rows, 8)
        copies.append(pltpu.make_async_copy(own_in[d].at[pl.ds(first, count * rows)], own_blocks[d], sems.at[d]))
        copies[-1].start()

    def speeds(row, _):
        for which, u_ref, c_ref in ((0, east_u, east_c), (1, north_u, north_c)):
            u = jnp.dot(tables[which], faces[row, which], preferred_element_type=jnp.float32)
            size = jnp.abs(u)
            u_ref[row] = u
            c_ref[row] = 0.5 * size * (1.0 - size)
        return 0

    lax.fori_loop(0, window.size, speeds, 0, unroll=True)

    for copy in copies:
        copy.wait()
    own = window.own(lat)

    def group(g, _):
        first = pl.multiple_of(g * GROUP, GROUP)
        here = pl.ds(first, GROUP)
        for row in window.zeros(lat):
            energy[row] = jnp.zeros((GROUP, width), jnp.float32)
            other[row] = jnp.zeros((GROUP, width), jnp.float32)
        sources = [(own, [(ref, 0) for ref in own_blocks])]
        for offset, ref in zip(window.received(lat), lat_in):
            sources.append((offset, [(ref, head + d * count) for d in range(n_lon)]))
        for offset, blocks in sources:
            for d, (ref, lead) in enumerate(blocks):
                for row in range(rows):
                    at = pl.ds((lead + first) * rows + row, GROUP, stride=rows)
                    sea = wet[offset + row, 0:1, d * lanes : (d + 1) * lanes]
                    energy[offset + row, :, d * lanes : (d + 1) * lanes] = ref[at, :] * sea

        for substep in range(SUBSTEPS):
            base, length = window.steps(lat, substep)
            old, new = (energy, other) if substep % 2 == 0 else (other, energy)
            prior = [old[base + i] for i in (-2, -1, 0, 1)]
            gap = [b - a for a, b in zip(prior, prior[1:])]
            slope_prior, slope_here = median_zero(gap[1], gap[0]), median_zero(gap[2], gap[1])
            south = flux(
                north_u[base - 1, here], north_c[base - 1, here], prior[1], prior[2], slope_prior, slope_here
            )

            def row_step(i, carry):
                south, this, after, gap_after, slope_this = carry
                row = base + i
                beyond = old[row + 2]
                gap_beyond = beyond - after
                slope_after = median_zero(gap_beyond, gap_after)
                north = flux(north_u[row, here], north_c[row, here], this, after, slope_this, slope_after)
                east_cell = pltpu.roll(this, width - 1, 1)
                gap_east = east_cell - this
                gap_west = pltpu.roll(gap_east, 1, 1)
                slope = median_zero(gap_east, gap_west)
                slope_east = pltpu.roll(slope, width - 1, 1)
                east = flux(east_u[row, here], east_c[row, here], this, east_cell, slope, slope_east)
                west = pltpu.roll(east, 1, 1)
                new[row] = this - (east - west) - (north - south)
                return north, after, beyond, gap_beyond, slope_after

            lax.fori_loop(0, length, row_step, (south, prior[2], prior[3], gap[2], slope_here), unroll=True)

        if split:
            share = rows // n_comp
            for r in range(n_comp):
                base = own + lax.rem(comp + r, n_comp) * share
                for d in range(n_lon):
                    for k in range(share):
                        outs[r][d, k, here, :] = energy[base + k, :, d * lanes : (d + 1) * lanes]
        else:
            for row in range(rows):
                for d in range(n_lon):
                    outs[0][row, d, here, :] = energy[own + row, :, d * lanes : (d + 1) * lanes]
        return 0

    lax.fori_loop(0, count // GROUP, group, 0)


def matrix_kernel(names, index, weight, after, out, columns):
    height = out.shape[1]

    @pl.when(pl.program_id(1) == 0)
    def _():
        columns[...] = jnp.transpose(jnp.concatenate([index[0], weight[0]], axis=0))

    base = pl.program_id(1) * height

    def step(i, _):
        at = pl.multiple_of(i * GROUP, GROUP)
        column = columns[pl.ds(base + at, GROUP), :]
        name = names[...]
        made = jnp.zeros((GROUP, name.shape[1]), jnp.float32)
        for corner in range(4):
            made = jnp.where(name == column[:, corner : corner + 1], column[:, corner + 4 : corner + 5], made)
        out[0, pl.ds(at, GROUP), :] = made.astype(jnp.bfloat16)
        return 0

    lax.fori_loop(0, height // GROUP, step, 0, unroll=3)


def transposed_kernel(half, half_own, index, weight, after, out):
    height, total = out.shape[1], out.shape[2]
    base = pl.program_id(1) * height

    def step(i, _):
        at = pl.multiple_of(i * GROUP, GROUP)
        row = base + at + lax.broadcasted_iota(jnp.int32, (GROUP, 1), 0)
        if half != half_own:
            row = jnp.where(row % half < half_own, row // half * half_own + row % half, -1)
        row = jnp.broadcast_to(row.astype(jnp.float32), (GROUP, total))
        made = jnp.zeros((GROUP, total), jnp.float32)
        for corner in range(4):
            made = jnp.where(row == index[0, corner : corner + 1, :], weight[0, corner : corner + 1, :], made)
        out[0, pl.ds(at, GROUP), :] = made.astype(jnp.bfloat16)
        return 0

    lax.fori_loop(0, height // GROUP, step, 0, unroll=3)


def forward_kernel(sizes, n_lon, split, place, matrix, coupling, *refs):
    pieces = refs[:-4]
    energy_out, source_out, source_low_out, low = refs[-4:]
    step = pl.program_id(0)
    block = coupling.shape[0]
    half = block // n_lon
    per_chunk = len(pieces) // len(sizes)
    share, lanes = pieces[0].shape[1], pieces[0].shape[3]

    n_comp = per_chunk - n_lon + 1

    @pl.when(step == 0)
    def _():
        for s in range(n_comp):
            of_comp = lax.rem(place[1] + n_comp - s, n_comp) if split else s
            for d in range(n_lon):
                of_lon = lax.rem(place[2] + n_lon - d, n_lon)
                first = (of_comp * n_lon + of_lon) * half
                for i, size in enumerate(sizes):
                    at = pl.ds(pl.multiple_of(first + sum(sizes[:i]), GROUP), size)
                    group = pieces[i * per_chunk : (i + 1) * per_chunk]
                    for k in range(share):
                        part = group[s][0, k] if d == 0 else group[d - n_lon][s, k]
                        energy_out[at, k * lanes : (k + 1) * lanes] = part
                        low[at, k * lanes : (k + 1) * lanes] = part.astype(jnp.bfloat16)

    here = pl.ds(pl.multiple_of(step * block, GROUP), block)
    energy = energy_out[here, :]
    plus_side = jnp.dot(matrix[0, here, :], low[...], preferred_element_type=jnp.float32)
    minus_side = jnp.dot(matrix[1, here, :], low[...], preferred_element_type=jnp.float32)
    source = coupling[...] * (
        energy * energy * (plus_factor * plus_side + minus_factor * minus_side)
        - cross_factor * energy * plus_side * minus_side
    )
    source_out[...] = source
    source_low_out[...] = source.astype(jnp.bfloat16)


def backward_kernel(s, n_comp, split, place, matrix_t, source_low, energy, source, out):
    block, lanes = out.shape[1], out.shape[2]
    home = lax.rem(place[1] + n_comp - s, n_comp) if split else s
    here = pl.ds(pl.multiple_of(home * block, GROUP), block)
    gain = (
        jnp.dot(matrix_t[0, here, :], source_low[...], preferred_element_type=jnp.float32)
        + jnp.dot(matrix_t[1, here, :], source_low[...], preferred_element_type=jnp.float32)
        - 2.0 * source[here, :]
    )
    result = energy[here, :] + gain / (1.0 + jnp.abs(gain))
    for k in range(out.shape[0]):
        out[k] = result[:, k * lanes : (k + 1) * lanes]


def gather_kernel(rows, place, *refs):
    pieces, out = refs[:-1], refs[-1]
    comp = place[1]
    n_comp = len(pieces)
    share = rows // n_comp
    for r, piece in enumerate(pieces):
        for k in range(share):
            row = lax.rem(comp + r, n_comp) * share + k
            for i in range(0, piece.shape[1], GROUP):
                out[pl.ds(i * rows + row, GROUP, stride=rows), :] = piece[k, i : i + GROUP, :]


def local(
    spectrum,
    sea_mask,
    depth_class,
    current_class,
    speed_table,
    current_table,
    coupling,
    quad_index,
    quad_weight,
):
    comps_local, rows, lanes = spectrum.shape
    n_comp, n_lat, n_lon = (lax.axis_size(a) for a in ("comp", "lat", "lon"))
    comp, lat, lon = (lax.axis_index(a) for a in ("comp", "lat", "lon"))
    place = jnp.stack([lat, comp, lon]).astype(jnp.int32)
    half_own = comps_local // n_lon
    half = -(-half_own // GROUP) * GROUP
    sizes = chunk_sizes(half)
    starts = [sum(sizes[:i]) for i in range(len(sizes))]
    window = Window(n_lat, rows)
    width = n_lon * lanes
    split = rows % n_comp == 0

    if half == half_own:
        flat = spectrum.reshape(comps_local * rows, lanes)
    else:
        flat = spectrum.reshape(n_lon, half_own, rows, lanes)
        flat = jnp.pad(flat, ((0, 0), (0, half - half_own), (0, 0), (0, 0))).reshape(-1, lanes)
    fields = jnp.concatenate([sea_mask, depth_class, current_class]).astype(jnp.float32)
    own_in, own_fields = [flat], [fields]
    for d in range(n_lon - 1, 0, -1):
        pairs = [(i, (i + d) % n_lon) for i in range(n_lon)]
        own_in.append(lax.ppermute(flat, "lon", pairs))
        own_fields.append(lax.ppermute(fields, "lon", pairs))
    if window.pair:
        moves = [[(0, 1), (1, 0)]]
    else:
        moves = [[(i, i + 1) for i in range(n_lat - 1)], [(i + 1, i) for i in range(n_lat - 1)]]
    lat_in, packed = [], []
    for i, (start, size) in enumerate(zip(starts, sizes)):
        head = own_fields if i == 0 else []
        length = n_lon * (size + (0 if i else 3)) * rows
        packed.append(
            pl.pallas_call(
                functools.partial(pack_kernel, start, half, rows),
                out_shape=jax.ShapeDtypeStruct((length, lanes), jnp.float32),
                in_specs=[scalars, [anywhere] * n_lon, [whole] * len(head), [anywhere] * (i > 0)],
                out_specs=whole,
                scratch_shapes=[pltpu.SemaphoreType.DMA((n_lon,))],
                compiler_params=params(),
                cost_estimate=cost(1),
            )(place, own_in, head, packed[-1:])
        )
        lat_in.append([lax.ppermute(packed[i], "lat", move) for move in moves])

    total = n_comp * n_lon * half
    block = n_lon * half

    def spread(array):
        if half == half_own:
            return array
        array = array.reshape(array.shape[:-1] + (n_comp * n_lon, half_own))
        array = jnp.pad(array, ((0, 0),) * (array.ndim - 1) + ((0, half - half_own),), constant_values=-1)
        return array.reshape(array.shape[:-2] + (total,))

    names = spread(jnp.arange(n_comp * comps_local, dtype=jnp.float32)[None])
    index = spread(jnp.swapaxes(quad_index, 1, 2).astype(jnp.float32))
    weight = jnp.maximum(spread(jnp.swapaxes(quad_weight, 1, 2)), 0.0)
    strength = spread(coupling[None]).reshape(total, 1)
    by_cols = pl.BlockSpec((1, 4, total), lambda s, i: (s, 0, 0))
    by_block = pl.BlockSpec((1, block, total), lambda s, i: (s, i, 0))
    matrix = pl.pallas_call(
        matrix_kernel,
        grid=(2, n_comp),
        out_shape=pltpu.VMEM((2, total, total), jnp.bfloat16),
        in_specs=[whole, by_cols, by_cols, anywhere],
        out_specs=by_block,
        scratch_shapes=[pltpu.VMEM((total, 8), jnp.float32)],
        compiler_params=params(),
        cost_estimate=cost(6),
    )(names, index, weight, packed[-1])

    n_class = speed_table.shape[0]
    head_block = pl.BlockSpec((3 * n_lon * rows, lanes), lambda i: (0, 0))
    faces, window_fields = pl.pallas_call(
        functools.partial(faces_kernel, window, n_lon),
        grid=(1,),
        out_shape=(
            jax.ShapeDtypeStruct((window.size, 2, 6 * n_class, width), jnp.bfloat16),
            jax.ShapeDtypeStruct((window.size, 3, width), jnp.float32),
        ),
        in_specs=[scalars, [whole] * n_lon, [head_block] * len(moves), anywhere],
        out_specs=(whole, whole),
        compiler_params=params(),
        cost_estimate=cost(2),
    )(place, own_fields, lat_in[0], matrix)

    ids = comp * comps_local + lon * half_own + jnp.arange(half, dtype=jnp.int32)
    freq_hot = ((ids // NDIR)[:, None] == jnp.arange(speed_table.shape[1], dtype=jnp.int32)[None, :]).astype(
        jnp.float32
    )
    speed = jnp.dot(freq_hot, speed_table.T, precision=lax.Precision.HIGHEST)
    angles = 2.0 * math.pi / NDIR * (ids % NDIR).astype(jnp.float32)
    tables = []
    for which, turn in ((0, jnp.cos(angles)), (1, jnp.sin(angles))):
        currents = jnp.broadcast_to(current_table[:, which][None], (half, n_class))
        left = jnp.concatenate([speed * turn[:, None], currents], axis=1)
        levels = []
        for _ in range(3):
            level = lax.reduce_precision(left, 8, 7)
            levels.append(level)
            left = left - level
        tables.append(jnp.concatenate(levels, axis=1).astype(jnp.bfloat16))
    tables = jnp.stack(tables)

    if split:
        share, span = rows // n_comp, lanes
    else:
        groups = n_comp // rows
        share, span = 1, lanes // groups
    arrived = []
    for i, (start, size) in enumerate(zip(starts, sizes)):
        table = lax.slice_in_dim(tables, start, start + size, axis=1)
        if split:
            shapes = [jax.ShapeDtypeStruct((n_lon, share, size, lanes), jnp.float32)] * n_comp
        else:
            shapes = [jax.ShapeDtypeStruct((rows, n_lon, size, lanes), jnp.float32)]
        pieces = pl.pallas_call(
            functools.partial(
                propagate_kernel, window, n_lon, n_comp, split, start, half, 0 if i else 3 * n_lon
            ),
            out_shape=shapes,
            in_specs=[
                scalars,
                whole,
                whole,
                whole,
                [anywhere] * n_lon,
                [whole] * len(moves),
                anywhere,
            ],
            out_specs=[whole] * len(shapes),
            scratch_shapes=propagate_scratch(window, size, lanes, n_lon),
            compiler_params=params(),
            cost_estimate=cost(1.5 + 0.11 * size),
        )(
            place,
            table,
            faces,
            window_fields,
            own_in,
            lat_in[i],
            matrix if i == 0 else pieces[0],
        )
        if split:
            sent = pieces[1:]
            if i > 0:
                sent = pl.pallas_call(
                    gate_kernel,
                    out_shape=shapes[1:],
                    in_specs=[anywhere] * (2 * len(sent)),
                    out_specs=[anywhere] * len(sent),
                    input_output_aliases={j: j for j in range(len(sent))},
                    compiler_params=params(),
                    cost_estimate=cost(0.1),
                )(*sent, *moved[1:])
            moved = [pieces[0]]
            for r in range(1, n_comp):
                pairs = [(a, (a + r) % n_comp) for a in range(n_comp)]
                moved.append(lax.ppermute(sent[r - 1], "comp", pairs))
        else:
            energy = pieces[0].reshape(rows, n_lon, size, groups, span)
            energy = jnp.transpose(energy, (0, 3, 1, 2, 4)).reshape(n_comp, n_lon, 1, size, span)
            energy = lax.all_to_all(energy, "comp", split_axis=0, concat_axis=0, tiled=True)
            moved = [energy[s] for s in range(n_comp)]
        after = []
        if i == len(sizes) - 1:
            matrix_t = pl.pallas_call(
                functools.partial(transposed_kernel, half, half_own),
                grid=(2, n_comp),
                out_shape=pltpu.VMEM((2, total, total), jnp.bfloat16),
                in_specs=[by_cols, by_cols, anywhere],
                out_specs=by_block,
                compiler_params=params(),
                cost_estimate=cost(4),
            )(index, weight, pieces[0])
            after = [matrix_t]
        crossed = []
        for d in range(1, n_lon):
            pairs = [(b, (b + d) % n_lon) for b in range(n_lon)]
            packed = pl.pallas_call(
                functools.partial(cross_pack_kernel, d),
                out_shape=jax.ShapeDtypeStruct((n_comp, share, size, span), jnp.float32),
                in_specs=[[anywhere] * n_comp, [anywhere] * len(after)],
                out_specs=whole,
                scratch_shapes=[pltpu.SemaphoreType.DMA((n_comp,))],
                compiler_params=params(),
                cost_estimate=cost(1),
            )(moved, after)
            crossed.append(lax.ppermute(packed, "lon", pairs))
        arrived += moved + crossed

    cells = share * span
    energy, source, source_low = pl.pallas_call(
        functools.partial(forward_kernel, sizes, n_lon, split),
        grid=(n_comp,),
        out_shape=(
            jax.ShapeDtypeStruct((total, cells), jnp.float32),
            jax.ShapeDtypeStruct((total, cells), jnp.float32),
            jax.ShapeDtypeStruct((total, cells), jnp.bfloat16),
        ),
        in_specs=[
            scalars,
            whole,
            pl.BlockSpec((block, 1), lambda s: (s, 0)),
        ]
        + [whole] * len(arrived),
        out_specs=(
            pl.BlockSpec((total, cells), lambda s: (0, 0)),
            pl.BlockSpec((block, cells), lambda s: (s, 0)),
            pl.BlockSpec((block, cells), lambda s: (s, 0)),
        ),
        scratch_shapes=[pltpu.VMEM((total, cells), jnp.bfloat16)],
        compiler_params=params(),
        cost_estimate=cost(4),
    )(place, matrix, strength, *arrived)

    back = []
    for s in range(n_comp):
        back.append(
            pl.pallas_call(
                functools.partial(backward_kernel, s, n_comp, split),
                out_shape=jax.ShapeDtypeStruct((share, block, span), jnp.float32),
                in_specs=[scalars] + [whole] * 4,
                out_specs=whole,
                compiler_params=params(),
                cost_estimate=cost(0.6),
            )(place, matrix_t, source_low, energy, source)
        )

    if split:
        home = [back[0]]
        for r in range(1, n_comp):
            home.append(lax.ppermute(back[r], "comp", [(a, (a - r) % n_comp) for a in range(n_comp)]))
        if half == half_own:
            out = pl.pallas_call(
                functools.partial(gather_kernel, rows),
                out_shape=jax.ShapeDtypeStruct((comps_local * rows, lanes), jnp.float32),
                in_specs=[scalars] + [whole] * n_comp,
                out_specs=whole,
                compiler_params=params(),
                cost_estimate=cost(2),
            )(place, *home)
            return out.reshape(comps_local, rows, lanes)
        home = jnp.stack(home).reshape(n_comp, share, n_lon, half, lanes)[:, :, :, :half_own]
        home = jnp.roll(home, comp, 0)
        return jnp.transpose(home, (2, 3, 0, 1, 4)).reshape(comps_local, rows, lanes)
    home = lax.all_to_all(jnp.concatenate(back), "comp", split_axis=0, concat_axis=0, tiled=True)
    home = home.reshape(rows, groups, n_lon, half, span)[:, :, :, :half_own]
    return jnp.transpose(home, (2, 3, 0, 1, 4)).reshape(comps_local, rows, lanes)


def solution(mesh):
    placed = (
        P(("ens", "comp"), "lat", "lon"),
        P("lat", "lon"),
        P("lat", "lon"),
        P("lat", "lon"),
        P(),
        P(),
        P(),
        P(),
        P(),
    )
    return jax.shard_map(
        local,
        mesh=mesh,
        in_specs=placed,
        out_specs=P(("ens", "comp"), "lat", "lon"),
        check_vma=False,
    )
```

time: 128 us -> 102 us (0.80)
  waiting for transfers between devices: 40.8 us -> 25.9 us
  local copies, waits for them, and re-layouts: 14.5 us -> 2.61 us
  Pallas kernels: 40 us -> 45 us
  other arithmetic: 4.69 us -> 2.8 us
  starting transfers between devices: 26.4 us -> 24.7 us
    ppermute x19 -> x17, waiting for transfers between devices: 15.5 us -> 1.29 us  [the longest x3 1.2 us: local(): crossed.append(lax.ppermute(packed, 'lon', pairs))]
    slice x13 -> x0, local copies, waits for them, and re-layouts: 5.63 us -> none  [the longest x12 3.25 us: local(): piece[d]]
    pallas_call x7 -> x16, Pallas kernels: 19.1 us -> 24.3 us  [the longest x1 7.33 us: local(): pl.pallas_call(matrix_kernel, grid=(2, n_comp), out_shape=pltpu.VMEM((2,...]
    unnamed x56 -> x8, local copies, waits for them, and re-layouts: 4.17 us -> 1.28 us
    rev x6 -> x0, local copies, waits for them, and re-layouts: 2.48 us -> none  [turned(): return jnp.roll(jnp.flip(array, axis), position + 1, axis)]
    ppermute x19 -> x17, starting transfers between devices: 23.2 us -> 20.8 us  [the longest x9 14.5 us: local(): moved.append(lax.ppermute(sent[r - 1], 'comp', pairs))]
    another operation x3 -> x0, other arithmetic: 2.08 us -> none  [local(): jnp.stack([piece[d] for piece in moved])]
    concatenate x8 -> x0, other arithmetic: 1.89 us -> none  [the longest x6 1.04 us: turned(): return jnp.roll(jnp.flip(array, axis), position + 1, axis)]
  transfers between devices with their start and end apart: 22 -> 20, of which waited for: 5 -> 5; matrix products, arithmetic and copies ran while one was open for 10% -> 4% of each run, Pallas kernels for 25% -> 35%
where the time goes in v2:
time: 102 us
  Pallas kernels  45 us (44%)
  waiting for transfers between devices  25.9 us (25%)
  starting transfers between devices  24.7 us (24%)
  other arithmetic  2.8 us (3%)
  local copies, waits for them, and re-layouts  2.61 us (3%)
    ppermute x3, waiting for transfers between devices, local(): lax.ppermute(back[r], 'comp', [(a, (a - r) % n_comp) for a in range(n_com...  24.7 us
    pallas_call x3, Pallas kernels, local(): pl.pallas_call(functools.partial(propagate_kernel, window, n_lon, n_comp,...  18.4 us
    ppermute x9, starting transfers between devices, local(): moved.append(lax.ppermute(sent[r - 1], 'comp', pairs))  14.5 us
    pallas_call x1, Pallas kernels, local(): pl.pallas_call(matrix_kernel, grid=(2, n_comp), out_shape=pltpu.VMEM((2,...  7.33 us
    ppermute x3, starting transfers between devices, local(): lat_in.append([lax.ppermute(packed[i], 'lat', move) for move in moves])  5.16 us
    pallas_call x4, Pallas kernels, local(): pl.pallas_call(functools.partial(backward_kernel, s, n_comp, split), out_...  4.43 us
    ppermute x3, starting transfers between devices, local(): lax.ppermute(back[r], 'comp', [(a, (a - r) % n_comp) for a in range(n_com...  3.87 us
    pallas_call x1, Pallas kernels, local(): pl.pallas_call(functools.partial(transposed_kernel, half, half_own), grid...  3.63 us
  transfers between devices with their start and end apart: 20, of which 5 were waited for; matrix products, arithmetic and copies ran while one was open for 4% of the time, Pallas kernels for 35%

profile of v2, /device:TPU:0, one launch (start us, length us, event | category | flops | bytes accessed | tf_op | source)
XLA Modules:
  0.0 101.5 jit_solution(12960089118919435804)
XLA Ops:
  0.0 0.7 add_convert_fusion.head_0_.own_0_
  0.7 0.5 collective-permute-start
  1.2 0.1 collective-permute-start.1
  1.3 0.1 fusion.16
  1.3 0.8 slice_bitcast_fusion.1
  2.1 0.1 pad.12.clone
  2.2 0.1 pad.10.clone
  2.2 0.2 broadcast_multiply_fusion.1
  2.4 0.1 pad_maximum_fusion.1
  2.6 0.1 copy.23
  2.7 0.1 pad_maximum_fusion
  2.8 0.8 convert_bitcast_fusion.index
  3.6 0.8 maximum_bitcast_fusion.weight
  4.3 0.1 pad_add_fusion.place
  4.4 0.1 copy.21
  4.5 0.0 collective-permute-done.1.own_in_1_
  4.5 0.0 copy-start.1
  4.5 1.3 %copy-done.1 = f32[288,8,128]{2,1,0:T(8,128)S(1)} copy-done((f32[288,8,128]{2,1,0:T(8,128)S(1)}, f32[288,8,128]{2,1,0:T(8,128)}, u32[]{:S(2)}) %copy-start.1) | copy-done | bytes 1179672
  5.8 1.1 %shard_map.91.after_0_ = f32[816,128]{1,0:T(8,128)S(1)} custom-call(s32[3]{0:T(128)S(1)} %pad_add_fusion.place, f32[2304,128]{1,0:T(8,128)S(1)} %bitcast.27, f32[2304,128]{1,0:T(8,128)S(1)} %collective-permute-done.1.own_in_1_, f32[24,128]{1,0:T(8,128)S(1)} %add_convert_fusion.head_0_.own_0_, f32[24,128]{1,0:T(8,128)S(1)} %collective-permute-done.head_1_.own_1_), custom_call_target="tpu_custom_call" | custom-call | bytes 3500000 | tf_op jit(solution)/shard_map/pallas_call | solution.py:392
  6.9 3.0 %collective-permute-start.2 = (f32[816,128]{1,0:T(8,128)S(1)}, f32[816,128]{1,0:T(8,128)S(1)}, u32[]{:S(2)}, u32[]{:S(2)}) collective-permute-start(f32[816,128]{1,0:T(8,128)S(1)} %shard_map.91.after_0_), channel_id=1, source_target_pairs={{0,2},{2,0},{1,3},{3,1},{4,6},{6,4},{5,7},{7,5},{8,10},{10,8},{9,1... | collective-permute-start | bytes 1253384 | tf_op jit(solution)/shard_map/ppermute | solution.py:402
  9.9 1.1 %shard_map.92.after_0_ = f32[768,128]{1,0:T(8,128)S(1)} custom-call(s32[3]{0:T(128)S(1)} %pad_add_fusion.place, f32[2304,128]{1,0:T(8,128)S(1)} %bitcast.28, f32[2304,128]{1,0:T(8,128)S(1)} %collective-permute-done.1.own_in_1_, f32[816,128]{1,0:T(8,128)S(1)} %shard_map.91.after_0_), custom_call_target="tpu_custom_call" | custom-call | bytes 3500000 | tf_op jit(solution)/shard_map/pallas_call | solution.py:392
  11.0 0.1 collective-permute-start.4
  11.1 0.1 maximum_maximum_fusion
  11.2 1.1 %shard_map.93.after = f32[768,128]{1,0:T(8,128)S(1)} custom-call(s32[3]{0:T(128)S(1)} %pad_add_fusion.place, f32[2304,128]{1,0:T(8,128)S(1)} %bitcast.29, f32[2304,128]{1,0:T(8,128)S(1)} %collective-permute-done.1.own_in_1_, f32[768,128]{1,0:T(8,128)S(1)} %shard_map.92.after_0_), custom_call_target="tpu_custom_call" | custom-call | bytes 3500000 | tf_op jit(solution)/shard_map/pallas_call | solution.py:392
  12.3 2.1 %collective-permute-start.3 = (f32[768,128]{1,0:T(8,128)S(1)}, f32[768,128]{1,0:T(8,128)S(1)}, u32[]{:S(2)}, u32[]{:S(2)}) collective-permute-start(f32[768,128]{1,0:T(8,128)S(1)} %shard_map.93.after), channel_id=1, source_target_pairs={{0,2},{2,0},{1,3},{3,1},{4,6},{6,4},{5,7},{7,5},{8,10},{10,8},{9,1... | collective-permute-start | bytes 1179656 | tf_op jit(solution)/shard_map/ppermute | solution.py:402
  14.4 7.3 %shard_map.94.after.matrix = bf16[2,1152,1152]{2,1,0:T(8,128)(2,1)S(1)} custom-call(f32[1,1152]{1,0:T(1,128)S(1)} %iota.18.names, f32[2,4,1152]{2,1,0:T(4,128)S(1)} %convert_bitcast_fusion.index, f32[2,4,1152]{2,1,0:T(4,128)S(1)} %maximum_bitcast_fusion.weight, f32[768,128]{1,0:T(8,128)S(1)} %shard_map.93.after), custom_call_target="tpu_custom_call" | custom-call | bytes 21000000 | tf_op jit(solution)/shard_map/pallas_call | solution.py:420
  21.7 0.0 copy-start.2
  21.7 2.2 %shard_map.95 = (bf16[20,2,96,256]{3,2,1,0:T(8,128)(2,1)S(1)}, f32[20,3,256]{2,1,0:T(4,128)S(1)}) custom-call(s32[3]{0:T(128)S(1)} %pad_add_fusion.place, f32[24,128]{1,0:T(8,128)S(1)} %add_convert_fusion.head_0_.own_0_, f32[24,128]{1,0:T(8,128)S(1)} %collective-permute-done.head_1_.own_1_, f32[816,128]{1,0:T(8,128)S(1)} %collective-permute-done.2.received_0_.lat_in_0_, ...), custom_call_target="tpu_custom_call" | custom-call | bytes 7000000 | tf_op jit(solution)/shard_map/pallas_call | solution.py:433
  24.0 6.1 %shard_map.96 = (f32[2,2,48,128]{3,2,1,0:T(8,128)S(1)}, f32[2,2,48,128]{3,2,1,0:T(8,128)S(1)}, f32[2,2,48,128]{3,2,1,0:T(8,128)S(1)}, f32[2,2,48,128]{3,2,1,0:T(8,128)S(1)}) custom-call(s32[3]{0:T(128)S(1)} %pad_add_fusion.place, bf16[2,48,96]{2,1,0:T(8,128)(2,1)S(1)} %get-tuple-element.51.tables, bf16[20,2,96,256]{3,2,1,0:T(8,128)(2,1)S(1)} %get-tuple-element.28.faces, ...), custom_call_target="tpu_custom_call" | custom-call | bytes 23730000 | tf_op jit(solution)/shard_map/pallas_call | solution.py:476
  30.1 1.6 %collective-permute-start.5 = (f32[2,2,48,128]{3,2,1,0:T(8,128)S(1)}, f32[2,2,48,128]{3,2,1,0:T(8,128)S(1)}, u32[]{:S(2)}, u32[]{:S(2)}) collective-permute-start(f32[2,2,48,128]{3,2,1,0:T(8,128)S(1)} %get-tuple-element.33), channel_id=1, source_target_pairs={{0,4},{4,8},{8,12},{12,0},{1,5},{5,9},{9,13},{13,1},{2,6},{6,10},{... | collective-permute-start | bytes 294920 | tf_op jit(solution)/shard_map/ppermute | solution.py:518
  31.7 2.6 %collective-permute-start.6 = (f32[2,2,48,128]{3,2,1,0:T(8,128)S(1)}, f32[2,2,48,128]{3,2,1,0:T(8,128)S(1)}, u32[]{:S(2)}, u32[]{:S(2)}) collective-permute-start(f32[2,2,48,128]{3,2,1,0:T(8,128)S(1)} %get-tuple-element.34), channel_id=1, source_target_pairs={{0,8},{4,12},{8,0},{12,4},{1,9},{5,13},{9,1},{13,5},{2,10},{6,14},... | collective-permute-start | bytes 294920 | tf_op jit(solution)/shard_map/ppermute | solution.py:518
  34.3 1.3 %collective-permute-start.7 = (f32[2,2,48,128]{3,2,1,0:T(8,128)S(1)}, f32[2,2,48,128]{3,2,1,0:T(8,128)S(1)}, u32[]{:S(2)}, u32[]{:S(2)}) collective-permute-start(f32[2,2,48,128]{3,2,1,0:T(8,128)S(1)} %get-tuple-element.35), channel_id=1, source_target_pairs={{0,12},{4,0},{8,4},{12,8},{1,13},{5,1},{9,5},{13,9},{2,14},{6,2},{... | collective-permute-start | bytes 294920 | tf_op jit(solution)/shard_map/ppermute | solution.py:518
  35.7 0.0 collective-permute-done.4.lat_in_0_
  35.7 6.1 %shard_map.97 = (f32[2,2,48,128]{3,2,1,0:T(8,128)S(1)}, f32[2,2,48,128]{3,2,1,0:T(8,128)S(1)}, f32[2,2,48,128]{3,2,1,0:T(8,128)S(1)}, f32[2,2,48,128]{3,2,1,0:T(8,128)S(1)}) custom-call(s32[3]{0:T(128)S(1)} %pad_add_fusion.place, bf16[2,48,96]{2,1,0:T(8,128)(2,1)S(1)} %get-tuple-element.52.tables, bf16[20,2,96,256]{3,2,1,0:T(8,128)(2,1)S(1)} %get-tuple-element.28.faces, ...), custom_call_target="tpu_custom_call" | custom-call | bytes 23730000 | tf_op jit(solution)/shard_map/pallas_call | solution.py:476
  41.9 0.9 collective-permute-start.9
  42.8 1.7 %collective-permute-start.10 = (f32[2,2,48,128]{3,2,1,0:T(8,128)S(1)}, f32[2,2,48,128]{3,2,1,0:T(8,128)S(1)}, u32[]{:S(2)}, u32[]{:S(2)}) collective-permute-start(f32[2,2,48,128]{3,2,1,0:T(8,128)S(1)} %get-tuple-element.40), channel_id=1, source_target_pairs={{0,8},{4,12},{8,0},{12,4},{1,9},{5,13},{9,1},{13,5},{2,10},{6,14},... | collective-permute-start | bytes 294920 | tf_op jit(solution)/shard_map/ppermute | solution.py:518
  44.5 1.3 %collective-permute-start.11 = (f32[2,2,48,128]{3,2,1,0:T(8,128)S(1)}, f32[2,2,48,128]{3,2,1,0:T(8,128)S(1)}, u32[]{:S(2)}, u32[]{:S(2)}) collective-permute-start(f32[2,2,48,128]{3,2,1,0:T(8,128)S(1)} %get-tuple-element.41), channel_id=1, source_target_pairs={{0,12},{4,0},{8,4},{12,8},{1,13},{5,1},{9,5},{13,9},{2,14},{6,2},{... | collective-permute-start | bytes 294920 | tf_op jit(solution)/shard_map/ppermute | solution.py:518
  45.8 6.1 %shard_map.98 = (f32[2,2,48,128]{3,2,1,0:T(8,128)S(1)}, f32[2,2,48,128]{3,2,1,0:T(8,128)S(1)}, f32[2,2,48,128]{3,2,1,0:T(8,128)S(1)}, f32[2,2,48,128]{3,2,1,0:T(8,128)S(1)}) custom-call(s32[3]{0:T(128)S(1)} %pad_add_fusion.place, bf16[2,48,96]{2,1,0:T(8,128)(2,1)S(1)} %get-tuple-element.53.tables, bf16[20,2,96,256]{3,2,1,0:T(8,128)(2,1)S(1)} %get-tuple-element.28.faces, ...), custom_call_target="tpu_custom_call" | custom-call | bytes 23730000 | tf_op jit(solution)/shard_map/pallas_call | solution.py:476
  52.0 1.7 %collective-permute-start.13 = (f32[2,2,48,128]{3,2,1,0:T(8,128)S(1)}, f32[2,2,48,128]{3,2,1,0:T(8,128)S(1)}, u32[]{:S(2)}, u32[]{:S(2)}) collective-permute-start(f32[2,2,48,128]{3,2,1,0:T(8,128)S(1)} %get-tuple-element.45), channel_id=1, source_target_pairs={{0,4},{4,8},{8,12},{12,0},{1,5},{5,9},{9,13},{13,1},{2,6},{6,10},{... | collective-permute-start | bytes 294920 | tf_op jit(solution)/shard_map/ppermute | solution.py:518
  53.6 1.3 %collective-permute-start.14 = (f32[2,2,48,128]{3,2,1,0:T(8,128)S(1)}, f32[2,2,48,128]{3,2,1,0:T(8,128)S(1)}, u32[]{:S(2)}, u32[]{:S(2)}) collective-permute-start(f32[2,2,48,128]{3,2,1,0:T(8,128)S(1)} %get-tuple-element.46), channel_id=1, source_target_pairs={{0,8},{4,12},{8,0},{12,4},{1,9},{5,13},{9,1},{13,5},{2,10},{6,14},... | collective-permute-start | bytes 294920 | tf_op jit(solution)/shard_map/ppermute | solution.py:518
  54.9 2.0 %collective-permute-start.15 = (f32[2,2,48,128]{3,2,1,0:T(8,128)S(1)}, f32[2,2,48,128]{3,2,1,0:T(8,128)S(1)}, u32[]{:S(2)}, u32[]{:S(2)}) collective-permute-start(f32[2,2,48,128]{3,2,1,0:T(8,128)S(1)} %get-tuple-element.47), channel_id=1, source_target_pairs={{0,12},{4,0},{8,4},{12,8},{1,13},{5,1},{9,5},{13,9},{2,14},{6,2},{... | collective-permute-start | bytes 294920 | tf_op jit(solution)/shard_map/ppermute | solution.py:518
  57.0 3.6 %shard_map.99.after_0_.matrix_t = bf16[2,1152,1152]{2,1,0:T(8,128)(2,1)S(1)} custom-call(f32[2,4,1152]{2,1,0:T(4,128)S(1)} %convert_bitcast_fusion.index, f32[2,4,1152]{2,1,0:T(4,128)S(1)} %maximum_bitcast_fusion.weight, f32[2,2,48,128]{3,2,1,0:T(8,128)S(1)} %get-tuple-element.32.after.pieces_0_.refs_10_), custom_call_target="tpu_custom_call" | custom-call | bytes 14000000 | tf_op jit(solution)/shard_map/pallas_call | solution.py:526
  60.6 0.3 shard_map.100
  60.9 0.1 collective-permute-start.8
  61.0 0.3 shard_map.102
  61.3 0.0 copy-start.3
  61.3 0.5 collective-permute-start.12
  61.8 0.1 collective-permute-done.14.pieces_2_.refs_12_
  61.9 0.3 shard_map.104
  62.2 0.1 collective-permute-start.16
  62.3 0.2 reshape_broadcast_in_dim.4.coupling
  62.5 0.4 collective-permute-done.12.refs_9_
  62.9 0.8 collective-permute-done.16.refs_14_
  63.7 3.1 %shard_map.105 = (f32[1152,256]{1,0:T(8,128)S(1)}, f32[1152,256]{1,0:T(8,128)S(1)}, bf16[1152,256]{1,0:T(8,128)(2,1)S(1)}) custom-call(s32[3]{0:T(128)S(1)} %pad_add_fusion.place, bf16[2,1152,1152]{2,1,0:T(8,128)(2,1)S(1)} %shard_map.94.after.matrix, f32[1152,1]{1,0:T(8,128)S(1)} %reshape_broadcast_in_dim.4.coupling, ...), custom_call_target="tpu_custom_call" | custom-call | bytes 14000000 | tf_op jit(solution)/shard_map/pallas_call | solution.py:552
  66.8 1.1 %shard_map.109 = f32[2,288,128]{2,1,0:T(8,128)S(1)} custom-call(s32[3]{0:T(128)S(1)} %pad_add_fusion.place, bf16[2,1152,1152]{2,1,0:T(8,128)(2,1)S(1)} %shard_map.99.after_0_.matrix_t, bf16[1152,256]{1,0:T(8,128)(2,1)S(1)} %get-tuple-element.48.source_low, f32[1152,256]{1,0:T(8,128)S(1)} %get-tuple-element.49.energy, f32[1152,256]{1,0:T(8,128)S(1)} %get-tuple-element.50.source), custom_call_target="tpu_custom_call" | custom-call | bytes 2100000 | tf_op jit(solution)/shard_map/pallas_call | solution.py:579
  67.9 1.1 %shard_map.108 = f32[2,288,128]{2,1,0:T(8,128)S(1)} custom-call(s32[3]{0:T(128)S(1)} %pad_add_fusion.place, bf16[2,1152,1152]{2,1,0:T(8,128)(2,1)S(1)} %shard_map.99.after_0_.matrix_t, bf16[1152,256]{1,0:T(8,128)(2,1)S(1)} %get-tuple-element.48.source_low, f32[1152,256]{1,0:T(8,128)S(1)} %get-tuple-element.49.energy, f32[1152,256]{1,0:T(8,128)S(1)} %get-tuple-element.50.source), custom_call_target="tpu_custom_call" | custom-call | bytes 2100000 | tf_op jit(solution)/shard_map/pallas_call | solution.py:579
  69.0 1.1 %shard_map.107 = f32[2,288,128]{2,1,0:T(8,128)S(1)} custom-call(s32[3]{0:T(128)S(1)} %pad_add_fusion.place, bf16[2,1152,1152]{2,1,0:T(8,128)(2,1)S(1)} %shard_map.99.after_0_.matrix_t, bf16[1152,256]{1,0:T(8,128)(2,1)S(1)} %get-tuple-element.48.source_low, f32[1152,256]{1,0:T(8,128)S(1)} %get-tuple-element.49.energy, f32[1152,256]{1,0:T(8,128)S(1)} %get-tuple-element.50.source), custom_call_target="tpu_custom_call" | custom-call | bytes 2100000 | tf_op jit(solution)/shard_map/pallas_call | solution.py:579
  70.2 3.2 %collective-permute-start.17 = (f32[2,288,128]{2,1,0:T(8,128)S(1)}, f32[2,288,128]{2,1,0:T(8,128)S(1)}, u32[]{:S(2)}, u32[]{:S(2)}) collective-permute-start(f32[2,288,128]{2,1,0:T(8,128)S(1)} %shard_map.107), channel_id=1, source_target_pairs={{0,12},{4,0},{8,4},{12,8},{1,13},{5,1},{9,5},{13,9},{2,14},{6,2},{... | collective-permute-start | bytes 884744 | tf_op jit(solution)/shard_map/ppermute | solution.py:592
  73.4 0.4 collective-permute-start.18
  73.8 0.2 collective-permute-start.19
  74.0 1.1 %shard_map.106.refs_0_ = f32[2,288,128]{2,1,0:T(8,128)S(1)} custom-call(s32[3]{0:T(128)S(1)} %pad_add_fusion.place, bf16[2,1152,1152]{2,1,0:T(8,128)(2,1)S(1)} %shard_map.99.after_0_.matrix_t, bf16[1152,256]{1,0:T(8,128)(2,1)S(1)} %get-tuple-element.48.source_low, f32[1152,256]{1,0:T(8,128)S(1)} %get-tuple-element.49.energy, ...), custom_call_target="tpu_custom_call" | custom-call | bytes 2100000 | tf_op jit(solution)/shard_map/pallas_call | solution.py:579
  75.2 5.7 %collective-permute-done.17.refs_1_ = f32[2,288,128]{2,1,0:T(8,128)S(1)} collective-permute-done((f32[2,288,128]{2,1,0:T(8,128)S(1)}, f32[2,288,128]{2,1,0:T(8,128)S(1)}, u32[]{:S(2)}, u32[]{:S(2)}) %collective-permute-start.17) | collective-permute-done | bytes 294944 | tf_op jit(solution)/shard_map/ppermute | solution.py:592
  80.9 18.9 %collective-permute-done.18.refs_2_ = f32[2,288,128]{2,1,0:T(8,128)S(1)} collective-permute-done((f32[2,288,128]{2,1,0:T(8,128)S(1)}, f32[2,288,128]{2,1,0:T(8,128)S(1)}, u32[]{:S(2)}, u32[]{:S(2)}) %collective-permute-start.18) | collective-permute-done | bytes 294944 | tf_op jit(solution)/shard_map/ppermute | solution.py:592
  99.8 1.7 %shard_map.110 = f32[2304,128]{1,0:T(8,128)} custom-call(s32[3]{0:T(128)S(1)} %pad_add_fusion.place, f32[2,288,128]{2,1,0:T(8,128)S(1)} %shard_map.106.refs_0_, f32[2,288,128]{2,1,0:T(8,128)S(1)} %collective-permute-done.17.refs_1_, f32[2,288,128]{2,1,0:T(8,128)S(1)} %collective-permute-done.18.refs_2_, f32[2,288,128]{2,1,0:T(8,128)S(1)} %collective-permute-done.19.refs_3_), custom_call_target="tpu_custom_call" | custom-call | bytes 7000000 | tf_op jit(solution)/shard_map/pallas_call | solution.py:594
  (24 shorter events, 0.1 us)
Async XLA Ops:
  0.0 2.2 %copy-start = (f32[16,32]{1,0:T(8,128)S(1)}, f32[16,32]{1,0:T(8,128)}, u32[]{:S(2)}) copy-start(f32[16,32]{1,0:T(8,128)} %param.13) | copy-start | bytes 6148
  0.7 3.8 %collective-permute-start = (f32[24,128]{1,0:T(8,128)S(1)}, f32[24,128]{1,0:T(8,128)S(1)}, u32[]{:S(2)}, u32[]{:S(2)}) collective-permute-start(f32[24,128]{1,0:T(8,128)S(1)} %add_convert_fusion.head_0_.own_0_), channel_id=1, source_target_pairs={{0,1},{1,0},{2,3},{3,2},{4,5},{5,4},{6,7},{7,6},{8,9},{9,8},{10,11... | collective-permute-start | bytes 36872 | tf_op jit(solution)/shard_map/ppermute | solution.py:382
  1.2 3.3 %collective-permute-start.1 = (f32[2304,128]{1,0:T(8,128)}, f32[2304,128]{1,0:T(8,128)S(1)}, u32[]{:S(2)}, u32[]{:S(2)}) collective-permute-start(f32[2304,128]{1,0:T(8,128)} %bitcast.26), channel_id=1, source_target_pairs={{0,1},{1,0},{2,3},{3,2},{4,5},{5,4},{6,7},{7,6},{8,9},{9,8},{10,11... | collective-permute-start | bytes 3538952 | tf_op jit(solution)/shard_map/ppermute | solution.py:381
  4.5 1.3 %copy-start.1 = (f32[288,8,128]{2,1,0:T(8,128)S(1)}, f32[288,8,128]{2,1,0:T(8,128)}, u32[]{:S(2)}) copy-start(f32[288,8,128]{2,1,0:T(8,128)} %param.9) | copy-start | bytes 3538948
  6.9 14.8 %collective-permute-start.2 = (f32[816,128]{1,0:T(8,128)S(1)}, f32[816,128]{1,0:T(8,128)S(1)}, u32[]{:S(2)}, u32[]{:S(2)}) collective-permute-start(f32[816,128]{1,0:T(8,128)S(1)} %shard_map.91.after_0_), channel_id=1, source_target_pairs={{0,2},{2,0},{1,3},{3,1},{4,6},{6,4},{5,7},{7,5},{8,10},{10,8},{9,1... | collective-permute-start | bytes 1253384 | tf_op jit(solution)/shard_map/ppermute | solution.py:402
  11.0 24.7 %collective-permute-start.4 = (f32[768,128]{1,0:T(8,128)S(1)}, f32[768,128]{1,0:T(8,128)S(1)}, u32[]{:S(2)}, u32[]{:S(2)}) collective-permute-start(f32[768,128]{1,0:T(8,128)S(1)} %shard_map.92.after_0_), channel_id=1, source_target_pairs={{0,2},{2,0},{1,3},{3,1},{4,6},{6,4},{5,7},{7,5},{8,10},{10,8},{9,1... | collective-permute-start | bytes 1179656 | tf_op jit(solution)/shard_map/ppermute | solution.py:402
  12.3 33.5 %collective-permute-start.3 = (f32[768,128]{1,0:T(8,128)S(1)}, f32[768,128]{1,0:T(8,128)S(1)}, u32[]{:S(2)}, u32[]{:S(2)}) collective-permute-start(f32[768,128]{1,0:T(8,128)S(1)} %shard_map.93.after), channel_id=1, source_target_pairs={{0,2},{2,0},{1,3},{3,1},{4,6},{6,4},{5,7},{7,5},{8,10},{10,8},{9,1... | collective-permute-start | bytes 1179656 | tf_op jit(solution)/shard_map/ppermute | solution.py:402
  21.7 2.2 %copy-start.2 = (f32[288,8,128]{2,1,0:T(8,128)S(1)}, f32[288,8,128]{2,1,0:T(8,128)}, u32[]{:S(2)}) copy-start(f32[288,8,128]{2,1,0:T(8,128)} %param.9) | copy-start | bytes 3538948
  30.1 11.7 %collective-permute-start.5 = (f32[2,2,48,128]{3,2,1,0:T(8,128)S(1)}, f32[2,2,48,128]{3,2,1,0:T(8,128)S(1)}, u32[]{:S(2)}, u32[]{:S(2)}) collective-permute-start(f32[2,2,48,128]{3,2,1,0:T(8,128)S(1)} %get-tuple-element.33), channel_id=1, source_target_pairs={{0,4},{4,8},{8,12},{12,0},{1,5},{5,9},{9,13},{13,1},{2,6},{6,10},{... | collective-permute-start | bytes 294920 | tf_op jit(solution)/shard_map/ppermute | solution.py:518
  31.7 10.1 %collective-permute-start.6 = (f32[2,2,48,128]{3,2,1,0:T(8,128)S(1)}, f32[2,2,48,128]{3,2,1,0:T(8,128)S(1)}, u32[]{:S(2)}, u32[]{:S(2)}) collective-permute-start(f32[2,2,48,128]{3,2,1,0:T(8,128)S(1)} %get-tuple-element.34), channel_id=1, source_target_pairs={{0,8},{4,12},{8,0},{12,4},{1,9},{5,13},{9,1},{13,5},{2,10},{6,14},... | collective-permute-start | bytes 294920 | tf_op jit(solution)/shard_map/ppermute | solution.py:518
  34.3 7.5 %collective-permute-start.7 = (f32[2,2,48,128]{3,2,1,0:T(8,128)S(1)}, f32[2,2,48,128]{3,2,1,0:T(8,128)S(1)}, u32[]{:S(2)}, u32[]{:S(2)}) collective-permute-start(f32[2,2,48,128]{3,2,1,0:T(8,128)S(1)} %get-tuple-element.35), channel_id=1, source_target_pairs={{0,12},{4,0},{8,4},{12,8},{1,13},{5,1},{9,5},{13,9},{2,14},{6,2},{... | collective-permute-start | bytes 294920 | tf_op jit(solution)/shard_map/ppermute | solution.py:518
  41.9 10.0 %collective-permute-start.9 = (f32[2,2,48,128]{3,2,1,0:T(8,128)S(1)}, f32[2,2,48,128]{3,2,1,0:T(8,128)S(1)}, u32[]{:S(2)}, u32[]{:S(2)}) collective-permute-start(f32[2,2,48,128]{3,2,1,0:T(8,128)S(1)} %get-tuple-element.39), channel_id=1, source_target_pairs={{0,4},{4,8},{8,12},{12,0},{1,5},{5,9},{9,13},{13,1},{2,6},{6,10},{... | collective-permute-start | bytes 294920 | tf_op jit(solution)/shard_map/ppermute | solution.py:518
  42.8 9.1 %collective-permute-start.10 = (f32[2,2,48,128]{3,2,1,0:T(8,128)S(1)}, f32[2,2,48,128]{3,2,1,0:T(8,128)S(1)}, u32[]{:S(2)}, u32[]{:S(2)}) collective-permute-start(f32[2,2,48,128]{3,2,1,0:T(8,128)S(1)} %get-tuple-element.40), channel_id=1, source_target_pairs={{0,8},{4,12},{8,0},{12,4},{1,9},{5,13},{9,1},{13,5},{2,10},{6,14},... | collective-permute-start | bytes 294920 | tf_op jit(solution)/shard_map/ppermute | solution.py:518
  44.5 7.5 %collective-permute-start.11 = (f32[2,2,48,128]{3,2,1,0:T(8,128)S(1)}, f32[2,2,48,128]{3,2,1,0:T(8,128)S(1)}, u32[]{:S(2)}, u32[]{:S(2)}) collective-permute-start(f32[2,2,48,128]{3,2,1,0:T(8,128)S(1)} %get-tuple-element.41), channel_id=1, source_target_pairs={{0,12},{4,0},{8,4},{12,8},{1,13},{5,1},{9,5},{13,9},{2,14},{6,2},{... | collective-permute-start | bytes 294920 | tf_op jit(solution)/shard_map/ppermute | solution.py:518
  52.0 9.9 %collective-permute-start.13 = (f32[2,2,48,128]{3,2,1,0:T(8,128)S(1)}, f32[2,2,48,128]{3,2,1,0:T(8,128)S(1)}, u32[]{:S(2)}, u32[]{:S(2)}) collective-permute-start(f32[2,2,48,128]{3,2,1,0:T(8,128)S(1)} %get-tuple-element.45), channel_id=1, source_target_pairs={{0,4},{4,8},{8,12},{12,0},{1,5},{5,9},{9,13},{13,1},{2,6},{6,10},{... | collective-permute-start | bytes 294920 | tf_op jit(solution)/shard_map/ppermute | solution.py:518
  53.6 8.3 %collective-permute-start.14 = (f32[2,2,48,128]{3,2,1,0:T(8,128)S(1)}, f32[2,2,48,128]{3,2,1,0:T(8,128)S(1)}, u32[]{:S(2)}, u32[]{:S(2)}) collective-permute-start(f32[2,2,48,128]{3,2,1,0:T(8,128)S(1)} %get-tuple-element.46), channel_id=1, source_target_pairs={{0,8},{4,12},{8,0},{12,4},{1,9},{5,13},{9,1},{13,5},{2,10},{6,14},... | collective-permute-start | bytes 294920 | tf_op jit(solution)/shard_map/ppermute | solution.py:518
  54.9 7.0 %collective-permute-start.15 = (f32[2,2,48,128]{3,2,1,0:T(8,128)S(1)}, f32[2,2,48,128]{3,2,1,0:T(8,128)S(1)}, u32[]{:S(2)}, u32[]{:S(2)}) collective-permute-start(f32[2,2,48,128]{3,2,1,0:T(8,128)S(1)} %get-tuple-element.47), channel_id=1, source_target_pairs={{0,12},{4,0},{8,4},{12,8},{1,13},{5,1},{9,5},{13,9},{2,14},{6,2},{... | collective-permute-start | bytes 294920 | tf_op jit(solution)/shard_map/ppermute | solution.py:518
  60.9 1.6 %collective-permute-start.8 = (f32[4,2,48,128]{3,2,1,0:T(8,128)S(1)}, f32[4,2,48,128]{3,2,1,0:T(8,128)S(1)}, u32[]{:S(2)}, u32[]{:S(2)}) collective-permute-start(f32[4,2,48,128]{3,2,1,0:T(8,128)S(1)} %shard_map.100), channel_id=1, source_target_pairs={{0,1},{1,0},{2,3},{3,2},{4,5},{5,4},{6,7},{7,6},{8,9},{9,8},{10,11... | collective-permute-start | bytes 589832 | tf_op jit(solution)/shard_map/ppermute | solution.py:548
  61.3 1.0 copy-start.3
  61.3 1.6 %collective-permute-start.12 = (f32[4,2,48,128]{3,2,1,0:T(8,128)S(1)}, f32[4,2,48,128]{3,2,1,0:T(8,128)S(1)}, u32[]{:S(2)}, u32[]{:S(2)}) collective-permute-start(f32[4,2,48,128]{3,2,1,0:T(8,128)S(1)} %shard_map.102), channel_id=1, source_target_pairs={{0,1},{1,0},{2,3},{3,2},{4,5},{5,4},{6,7},{7,6},{8,9},{9,8},{10,11... | collective-permute-start | bytes 589832 | tf_op jit(solution)/shard_map/ppermute | solution.py:548
  62.2 1.5 %collective-permute-start.16 = (f32[4,2,48,128]{3,2,1,0:T(8,128)S(1)}, f32[4,2,48,128]{3,2,1,0:T(8,128)S(1)}, u32[]{:S(2)}, u32[]{:S(2)}) collective-permute-start(f32[4,2,48,128]{3,2,1,0:T(8,128)S(1)} %shard_map.104), channel_id=1, source_target_pairs={{0,1},{1,0},{2,3},{3,2},{4,5},{5,4},{6,7},{7,6},{8,9},{9,8},{10,11... | collective-permute-start | bytes 589832 | tf_op jit(solution)/shard_map/ppermute | solution.py:548
  70.2 10.7 %collective-permute-start.17 = (f32[2,288,128]{2,1,0:T(8,128)S(1)}, f32[2,288,128]{2,1,0:T(8,128)S(1)}, u32[]{:S(2)}, u32[]{:S(2)}) collective-permute-start(f32[2,288,128]{2,1,0:T(8,128)S(1)} %shard_map.107), channel_id=1, source_target_pairs={{0,12},{4,0},{8,4},{12,8},{1,13},{5,1},{9,5},{13,9},{2,14},{6,2},{... | collective-permute-start | bytes 884744 | tf_op jit(solution)/shard_map/ppermute | solution.py:592
  73.4 26.4 %collective-permute-start.18 = (f32[2,288,128]{2,1,0:T(8,128)S(1)}, f32[2,288,128]{2,1,0:T(8,128)S(1)}, u32[]{:S(2)}, u32[]{:S(2)}) collective-permute-start(f32[2,288,128]{2,1,0:T(8,128)S(1)} %shard_map.108), channel_id=1, source_target_pairs={{0,8},{4,12},{8,0},{12,4},{1,9},{5,13},{9,1},{13,5},{2,10},{6,14},... | collective-permute-start | bytes 884744 | tf_op jit(solution)/shard_map/ppermute | solution.py:592
  73.8 26.0 %collective-permute-start.19 = (f32[2,288,128]{2,1,0:T(8,128)S(1)}, f32[2,288,128]{2,1,0:T(8,128)S(1)}, u32[]{:S(2)}, u32[]{:S(2)}) collective-permute-start(f32[2,288,128]{2,1,0:T(8,128)S(1)} %shard_map.109), channel_id=1, source_target_pairs={{0,4},{4,8},{8,12},{12,0},{1,5},{5,9},{9,13},{13,1},{2,6},{6,10},{... | collective-permute-start | bytes 884744 | tf_op jit(solution)/shard_map/ppermute | solution.py:592

commit v3 on v2

--- a/solution.py
+++ b/solution.py
@@ -67,17 +67,14 @@
 
 def faces_kernel(window, n_lon, place, own, received, after, out, fields):
     lat = place[0]
-    rows, lanes = own[0].shape[0] // 3, own[0].shape[1]
+    rows, lanes = window.rows, own[0].shape[1]
     for row in window.zeros(lat):
         fields[row] = jnp.zeros((3, n_lon * lanes), jnp.float32)
-    sources = [(window.own(lat), [(ref, 0) for ref in own])]
-    for offset, ref in zip(window.received(lat), received):
-        sources.append((offset, [(ref, 3 * d) for d in range(n_lon)]))
-    for offset, blocks in sources:
-        for d, (ref, lead) in enumerate(blocks):
+    for offset, blocks in [(window.own(lat), own)] + list(zip(window.received(lat), received)):
+        for d, ref in enumerate(blocks):
             for f in range(3):
                 for row in range(rows):
-                    at = (lead + f) * rows + row
+                    at = f * rows + row
                     fields[offset + row, f : f + 1, d * lanes : (d + 1) * lanes] = ref[at : at + 1, :]
     width = n_lon * lanes
     n_class = out.shape[2] // 6
@@ -101,21 +98,42 @@
             out[row, 1, copy * span : (copy + 1) * span, :] = north
         return 0
 
-    lax.fori_loop(0, window.size - 1, step, 0)
+    lax.fori_loop(0, window.size - 1, step, 0, unroll=4)
     out[window.size - 1] = jnp.zeros(out.shape[1:], jnp.bfloat16)
 
 
-def pack_kernel(start, half, rows, place, own_in, head, after, out, sems):
-    lead = sum(ref.shape[0] for ref in head)
-    length = (out.shape[0] - lead) // len(own_in)
-    first = pl.multiple_of((place[2] * half + start) * rows, 8)
+def pack_raw_kernel(half, rows, flat, sea, depth, current, out, fields_out, held, sems):
+    fields = [sea, depth, current]
+    lead = len(fields) * rows
+    parts = flat.shape[0] // (half * rows)
+    length = (out.shape[0] - lead) // parts
     copies = []
-    for d, ref in enumerate(own_in):
-        to = out.at[pl.ds(lead + d * length, length)]
-        copies.append(pltpu.make_async_copy(ref.at[pl.ds(first, length)], to, sems.at[d]))
-        copies[-1].start()
-    for i, ref in enumerate(head):
-        out[i * ref.shape[0] : (i + 1) * ref.shape[0], :] = ref[...]
+    for i in range(parts):
+        to = out.at[pl.ds(lead + i * length, length)]
+        copies.append(pltpu.make_async_copy(flat.at[pl.ds(i * half * rows, length)], to, sems.at[0, i]))
+    for i, ref in enumerate(fields):
+        copies.append(pltpu.make_async_copy(ref, held.at[i], sems.at[1, i]))
+    for copy in copies:
+        copy.start()
+    for copy in copies:
+        copy.wait()
+    for i in range(len(fields)):
+        at = slice(i * rows, (i + 1) * rows)
+        out[at, :] = held[i].astype(jnp.float32)
+        fields_out[at, :] = held[i].astype(jnp.float32)
+
+
+def pack_kernel(starts, half, rows, place, own_in, after, *refs):
+    outs, sems = refs[:-1], refs[-1]
+    copies = []
+    for i, (start, out) in enumerate(zip(starts, outs)):
+        length = out.shape[0] // len(own_in)
+        first = pl.multiple_of((place[2] * half + start) * rows, 8)
+        for d, ref in enumerate(own_in):
+            there = ref.at[pl.ds(first, length)]
+            copies.append(pltpu.make_async_copy(there, out.at[pl.ds(d * length, length)], sems.at[i, d]))
+    for copy in copies:
+        copy.start()
     for copy in copies:
         copy.wait()
 
@@ -131,6 +149,18 @@
 
 def gate_kernel(*refs):
     pass
+
+
+def gated(arrays, after):
+    return pl.pallas_call(
+        gate_kernel,
+        out_shape=[jax.ShapeDtypeStruct(a.shape, a.dtype) for a in arrays],
+        in_specs=[anywhere] * (len(arrays) + len(after)),
+        out_specs=[anywhere] * len(arrays),
+        input_output_aliases={i: i for i in range(len(arrays))},
+        compiler_params=params(),
+        cost_estimate=cost(0.1),
+    )(*arrays, *after)
 
 
 def median_zero(a, b):
@@ -187,8 +217,11 @@
             energy[row] = jnp.zeros((GROUP, width), jnp.float32)
             other[row] = jnp.zeros((GROUP, width), jnp.float32)
         sources = [(own, [(ref, 0) for ref in own_blocks])]
-        for offset, ref in zip(window.received(lat), lat_in):
-            sources.append((offset, [(ref, head + d * count) for d in range(n_lon)]))
+        for offset, blocks in zip(window.received(lat), lat_in):
+            if head:
+                sources.append((offset, [(ref, head + lon * count) for ref in blocks]))
+            else:
+                sources.append((offset, [(blocks[0], d * count) for d in range(n_lon)]))
         for offset, blocks in sources:
             for d, (ref, lead) in enumerate(blocks):
                 for row in range(rows):
@@ -241,14 +274,14 @@
     lax.fori_loop(0, count // GROUP, group, 0)
 
 
-def matrix_kernel(names, index, weight, after, out, columns):
+def matrix_kernel(home, place, names, index, weight, after, out, columns):
     height = out.shape[1]
 
     @pl.when(pl.program_id(1) == 0)
     def _():
         columns[...] = jnp.transpose(jnp.concatenate([index[0], weight[0]], axis=0))
 
-    base = pl.program_id(1) * height
+    base = pl.multiple_of(home(place, pl.program_id(1)) * height, GROUP)
 
     def step(i, _):
         at = pl.multiple_of(i * GROUP, GROUP)
@@ -260,12 +293,12 @@
         out[0, pl.ds(at, GROUP), :] = made.astype(jnp.bfloat16)
         return 0
 
-    lax.fori_loop(0, height // GROUP, step, 0, unroll=3)
-
-
-def transposed_kernel(half, half_own, index, weight, after, out):
+    lax.fori_loop(0, height // GROUP, step, 0, unroll=True)
+
+
+def transposed_kernel(home, half, half_own, place, index, weight, after, out):
     height, total = out.shape[1], out.shape[2]
-    base = pl.program_id(1) * height
+    base = home(place, pl.program_id(1)) * height
 
     def step(i, _):
         at = pl.multiple_of(i * GROUP, GROUP)
@@ -282,48 +315,43 @@
     lax.fori_loop(0, height // GROUP, step, 0, unroll=3)
 
 
-def forward_kernel(sizes, n_lon, split, place, matrix, coupling, *refs):
+def forward_kernel(sizes, n_lon, home, place, matrix, coupling, *refs):
     pieces = refs[:-4]
     energy_out, source_out, source_low_out, low = refs[-4:]
-    step = pl.program_id(0)
-    block = coupling.shape[0]
+    per_chunk = len(pieces) // len(sizes)
+    n_comp = per_chunk - n_lon + 1
+    block = coupling.shape[0] // n_comp
     half = block // n_lon
-    per_chunk = len(pieces) // len(sizes)
     share, lanes = pieces[0].shape[1], pieces[0].shape[3]
-
-    n_comp = per_chunk - n_lon + 1
-
-    @pl.when(step == 0)
-    def _():
-        for s in range(n_comp):
-            of_comp = lax.rem(place[1] + n_comp - s, n_comp) if split else s
-            for d in range(n_lon):
-                of_lon = lax.rem(place[2] + n_lon - d, n_lon)
-                first = (of_comp * n_lon + of_lon) * half
-                for i, size in enumerate(sizes):
-                    at = pl.ds(pl.multiple_of(first + sum(sizes[:i]), GROUP), size)
-                    group = pieces[i * per_chunk : (i + 1) * per_chunk]
-                    for k in range(share):
-                        part = group[s][0, k] if d == 0 else group[d - n_lon][s, k]
-                        energy_out[at, k * lanes : (k + 1) * lanes] = part
-                        low[at, k * lanes : (k + 1) * lanes] = part.astype(jnp.bfloat16)
-
-    here = pl.ds(pl.multiple_of(step * block, GROUP), block)
-    energy = energy_out[here, :]
-    plus_side = jnp.dot(matrix[0, here, :], low[...], preferred_element_type=jnp.float32)
-    minus_side = jnp.dot(matrix[1, here, :], low[...], preferred_element_type=jnp.float32)
-    source = coupling[...] * (
-        energy * energy * (plus_factor * plus_side + minus_factor * minus_side)
-        - cross_factor * energy * plus_side * minus_side
-    )
-    source_out[...] = source
-    source_low_out[...] = source.astype(jnp.bfloat16)
-
-
-def backward_kernel(s, n_comp, split, place, matrix_t, source_low, energy, source, out):
+    for s in range(n_comp):
+        for d in range(n_lon):
+            first = lax.rem(place[2] + n_lon - d, n_lon) * half
+            for i, size in enumerate(sizes):
+                group = pieces[i * per_chunk : (i + 1) * per_chunk]
+                to = first + sum(sizes[:i])
+                here = pl.ds(pl.multiple_of(s * block + to, GROUP), size)
+                there = pl.ds(pl.multiple_of(home(place, s) * block + to, GROUP), size)
+                for k in range(share):
+                    part = group[s][0, k] if d == 0 else group[d - n_lon][s, k]
+                    energy_out[here, k * lanes : (k + 1) * lanes] = part
+                    low[there, k * lanes : (k + 1) * lanes] = part.astype(jnp.bfloat16)
+    for s in range(n_comp):
+        here = slice(s * block, (s + 1) * block)
+        there = pl.ds(pl.multiple_of(home(place, s) * block, GROUP), block)
+        energy = energy_out[here, :]
+        plus_side = jnp.dot(matrix[0, here, :], low[...], preferred_element_type=jnp.float32)
+        minus_side = jnp.dot(matrix[1, here, :], low[...], preferred_element_type=jnp.float32)
+        source = coupling[there, :] * (
+            energy * energy * (plus_factor * plus_side + minus_factor * minus_side)
+            - cross_factor * energy * plus_side * minus_side
+        )
+        source_out[here, :] = source
+        source_low_out[there, :] = source.astype(jnp.bfloat16)
+
+
+def backward_kernel(s, matrix_t, source_low, energy, source, out):
     block, lanes = out.shape[1], out.shape[2]
-    home = lax.rem(place[1] + n_comp - s, n_comp) if split else s
-    here = pl.ds(pl.multiple_of(home * block, GROUP), block)
+    here = slice(s * block, (s + 1) * block)
     gain = (
         jnp.dot(matrix_t[0, here, :], source_low[...], preferred_element_type=jnp.float32)
         + jnp.dot(matrix_t[1, here, :], source_low[...], preferred_element_type=jnp.float32)
@@ -374,32 +402,47 @@
     else:
         flat = spectrum.reshape(n_lon, half_own, rows, lanes)
         flat = jnp.pad(flat, ((0, 0), (0, half - half_own), (0, 0), (0, 0))).reshape(-1, lanes)
-    fields = jnp.concatenate([sea_mask, depth_class, current_class]).astype(jnp.float32)
-    own_in, own_fields = [flat], [fields]
-    for d in range(n_lon - 1, 0, -1):
-        pairs = [(i, (i + d) % n_lon) for i in range(n_lon)]
-        own_in.append(lax.ppermute(flat, "lon", pairs))
-        own_fields.append(lax.ppermute(fields, "lon", pairs))
     if window.pair:
         moves = [[(0, 1), (1, 0)]]
     else:
         moves = [[(i, i + 1) for i in range(n_lat - 1)], [(i + 1, i) for i in range(n_lat - 1)]]
-    lat_in, packed = [], []
-    for i, (start, size) in enumerate(zip(starts, sizes)):
-        head = own_fields if i == 0 else []
-        length = n_lon * (size + (0 if i else 3)) * rows
-        packed.append(
-            pl.pallas_call(
-                functools.partial(pack_kernel, start, half, rows),
-                out_shape=jax.ShapeDtypeStruct((length, lanes), jnp.float32),
-                in_specs=[scalars, [anywhere] * n_lon, [whole] * len(head), [anywhere] * (i > 0)],
-                out_specs=whole,
-                scratch_shapes=[pltpu.SemaphoreType.DMA((n_lon,))],
-                compiler_params=params(),
-                cost_estimate=cost(1),
-            )(place, own_in, head, packed[-1:])
-        )
-        lat_in.append([lax.ppermute(packed[i], "lat", move) for move in moves])
+    lengths = [n_lon * size * rows for size in sizes]
+
+
+    def on_all_columns(block):
+        found = [block]
+        for d in range(n_lon - 1, 0, -1):
+            found.append(lax.ppermute(block, "lon", [(i, (i + d) % n_lon) for i in range(n_lon)]))
+        return found
+
+    first_block, fields = pl.pallas_call(
+        functools.partial(pack_raw_kernel, half, rows),
+        out_shape=(
+            jax.ShapeDtypeStruct((lengths[0] + 3 * rows, lanes), jnp.float32),
+            jax.ShapeDtypeStruct((3 * rows, lanes), jnp.float32),
+        ),
+        in_specs=[anywhere] * 4,
+        out_specs=(whole, whole),
+        scratch_shapes=[pltpu.VMEM((3, rows, lanes), jnp.int32), pltpu.SemaphoreType.DMA((2, max(n_lon, 3)))],
+        compiler_params=params(),
+        cost_estimate=cost(1),
+    )(*[pltpu.with_memory_space_constraint(a, pltpu.HBM) for a in (flat, sea_mask, depth_class, current_class)])
+    own_in, own_fields = on_all_columns(flat), on_all_columns(fields)
+    blocks = [first_block]
+    if len(sizes) > 1:
+        blocks += pl.pallas_call(
+            functools.partial(pack_kernel, starts[1:], half, rows),
+            out_shape=[jax.ShapeDtypeStruct((length, lanes), jnp.float32) for length in lengths[1:]],
+            in_specs=[scalars, [anywhere] * n_lon, [anywhere] * (n_lon + 1)],
+            out_specs=[whole] * len(lengths[1:]),
+            scratch_shapes=[pltpu.SemaphoreType.DMA((len(lengths) - 1, n_lon))],
+            compiler_params=params(),
+            cost_estimate=cost(1.5),
+        )(place, own_in, [first_block] + own_fields)
+    lat_in = [[lax.ppermute(block, "lat", move) for move in moves] for block in blocks]
+
+    def home_of(place, s):
+        return lax.rem(place[1] + n_comp - s, n_comp) if split else s
 
     total = n_comp * n_lon * half
     block = n_lon * half
@@ -418,18 +461,21 @@
     by_cols = pl.BlockSpec((1, 4, total), lambda s, i: (s, 0, 0))
     by_block = pl.BlockSpec((1, block, total), lambda s, i: (s, i, 0))
     matrix = pl.pallas_call(
-        matrix_kernel,
+        functools.partial(matrix_kernel, home_of),
         grid=(2, n_comp),
         out_shape=pltpu.VMEM((2, total, total), jnp.bfloat16),
-        in_specs=[whole, by_cols, by_cols, anywhere],
+        in_specs=[scalars, whole, by_cols, by_cols, anywhere],
         out_specs=by_block,
         scratch_shapes=[pltpu.VMEM((total, 8), jnp.float32)],
         compiler_params=params(),
         cost_estimate=cost(6),
-    )(names, index, weight, packed[-1])
+    )(place, names, index, weight, blocks[-1])
+
+    lat_in[0] = [on_all_columns(block) for block in gated(lat_in[0], [matrix])]
+    lat_in[1:] = [[[block] for block in found] for found in lat_in[1:]]
 
     n_class = speed_table.shape[0]
-    head_block = pl.BlockSpec((3 * n_lon * rows, lanes), lambda i: (0, 0))
+    head_block = pl.BlockSpec((3 * rows, lanes), lambda i: (0, 0))
     faces, window_fields = pl.pallas_call(
         functools.partial(faces_kernel, window, n_lon),
         grid=(1,),
@@ -437,7 +483,7 @@
             jax.ShapeDtypeStruct((window.size, 2, 6 * n_class, width), jnp.bfloat16),
             jax.ShapeDtypeStruct((window.size, 3, width), jnp.float32),
         ),
-        in_specs=[scalars, [whole] * n_lon, [head_block] * len(moves), anywhere],
+        in_specs=[scalars, [whole] * n_lon, [[head_block] * n_lon] * len(moves), anywhere],
         out_specs=(whole, whole),
         compiler_params=params(),
         cost_estimate=cost(2),
@@ -475,7 +521,7 @@
             shapes = [jax.ShapeDtypeStruct((rows, n_lon, size, lanes), jnp.float32)]
         pieces = pl.pallas_call(
             functools.partial(
-                propagate_kernel, window, n_lon, n_comp, split, start, half, 0 if i else 3 * n_lon
+                propagate_kernel, window, n_lon, n_comp, split, start, half, 0 if i else 3
             ),
             out_shape=shapes,
             in_specs=[
@@ -484,7 +530,7 @@
                 whole,
                 whole,
                 [anywhere] * n_lon,
-                [whole] * len(moves),
+                [[whole] * len(found) for found in lat_in[i]],
                 anywhere,
             ],
             out_specs=[whole] * len(shapes),
@@ -503,15 +549,7 @@
         if split:
             sent = pieces[1:]
             if i > 0:
-                sent = pl.pallas_call(
-                    gate_kernel,
-                    out_shape=shapes[1:],
-                    in_specs=[anywhere] * (2 * len(sent)),
-                    out_specs=[anywhere] * len(sent),
-                    input_output_aliases={j: j for j in range(len(sent))},
-                    compiler_params=params(),
-                    cost_estimate=cost(0.1),
-                )(*sent, *moved[1:])
+                sent = gated(sent, moved[1 : n_comp - 1])
             moved = [pieces[0]]
             for r in range(1, n_comp):
                 pairs = [(a, (a + r) % n_comp) for a in range(n_comp)]
@@ -524,14 +562,14 @@
         after = []
         if i == len(sizes) - 1:
             matrix_t = pl.pallas_call(
-                functools.partial(transposed_kernel, half, half_own),
+                functools.partial(transposed_kernel, home_of, half, half_own),
                 grid=(2, n_comp),
                 out_shape=pltpu.VMEM((2, total, total), jnp.bfloat16),
-                in_specs=[by_cols, by_cols, anywhere],
+                in_specs=[scalars, by_cols, by_cols, anywhere],
                 out_specs=by_block,
                 compiler_params=params(),
                 cost_estimate=cost(4),
-            )(index, weight, pieces[0])
+            )(place, index, weight, pieces[0])
             after = [matrix_t]
         crossed = []
         for d in range(1, n_lon):
@@ -550,24 +588,14 @@
 
     cells = share * span
     energy, source, source_low = pl.pallas_call(
-        functools.partial(forward_kernel, sizes, n_lon, split),
-        grid=(n_comp,),
+        functools.partial(forward_kernel, sizes, n_lon, home_of),
         out_shape=(
             jax.ShapeDtypeStruct((total, cells), jnp.float32),
             jax.ShapeDtypeStruct((total, cells), jnp.float32),
             jax.ShapeDtypeStruct((total, cells), jnp.bfloat16),
         ),
-        in_specs=[
-            scalars,
-            whole,
-            pl.BlockSpec((block, 1), lambda s: (s, 0)),
-        ]
-        + [whole] * len(arrived),
-        out_specs=(
-            pl.BlockSpec((total, cells), lambda s: (0, 0)),
-            pl.BlockSpec((block, cells), lambda s: (s, 0)),
-            pl.BlockSpec((block, cells), lambda s: (s, 0)),
-        ),
+        in_specs=[scalars, whole, whole] + [whole] * len(arrived),
+        out_specs=(whole, whole, whole),
         scratch_shapes=[pltpu.VMEM((total, cells), jnp.bfloat16)],
         compiler_params=params(),
         cost_estimate=cost(4),
@@ -577,13 +605,13 @@
     for s in range(n_comp):
         back.append(
             pl.pallas_call(
-                functools.partial(backward_kernel, s, n_comp, split),
+                functools.partial(backward_kernel, s),
                 out_shape=jax.ShapeDtypeStruct((share, block, span), jnp.float32),
-                in_specs=[scalars] + [whole] * 4,
+                in_specs=[whole] * 4,
                 out_specs=whole,
                 compiler_params=params(),
                 cost_estimate=cost(0.6),
-            )(place, matrix_t, source_low, energy, source)
+            )(matrix_t, source_low, energy, source)
         )
 
     if split:

time: 102 us -> 94.2 us (0.924)
  Pallas kernels: 45 us -> 39.3 us
  waiting for transfers between devices: 25.9 us -> 29.2 us
  other arithmetic: 2.8 us -> 0.54 us
  local copies, waits for them, and re-layouts: 2.61 us -> 0.6 us
    pallas_call x12, Pallas kernels: 21.7 us -> 17 us  [the longest x1 5.3 us: local(): pl.pallas_call(functools.partial(matrix_kernel, home_of), grid=(2, n_comp...]
    ppermute x5 -> x6, waiting for transfers between devices: 0.01 us -> 1.67 us  [the longest x3 1.66 us: local(): lax.ppermute(block, 'lat', move)]
    ppermute x9, waiting for transfers between devices: 0.08 us -> 1.44 us  [local(): moved.append(lax.ppermute(sent[r - 1], 'comp', pairs))]
    unnamed x8 -> x12, local copies, waits for them, and re-layouts: 1.28 us -> 0.03 us
    ppermute x9, starting transfers between devices: 14.5 us -> 13.3 us  [local(): moved.append(lax.ppermute(sent[r - 1], 'comp', pairs))]
    ppermute x5 -> x6, starting transfers between devices: 5.67 us -> 5.75 us  [the longest x3 5.02 us: local(): lax.ppermute(block, 'lat', move)]
  transfers between devices with their start and end apart: 20 -> 21, of which waited for: 5 -> 7; matrix products, arithmetic and copies ran while one was open for 4% -> 1% of each run, Pallas kernels for 35% -> 35%
where the time goes in v3:
time: 94.2 us; the launch traced here: 94.1 us
  Pallas kernels  39.3 us (42%)
  waiting for transfers between devices  29.2 us (31%)
  starting transfers between devices  24 us (25%)
    ppermute x3, waiting for transfers between devices, local(): lax.ppermute(back[r], 'comp', [(a, (a - r) % n_comp) for a in range(n_com...  24.9 us
    pallas_call x3, Pallas kernels, local(): pl.pallas_call(functools.partial(propagate_kernel, window, n_lon, n_comp,...  18.4 us
    ppermute x9, starting transfers between devices, local(): moved.append(lax.ppermute(sent[r - 1], 'comp', pairs))  13.3 us
    pallas_call x1, Pallas kernels, local(): pl.pallas_call(functools.partial(matrix_kernel, home_of), grid=(2, n_comp...  5.3 us
    ppermute x3, starting transfers between devices, local(): lax.ppermute(block, 'lat', move)  5.02 us
    ppermute x3, starting transfers between devices, local(): lax.ppermute(back[r], 'comp', [(a, (a - r) % n_comp) for a in range(n_com...  4.27 us
    pallas_call x1, Pallas kernels, local(): pl.pallas_call(functools.partial(transposed_kernel, home_of, half, half_o...  4.17 us
    pallas_call x1, Pallas kernels, local(): pl.pallas_call(functools.partial(forward_kernel, sizes, n_lon, home_of),...  2.55 us
  transfers between devices with their start and end apart: 21, of which 7 were waited for; matrix products, arithmetic and copies ran while one was open for 1% of the time, Pallas kernels for 35%

profile of v3, /device:TPU:0, one launch (start us, length us, event | category | flops | bytes accessed | tf_op | source)
XLA Modules:
  0.0 94.1 jit_solution(1751255502396241696)
XLA Ops:
  0.0 0.5 collective-permute-start.2
  0.5 1.1 %shard_map.91 = (f32[792,128]{1,0:T(8,128)S(1)}, f32[24,128]{1,0:T(8,128)S(1)}) custom-call(f32[2304,128]{1,0:T(8,128)} %bitcast.27, s32[8,128]{1,0:T(8,128)} %sea.1, s32[8,128]{1,0:T(8,128)} %depth.1, s32[8,128]{1,0:T(8,128)} %current.1), custom_call_target="tpu_custom_call" | custom-call | bytes 3500000 | tf_op jit(solution)/shard_map/pallas_call | solution.py:418
  1.6 0.2 collective-permute-start
  1.8 2.9 %collective-permute-start.1 = (f32[792,128]{1,0:T(8,128)S(1)}, f32[792,128]{1,0:T(8,128)S(1)}, u32[]{:S(2)}, u32[]{:S(2)}) collective-permute-start(f32[792,128]{1,0:T(8,128)S(1)} %get-tuple-element.33.after_0_), channel_id=1, source_target_pairs={{0,2},{2,0},{1,3},{3,1},{4,6},{6,4},{5,7},{7,5},{8,10},{10,8},{9,1... | collective-permute-start | bytes 1216520 | tf_op jit(solution)/shard_map/ppermute | solution.py:442
  4.7 0.1 fusion.16
  4.8 0.1 pad.9.clone
  4.9 0.1 pad.7.clone
  5.0 0.2 broadcast_multiply_fusion.1
  5.2 0.1 pad_maximum_fusion
  5.3 0.1 pad_maximum_fusion.1
  5.4 0.1 copy.24
  5.5 0.1 pad_add_fusion.place
  5.6 0.1 copy.22
  5.7 0.0 collective-permute-done.after_2_.own_1_
  5.7 0.0 collective-permute-done.2.own_in_1_
  5.7 1.6 %shard_map.92 = (f32[768,128]{1,0:T(8,128)S(1)}, f32[768,128]{1,0:T(8,128)S(1)}) custom-call(s32[3]{0:T(128)S(1)} %pad_add_fusion.place, f32[2304,128]{1,0:T(8,128)S(1)} %bitcast.28, f32[2304,128]{1,0:T(8,128)S(1)} %collective-permute-done.2.own_in_1_, f32[792,128]{1,0:T(8,128)S(1)} %get-tuple-element.33.after_0_, ...), custom_call_target="tpu_custom_call" | custom-call | bytes 5250000 | tf_op jit(solution)/shard_map/pallas_call | solution.py:433
  7.4 5.3 %shard_map.93.refs_1_.after.matrix = bf16[2,1152,1152]{2,1,0:T(8,128)(2,1)S(1)} custom-call(s32[3]{0:T(128)S(1)} %pad_add_fusion.place, f32[1,1152]{1,0:T(1,128)S(1)} %iota.18.names, f32[2,4,1152]{2,1,0:T(4,128)S(1)} %convert_bitcast_fusion.index, f32[2,4,1152]{2,1,0:T(4,128)S(1)} %maximum_bitcast_fusion.weight, f32[768,128]{1,0:T(8,128)S(1)} %get-tuple-element.34.after), custom_call_target="tpu_custom_call" | custom-call | bytes 21000000 | tf_op jit(solution)/shard_map/pallas_call | solution.py:463
  12.7 1.7 %collective-permute-done.1.refs_0_ = f32[792,128]{1,0:T(8,128)S(1)} collective-permute-done((f32[792,128]{1,0:T(8,128)S(1)}, f32[792,128]{1,0:T(8,128)S(1)}, u32[]{:S(2)}, u32[]{:S(2)}) %collective-permute-start.1) | collective-permute-done | bytes 405536 | tf_op jit(solution)/shard_map/ppermute | solution.py:442
  14.4 1.8 %collective-permute-start.5 = (f32[768,128]{1,0:T(8,128)S(1)}, f32[768,128]{1,0:T(8,128)S(1)}, u32[]{:S(2)}, u32[]{:S(2)}) collective-permute-start(f32[768,128]{1,0:T(8,128)S(1)} %get-tuple-element.37), channel_id=1, source_target_pairs={{0,2},{2,0},{1,3},{3,1},{4,6},{6,4},{5,7},{7,5},{8,10},{10,8},{9,1... | collective-permute-start | bytes 1179656 | tf_op jit(solution)/shard_map/ppermute | solution.py:442
  16.2 0.1 maximum_maximum_fusion
  16.3 0.3 collective-permute-start.4
  16.7 1.2 %shard_map.95 = (bf16[20,2,96,256]{3,2,1,0:T(8,128)(2,1)S(1)}, f32[20,3,256]{2,1,0:T(4,128)S(1)}) custom-call(s32[3]{0:T(128)S(1)} %pad_add_fusion.place, f32[24,128]{1,0:T(8,128)S(1)} %get-tuple-element.32.after_1_.own_0_, f32[24,128]{1,0:T(8,128)S(1)} %collective-permute-done.after_2_.own_1_, f32[792,128]{1,0:T(8,128)S(1)} %shard_map.94.received_0__0_.lat_in_0__0_, ...), custom_call_target="tpu_custom_call" | custom-call | bytes 7000000 | tf_op jit(solution)/shard_map/pallas_call | solution.py:479
  17.9 6.1 %shard_map.96 = (f32[2,2,48,128]{3,2,1,0:T(8,128)S(1)}, f32[2,2,48,128]{3,2,1,0:T(8,128)S(1)}, f32[2,2,48,128]{3,2,1,0:T(8,128)S(1)}, f32[2,2,48,128]{3,2,1,0:T(8,128)S(1)}) custom-call(s32[3]{0:T(128)S(1)} %pad_add_fusion.place, bf16[2,48,96]{2,1,0:T(8,128)(2,1)S(1)} %get-tuple-element.59.tables, bf16[20,2,96,256]{3,2,1,0:T(8,128)(2,1)S(1)} %get-tuple-element.35.faces, ...), custom_call_target="tpu_custom_call" | custom-call | bytes 23730000 | tf_op jit(solution)/shard_map/pallas_call | solution.py:522
  24.1 1.9 %collective-permute-start.6 = (f32[2,2,48,128]{3,2,1,0:T(8,128)S(1)}, f32[2,2,48,128]{3,2,1,0:T(8,128)S(1)}, u32[]{:S(2)}, u32[]{:S(2)}) collective-permute-start(f32[2,2,48,128]{3,2,1,0:T(8,128)S(1)} %get-tuple-element.41), channel_id=1, source_target_pairs={{0,4},{4,8},{8,12},{12,0},{1,5},{5,9},{9,13},{13,1},{2,6},{6,10},{... | collective-permute-start | bytes 294920 | tf_op jit(solution)/shard_map/ppermute | solution.py:556
  25.9 2.6 %collective-permute-start.7 = (f32[2,2,48,128]{3,2,1,0:T(8,128)S(1)}, f32[2,2,48,128]{3,2,1,0:T(8,128)S(1)}, u32[]{:S(2)}, u32[]{:S(2)}) collective-permute-start(f32[2,2,48,128]{3,2,1,0:T(8,128)S(1)} %get-tuple-element.42), channel_id=1, source_target_pairs={{0,8},{4,12},{8,0},{12,4},{1,9},{5,13},{9,1},{13,5},{2,10},{6,14},... | collective-permute-start | bytes 294920 | tf_op jit(solution)/shard_map/ppermute | solution.py:556
  28.6 6.1 %shard_map.97 = (f32[2,2,48,128]{3,2,1,0:T(8,128)S(1)}, f32[2,2,48,128]{3,2,1,0:T(8,128)S(1)}, f32[2,2,48,128]{3,2,1,0:T(8,128)S(1)}, f32[2,2,48,128]{3,2,1,0:T(8,128)S(1)}) custom-call(s32[3]{0:T(128)S(1)} %pad_add_fusion.place, bf16[2,48,96]{2,1,0:T(8,128)(2,1)S(1)} %get-tuple-element.60.tables, bf16[20,2,96,256]{3,2,1,0:T(8,128)(2,1)S(1)} %get-tuple-element.35.faces, ...), custom_call_target="tpu_custom_call" | custom-call | bytes 23730000 | tf_op jit(solution)/shard_map/pallas_call | solution.py:522
  34.7 0.0 collective-permute-done.6.pieces_1_.refs_3_.refs_1_
  34.7 0.4 collective-permute-done.7.pieces_2_.refs_4_.refs_2_
  35.1 0.0 collective-permute-start.10
  35.1 2.2 %collective-permute-start.11 = (f32[2,2,48,128]{3,2,1,0:T(8,128)S(1)}, f32[2,2,48,128]{3,2,1,0:T(8,128)S(1)}, u32[]{:S(2)}, u32[]{:S(2)}) collective-permute-start(f32[2,2,48,128]{3,2,1,0:T(8,128)S(1)} %get-tuple-element.48), channel_id=1, source_target_pairs={{0,8},{4,12},{8,0},{12,4},{1,9},{5,13},{9,1},{13,5},{2,10},{6,14},... | collective-permute-start | bytes 294920 | tf_op jit(solution)/shard_map/ppermute | solution.py:556
  37.3 1.6 %collective-permute-start.8 = (f32[2,2,48,128]{3,2,1,0:T(8,128)S(1)}, f32[2,2,48,128]{3,2,1,0:T(8,128)S(1)}, u32[]{:S(2)}, u32[]{:S(2)}) collective-permute-start(f32[2,2,48,128]{3,2,1,0:T(8,128)S(1)} %get-tuple-element.43), channel_id=1, source_target_pairs={{0,12},{4,0},{8,4},{12,8},{1,13},{5,1},{9,5},{13,9},{2,14},{6,2},{... | collective-permute-start | bytes 294920 | tf_op jit(solution)/shard_map/ppermute | solution.py:556
  38.9 6.1 %shard_map.98 = (f32[2,2,48,128]{3,2,1,0:T(8,128)S(1)}, f32[2,2,48,128]{3,2,1,0:T(8,128)S(1)}, f32[2,2,48,128]{3,2,1,0:T(8,128)S(1)}, f32[2,2,48,128]{3,2,1,0:T(8,128)S(1)}) custom-call(s32[3]{0:T(128)S(1)} %pad_add_fusion.place, bf16[2,48,96]{2,1,0:T(8,128)(2,1)S(1)} %get-tuple-element.61.tables, bf16[20,2,96,256]{3,2,1,0:T(8,128)(2,1)S(1)} %get-tuple-element.35.faces, ...), custom_call_target="tpu_custom_call" | custom-call | bytes 23730000 | tf_op jit(solution)/shard_map/pallas_call | solution.py:522
  45.1 0.6 collective-permute-start.12
  45.7 0.0 collective-permute-done.10.pieces_1_.refs_3_.refs_6_
  45.7 0.1 collective-permute-done.11.pieces_2_.refs_4_.refs_7_
  45.9 1.3 %collective-permute-start.14 = (f32[2,2,48,128]{3,2,1,0:T(8,128)S(1)}, f32[2,2,48,128]{3,2,1,0:T(8,128)S(1)}, u32[]{:S(2)}, u32[]{:S(2)}) collective-permute-start(f32[2,2,48,128]{3,2,1,0:T(8,128)S(1)} %get-tuple-element.53), channel_id=1, source_target_pairs={{0,4},{4,8},{8,12},{12,0},{1,5},{5,9},{9,13},{13,1},{2,6},{6,10},{... | collective-permute-start | bytes 294920 | tf_op jit(solution)/shard_map/ppermute | solution.py:556
  47.2 2.0 %collective-permute-start.15 = (f32[2,2,48,128]{3,2,1,0:T(8,128)S(1)}, f32[2,2,48,128]{3,2,1,0:T(8,128)S(1)}, u32[]{:S(2)}, u32[]{:S(2)}) collective-permute-start(f32[2,2,48,128]{3,2,1,0:T(8,128)S(1)} %get-tuple-element.54), channel_id=1, source_target_pairs={{0,8},{4,12},{8,0},{12,4},{1,9},{5,13},{9,1},{13,5},{2,10},{6,14},... | collective-permute-start | bytes 294920 | tf_op jit(solution)/shard_map/ppermute | solution.py:556
  49.2 1.0 %collective-permute-start.16 = (f32[2,2,48,128]{3,2,1,0:T(8,128)S(1)}, f32[2,2,48,128]{3,2,1,0:T(8,128)S(1)}, u32[]{:S(2)}, u32[]{:S(2)}) collective-permute-start(f32[2,2,48,128]{3,2,1,0:T(8,128)S(1)} %get-tuple-element.55), channel_id=1, source_target_pairs={{0,12},{4,0},{8,4},{12,8},{1,13},{5,1},{9,5},{13,9},{2,14},{6,2},{... | collective-permute-start | bytes 294920 | tf_op jit(solution)/shard_map/ppermute | solution.py:556
  50.2 4.2 %shard_map.99.after_0_.matrix_t = bf16[2,1152,1152]{2,1,0:T(8,128)(2,1)S(1)} custom-call(s32[3]{0:T(128)S(1)} %pad_add_fusion.place, f32[2,4,1152]{2,1,0:T(4,128)S(1)} %convert_bitcast_fusion.index, f32[2,4,1152]{2,1,0:T(4,128)S(1)} %maximum_bitcast_fusion.weight, f32[2,2,48,128]{3,2,1,0:T(8,128)S(1)} %get-tuple-element.40.after.pieces_0_.refs_10_), custom_call_target="tpu_custom_call" | custom-call | bytes 14000000 | tf_op jit(solution)/shard_map/pallas_call | solution.py:564
  54.4 0.0 collective-permute-done.8.pieces_3_.refs_3_
  54.4 0.3 shard_map.100
  54.7 0.1 collective-permute-start.9
  54.8 0.0 collective-permute-done.12.pieces_3_.refs_8_
  54.8 0.3 shard_map.102
  55.1 0.0 copy-start.4
  55.1 0.5 collective-permute-start.13
  55.6 0.0 collective-permute-done.14.pieces_1_.refs_11_
  55.6 0.9 collective-permute-done.15.pieces_2_.refs_12_
  56.5 0.3 shard_map.104
  56.8 0.1 collective-permute-start.17
  56.9 0.2 reshape_broadcast_in_dim.4.coupling
  57.1 0.0 collective-permute-done.9.refs_4_
  57.1 1.2 %collective-permute-done.17.refs_14_ = f32[4,2,48,128]{3,2,1,0:T(8,128)S(1)} collective-permute-done((f32[4,2,48,128]{3,2,1,0:T(8,128)S(1)}, f32[4,2,48,128]{3,2,1,0:T(8,128)S(1)}, u32[]{:S(2)}, u32[]{:S(2)}) %collective-permute-start.17) | collective-permute-done | bytes 196640 | tf_op jit(solution)/shard_map/ppermute | solution.py:586
  58.3 2.5 %shard_map.105 = (f32[1152,256]{1,0:T(8,128)S(1)}, f32[1152,256]{1,0:T(8,128)S(1)}, bf16[1152,256]{1,0:T(8,128)(2,1)S(1)}) custom-call(s32[3]{0:T(128)S(1)} %pad_add_fusion.place, bf16[2,1152,1152]{2,1,0:T(8,128)(2,1)S(1)} %shard_map.93.refs_1_.after.matrix, f32[1152,1]{1,0:T(8,128)S(1)} %reshape_broadcast_in_dim.4.coupling, ...), custom_call_target="tpu_custom_call" | custom-call | bytes 14000000 | tf_op jit(solution)/shard_map/pallas_call | solution.py:590
  60.9 0.6 shard_map.109
  61.4 0.6 shard_map.108
  62.0 0.6 shard_map.107
  62.6 3.6 %collective-permute-start.18 = (f32[2,288,128]{2,1,0:T(8,128)S(1)}, f32[2,288,128]{2,1,0:T(8,128)S(1)}, u32[]{:S(2)}, u32[]{:S(2)}) collective-permute-start(f32[2,288,128]{2,1,0:T(8,128)S(1)} %shard_map.107), channel_id=1, source_target_pairs={{0,12},{4,0},{8,4},{12,8},{1,13},{5,1},{9,5},{13,9},{2,14},{6,2},{... | collective-permute-start | bytes 884744 | tf_op jit(solution)/shard_map/ppermute | solution.py:620
  66.2 0.1 collective-permute-start.19
  66.3 0.5 collective-permute-start.20
  66.9 0.6 shard_map.106.refs_0_
  67.4 6.2 %collective-permute-done.18.refs_1_ = f32[2,288,128]{2,1,0:T(8,128)S(1)} collective-permute-done((f32[2,288,128]{2,1,0:T(8,128)S(1)}, f32[2,288,128]{2,1,0:T(8,128)S(1)}, u32[]{:S(2)}, u32[]{:S(2)}) %collective-permute-start.18) | collective-permute-done | bytes 294944 | tf_op jit(solution)/shard_map/ppermute | solution.py:620
  73.7 18.6 %collective-permute-done.19.refs_2_ = f32[2,288,128]{2,1,0:T(8,128)S(1)} collective-permute-done((f32[2,288,128]{2,1,0:T(8,128)S(1)}, f32[2,288,128]{2,1,0:T(8,128)S(1)}, u32[]{:S(2)}, u32[]{:S(2)}) %collective-permute-start.19) | collective-permute-done | bytes 294944 | tf_op jit(solution)/shard_map/ppermute | solution.py:620
  92.3 1.8 %shard_map.110 = f32[2304,128]{1,0:T(8,128)} custom-call(s32[3]{0:T(128)S(1)} %pad_add_fusion.place, f32[2,288,128]{2,1,0:T(8,128)S(1)} %shard_map.106.refs_0_, f32[2,288,128]{2,1,0:T(8,128)S(1)} %collective-permute-done.18.refs_1_, f32[2,288,128]{2,1,0:T(8,128)S(1)} %collective-permute-done.19.refs_2_, f32[2,288,128]{2,1,0:T(8,128)S(1)} %collective-permute-done.20.refs_3_), custom_call_target="tpu_custom_call" | custom-call | bytes 7000000 | tf_op jit(solution)/shard_map/pallas_call | solution.py:622
  (29 shorter events, 0.1 us)
Async XLA Ops:
  0.0 5.0 %copy-start = (f32[16,32]{1,0:T(8,128)S(1)}, f32[16,32]{1,0:T(8,128)}, u32[]{:S(2)}) copy-start(f32[16,32]{1,0:T(8,128)} %param.13) | copy-start | bytes 6148
  0.0 5.7 %copy-start.1 = (f32[288,8,128]{2,1,0:T(8,128)S(1)}, f32[288,8,128]{2,1,0:T(8,128)}, u32[]{:S(2)}) copy-start(f32[288,8,128]{2,1,0:T(8,128)} %param.9) | copy-start | bytes 3538948
  0.0 4.8 %copy-start.5 = (f32[16,2]{0,1:T(2,128)S(1)}, f32[16,2]{0,1:T(2,128)}, u32[]{:S(2)}) copy-start(f32[16,2]{0,1:T(2,128)} %param.14) | copy-start | bytes 388
  0.0 4.9 %copy-start.2 = (s32[2,1152,4]{1,2,0:T(4,128)S(1)}, s32[2,1152,4]{1,2,0:T(4,128)}, u32[]{:S(2)}) copy-start(s32[2,1152,4]{1,2,0:T(4,128)} %param.16) | copy-start | bytes 110596
  0.0 5.3 %copy-start.3 = (f32[2,1152,4]{1,2,0:T(4,128)S(1)}, f32[2,1152,4]{1,2,0:T(4,128)}, u32[]{:S(2)}) copy-start(f32[2,1152,4]{1,2,0:T(4,128)} %param.17) | copy-start | bytes 110596
  0.0 5.7 %collective-permute-start.2 = (f32[2304,128]{1,0:T(8,128)}, f32[2304,128]{1,0:T(8,128)S(1)}, u32[]{:S(2)}, u32[]{:S(2)}) collective-permute-start(f32[2304,128]{1,0:T(8,128)} %bitcast.26), channel_id=1, source_target_pairs={{0,1},{1,0},{2,3},{3,2},{4,5},{5,4},{6,7},{7,6},{8,9},{9,8},{10,11... | collective-permute-start | bytes 3538952 | tf_op jit(solution)/shard_map/ppermute | solution.py:415
  1.6 4.1 %collective-permute-start = (f32[24,128]{1,0:T(8,128)S(1)}, f32[24,128]{1,0:T(8,128)S(1)}, u32[]{:S(2)}, u32[]{:S(2)}) collective-permute-start(f32[24,128]{1,0:T(8,128)S(1)} %get-tuple-element.32.after_1_.own_0_), channel_id=1, source_target_pairs={{0,1},{1,0},{2,3},{3,2},{4,5},{5,4},{6,7},{7,6},{8,9},{9,8},{10,11... | collective-permute-start | bytes 36872 | tf_op jit(solution)/shard_map/ppermute | solution.py:415
  1.8 12.5 %collective-permute-start.1 = (f32[792,128]{1,0:T(8,128)S(1)}, f32[792,128]{1,0:T(8,128)S(1)}, u32[]{:S(2)}, u32[]{:S(2)}) collective-permute-start(f32[792,128]{1,0:T(8,128)S(1)} %get-tuple-element.33.after_0_), channel_id=1, source_target_pairs={{0,2},{2,0},{1,3},{3,1},{4,6},{6,4},{5,7},{7,5},{8,10},{10,8},{9,1... | collective-permute-start | bytes 1216520 | tf_op jit(solution)/shard_map/ppermute | solution.py:442
  14.3 2.3 %collective-permute-start.3 = (f32[792,128]{1,0:T(8,128)S(1)}, f32[792,128]{1,0:T(8,128)S(1)}, u32[]{:S(2)}, u32[]{:S(2)}) collective-permute-start(f32[792,128]{1,0:T(8,128)S(1)} %shard_map.94.received_0__0_.lat_in_0__0_), channel_id=1, source_target_pairs={{0,1},{1,0},{2,3},{3,2},{4,5},{5,4},{6,7},{7,6},{8,9},{9,8},{10,11... | collective-permute-start | bytes 1216520 | tf_op jit(solution)/shard_map/ppermute | solution.py:415
  14.4 14.2 %collective-permute-start.5 = (f32[768,128]{1,0:T(8,128)S(1)}, f32[768,128]{1,0:T(8,128)S(1)}, u32[]{:S(2)}, u32[]{:S(2)}) collective-permute-start(f32[768,128]{1,0:T(8,128)S(1)} %get-tuple-element.37), channel_id=1, source_target_pairs={{0,2},{2,0},{1,3},{3,1},{4,6},{6,4},{5,7},{7,5},{8,10},{10,8},{9,1... | collective-permute-start | bytes 1179656 | tf_op jit(solution)/shard_map/ppermute | solution.py:442
  16.3 22.6 %collective-permute-start.4 = (f32[768,128]{1,0:T(8,128)S(1)}, f32[768,128]{1,0:T(8,128)S(1)}, u32[]{:S(2)}, u32[]{:S(2)}) collective-permute-start(f32[768,128]{1,0:T(8,128)S(1)} %get-tuple-element.34.after), channel_id=1, source_target_pairs={{0,2},{2,0},{1,3},{3,1},{4,6},{6,4},{5,7},{7,5},{8,10},{10,8},{9,1... | collective-permute-start | bytes 1179656 | tf_op jit(solution)/shard_map/ppermute | solution.py:442
  24.1 10.6 %collective-permute-start.6 = (f32[2,2,48,128]{3,2,1,0:T(8,128)S(1)}, f32[2,2,48,128]{3,2,1,0:T(8,128)S(1)}, u32[]{:S(2)}, u32[]{:S(2)}) collective-permute-start(f32[2,2,48,128]{3,2,1,0:T(8,128)S(1)} %get-tuple-element.41), channel_id=1, source_target_pairs={{0,4},{4,8},{8,12},{12,0},{1,5},{5,9},{9,13},{13,1},{2,6},{6,10},{... | collective-permute-start | bytes 294920 | tf_op jit(solution)/shard_map/ppermute | solution.py:556
  25.9 9.2 %collective-permute-start.7 = (f32[2,2,48,128]{3,2,1,0:T(8,128)S(1)}, f32[2,2,48,128]{3,2,1,0:T(8,128)S(1)}, u32[]{:S(2)}, u32[]{:S(2)}) collective-permute-start(f32[2,2,48,128]{3,2,1,0:T(8,128)S(1)} %get-tuple-element.42), channel_id=1, source_target_pairs={{0,8},{4,12},{8,0},{12,4},{1,9},{5,13},{9,1},{13,5},{2,10},{6,14},... | collective-permute-start | bytes 294920 | tf_op jit(solution)/shard_map/ppermute | solution.py:556
  35.1 10.6 %collective-permute-start.10 = (f32[2,2,48,128]{3,2,1,0:T(8,128)S(1)}, f32[2,2,48,128]{3,2,1,0:T(8,128)S(1)}, u32[]{:S(2)}, u32[]{:S(2)}) collective-permute-start(f32[2,2,48,128]{3,2,1,0:T(8,128)S(1)} %get-tuple-element.47), channel_id=1, source_target_pairs={{0,4},{4,8},{8,12},{12,0},{1,5},{5,9},{9,13},{13,1},{2,6},{6,10},{... | collective-permute-start | bytes 294920 | tf_op jit(solution)/shard_map/ppermute | solution.py:556
  35.1 10.8 %collective-permute-start.11 = (f32[2,2,48,128]{3,2,1,0:T(8,128)S(1)}, f32[2,2,48,128]{3,2,1,0:T(8,128)S(1)}, u32[]{:S(2)}, u32[]{:S(2)}) collective-permute-start(f32[2,2,48,128]{3,2,1,0:T(8,128)S(1)} %get-tuple-element.48), channel_id=1, source_target_pairs={{0,8},{4,12},{8,0},{12,4},{1,9},{5,13},{9,1},{13,5},{2,10},{6,14},... | collective-permute-start | bytes 294920 | tf_op jit(solution)/shard_map/ppermute | solution.py:556
  37.3 17.1 %collective-permute-start.8 = (f32[2,2,48,128]{3,2,1,0:T(8,128)S(1)}, f32[2,2,48,128]{3,2,1,0:T(8,128)S(1)}, u32[]{:S(2)}, u32[]{:S(2)}) collective-permute-start(f32[2,2,48,128]{3,2,1,0:T(8,128)S(1)} %get-tuple-element.43), channel_id=1, source_target_pairs={{0,12},{4,0},{8,4},{12,8},{1,13},{5,1},{9,5},{13,9},{2,14},{6,2},{... | collective-permute-start | bytes 294920 | tf_op jit(solution)/shard_map/ppermute | solution.py:556
  45.1 9.7 %collective-permute-start.12 = (f32[2,2,48,128]{3,2,1,0:T(8,128)S(1)}, f32[2,2,48,128]{3,2,1,0:T(8,128)S(1)}, u32[]{:S(2)}, u32[]{:S(2)}) collective-permute-start(f32[2,2,48,128]{3,2,1,0:T(8,128)S(1)} %get-tuple-element.49), channel_id=1, source_target_pairs={{0,12},{4,0},{8,4},{12,8},{1,13},{5,1},{9,5},{13,9},{2,14},{6,2},{... | collective-permute-start | bytes 294920 | tf_op jit(solution)/shard_map/ppermute | solution.py:556
  45.9 9.8 %collective-permute-start.14 = (f32[2,2,48,128]{3,2,1,0:T(8,128)S(1)}, f32[2,2,48,128]{3,2,1,0:T(8,128)S(1)}, u32[]{:S(2)}, u32[]{:S(2)}) collective-permute-start(f32[2,2,48,128]{3,2,1,0:T(8,128)S(1)} %get-tuple-element.53), channel_id=1, source_target_pairs={{0,4},{4,8},{8,12},{12,0},{1,5},{5,9},{9,13},{13,1},{2,6},{6,10},{... | collective-permute-start | bytes 294920 | tf_op jit(solution)/shard_map/ppermute | solution.py:556
  47.2 9.3 %collective-permute-start.15 = (f32[2,2,48,128]{3,2,1,0:T(8,128)S(1)}, f32[2,2,48,128]{3,2,1,0:T(8,128)S(1)}, u32[]{:S(2)}, u32[]{:S(2)}) collective-permute-start(f32[2,2,48,128]{3,2,1,0:T(8,128)S(1)} %get-tuple-element.54), channel_id=1, source_target_pairs={{0,8},{4,12},{8,0},{12,4},{1,9},{5,13},{9,1},{13,5},{2,10},{6,14},... | collective-permute-start | bytes 294920 | tf_op jit(solution)/shard_map/ppermute | solution.py:556
  49.2 7.3 %collective-permute-start.16 = (f32[2,2,48,128]{3,2,1,0:T(8,128)S(1)}, f32[2,2,48,128]{3,2,1,0:T(8,128)S(1)}, u32[]{:S(2)}, u32[]{:S(2)}) collective-permute-start(f32[2,2,48,128]{3,2,1,0:T(8,128)S(1)} %get-tuple-element.55), channel_id=1, source_target_pairs={{0,12},{4,0},{8,4},{12,8},{1,13},{5,1},{9,5},{13,9},{2,14},{6,2},{... | collective-permute-start | bytes 294920 | tf_op jit(solution)/shard_map/ppermute | solution.py:556
  54.7 2.4 %collective-permute-start.9 = (f32[4,2,48,128]{3,2,1,0:T(8,128)S(1)}, f32[4,2,48,128]{3,2,1,0:T(8,128)S(1)}, u32[]{:S(2)}, u32[]{:S(2)}) collective-permute-start(f32[4,2,48,128]{3,2,1,0:T(8,128)S(1)} %shard_map.100), channel_id=1, source_target_pairs={{0,1},{1,0},{2,3},{3,2},{4,5},{5,4},{6,7},{7,6},{8,9},{9,8},{10,11... | collective-permute-start | bytes 589832 | tf_op jit(solution)/shard_map/ppermute | solution.py:586
  55.1 1.8 %copy-start.4 = (f32[1152]{0:T(1024)S(1)}, f32[1152]{0:T(1024)}, u32[]{:S(2)}) copy-start(f32[1152]{0:T(1024)} %param.15) | copy-start | bytes 13828
  55.1 2.0 %collective-permute-start.13 = (f32[4,2,48,128]{3,2,1,0:T(8,128)S(1)}, f32[4,2,48,128]{3,2,1,0:T(8,128)S(1)}, u32[]{:S(2)}, u32[]{:S(2)}) collective-permute-start(f32[4,2,48,128]{3,2,1,0:T(8,128)S(1)} %shard_map.102), channel_id=1, source_target_pairs={{0,1},{1,0},{2,3},{3,2},{4,5},{5,4},{6,7},{7,6},{8,9},{9,8},{10,11... | collective-permute-start | bytes 589832 | tf_op jit(solution)/shard_map/ppermute | solution.py:586
  56.8 1.5 %collective-permute-start.17 = (f32[4,2,48,128]{3,2,1,0:T(8,128)S(1)}, f32[4,2,48,128]{3,2,1,0:T(8,128)S(1)}, u32[]{:S(2)}, u32[]{:S(2)}) collective-permute-start(f32[4,2,48,128]{3,2,1,0:T(8,128)S(1)} %shard_map.104), channel_id=1, source_target_pairs={{0,1},{1,0},{2,3},{3,2},{4,5},{5,4},{6,7},{7,6},{8,9},{9,8},{10,11... | collective-permute-start | bytes 589832 | tf_op jit(solution)/shard_map/ppermute | solution.py:586
  62.6 11.1 %collective-permute-start.18 = (f32[2,288,128]{2,1,0:T(8,128)S(1)}, f32[2,288,128]{2,1,0:T(8,128)S(1)}, u32[]{:S(2)}, u32[]{:S(2)}) collective-permute-start(f32[2,288,128]{2,1,0:T(8,128)S(1)} %shard_map.107), channel_id=1, source_target_pairs={{0,12},{4,0},{8,4},{12,8},{1,13},{5,1},{9,5},{13,9},{2,14},{6,2},{... | collective-permute-start | bytes 884744 | tf_op jit(solution)/shard_map/ppermute | solution.py:620
  66.2 26.1 %collective-permute-start.19 = (f32[2,288,128]{2,1,0:T(8,128)S(1)}, f32[2,288,128]{2,1,0:T(8,128)S(1)}, u32[]{:S(2)}, u32[]{:S(2)}) collective-permute-start(f32[2,288,128]{2,1,0:T(8,128)S(1)} %shard_map.108), channel_id=1, source_target_pairs={{0,8},{4,12},{8,0},{12,4},{1,9},{5,13},{9,1},{13,5},{2,10},{6,14},... | collective-permute-start | bytes 884744 | tf_op jit(solution)/shard_map/ppermute | solution.py:620
  66.3 26.0 %collective-permute-start.20 = (f32[2,288,128]{2,1,0:T(8,128)S(1)}, f32[2,288,128]{2,1,0:T(8,128)S(1)}, u32[]{:S(2)}, u32[]{:S(2)}) collective-permute-start(f32[2,288,128]{2,1,0:T(8,128)S(1)} %shard_map.109), channel_id=1, source_target_pairs={{0,4},{4,8},{8,12},{12,0},{1,5},{5,9},{9,13},{13,1},{2,6},{6,10},{... | collective-permute-start | bytes 884744 | tf_op jit(solution)/shard_map/ppermute | solution.py:620

commit v4 on v3

--- a/solution.py
+++ b/solution.py
@@ -362,12 +362,12 @@
         out[k] = result[:, k * lanes : (k + 1) * lanes]
 
 
-def gather_kernel(rows, place, *refs):
+def gather_kernel(rows, order, place, *refs):
     pieces, out = refs[:-1], refs[-1]
     comp = place[1]
     n_comp = len(pieces)
     share = rows // n_comp
-    for r, piece in enumerate(pieces):
+    for r, piece in zip(order, pieces):
         for k in range(share):
             row = lax.rem(comp + r, n_comp) * share + k
             for i in range(0, piece.shape[1], GROUP):
@@ -512,6 +512,7 @@
     else:
         groups = n_comp // rows
         share, span = 1, lanes // groups
+    far_first = sorted(range(1, n_comp), key=lambda r: abs(2 * r - n_comp))
     arrived = []
     for i, (start, size) in enumerate(zip(starts, sizes)):
         table = lax.slice_in_dim(tables, start, start + size, axis=1)
@@ -549,11 +550,11 @@
         if split:
             sent = pieces[1:]
             if i > 0:
-                sent = gated(sent, moved[1 : n_comp - 1])
-            moved = [pieces[0]]
-            for r in range(1, n_comp):
+                sent = gated(sent, [moved[r] for r in far_first[:2]])
+            moved = [pieces[0]] + [None] * (n_comp - 1)
+            for r in far_first:
                 pairs = [(a, (a + r) % n_comp) for a in range(n_comp)]
-                moved.append(lax.ppermute(sent[r - 1], "comp", pairs))
+                moved[r] = lax.ppermute(sent[r - 1], "comp", pairs)
         else:
             energy = pieces[0].reshape(rows, n_lon, size, groups, span)
             energy = jnp.transpose(energy, (0, 3, 1, 2, 4)).reshape(n_comp, n_lon, 1, size, span)
@@ -615,18 +616,18 @@
         )
 
     if split:
-        home = [back[0]]
-        for r in range(1, n_comp):
-            home.append(lax.ppermute(back[r], "comp", [(a, (a - r) % n_comp) for a in range(n_comp)]))
+        home = [back[0]] + [None] * (n_comp - 1)
+        for r in far_first:
+            home[r] = lax.ppermute(back[r], "comp", [(a, (a - r) % n_comp) for a in range(n_comp)])
         if half == half_own:
             out = pl.pallas_call(
-                functools.partial(gather_kernel, rows),
+                functools.partial(gather_kernel, rows, [0] + far_first),
                 out_shape=jax.ShapeDtypeStruct((comps_local * rows, lanes), jnp.float32),
                 in_specs=[scalars] + [whole] * n_comp,
                 out_specs=whole,
                 compiler_params=params(),
                 cost_estimate=cost(2),
-            )(place, *home)
+            )(place, *[home[r] for r in [0] + far_first])
             return out.reshape(comps_local, rows, lanes)
         home = jnp.stack(home).reshape(n_comp, share, n_lon, half, lanes)[:, :, :, :half_own]
         home = jnp.roll(home, comp, 0)

time: 94.2 us -> 91.2 us (0.968)
  the two profiles are of different devices: /device:TPU:0 before, /device:TPU:19 now
where the time goes in v4:
time: 91.2 us; the launch traced here: 91 us
  Pallas kernels  39.3 us (43%)
  waiting for transfers between devices  28.3 us (31%)
  starting transfers between devices  21.7 us (24%)
    ppermute x3, waiting for transfers between devices, local(): lax.ppermute(back[r], 'comp', [(a, (a - r) % n_comp) for a in range(n_com...  24.7 us
    pallas_call x3, Pallas kernels, local(): pl.pallas_call(functools.partial(propagate_kernel, window, n_lon, n_comp,...  18.5 us
    ppermute x9, starting transfers between devices, local(): moved[r] = lax.ppermute(sent[r - 1], 'comp', pairs)  10.4 us
    pallas_call x1, Pallas kernels, local(): pl.pallas_call(functools.partial(matrix_kernel, home_of), grid=(2, n_comp...  5.3 us
    pallas_call x1, Pallas kernels, local(): pl.pallas_call(functools.partial(transposed_kernel, home_of, half, half_o...  4.17 us
    ppermute x3, starting transfers between devices, local(): lax.ppermute(back[r], 'comp', [(a, (a - r) % n_comp) for a in range(n_com...  3.68 us
    ppermute x3, starting transfers between devices, local(): crossed.append(lax.ppermute(packed, 'lon', pairs))  3.6 us
    pallas_call x1, Pallas kernels, local(): pl.pallas_call(functools.partial(forward_kernel, sizes, n_lon, home_of),...  2.54 us
  transfers between devices with their start and end apart: 21, of which 8 were waited for; matrix products, arithmetic and copies ran while one was open for 1% of the time, Pallas kernels for 37%

profile of v4, /device:TPU:19, one launch (start us, length us, event | category | flops | bytes accessed | tf_op | source)
XLA Modules:
  0.0 91.0 jit_solution(6940756211864180039)
XLA Ops:
  0.0 0.7 collective-permute-start.2
  0.8 1.1 %shard_map.91 = (f32[792,128]{1,0:T(8,128)S(1)}, f32[24,128]{1,0:T(8,128)S(1)}) custom-call(f32[2304,128]{1,0:T(8,128)} %bitcast.27, s32[8,128]{1,0:T(8,128)} %sea.1, s32[8,128]{1,0:T(8,128)} %depth.1, s32[8,128]{1,0:T(8,128)} %current.1), custom_call_target="tpu_custom_call" | custom-call | bytes 3500000 | tf_op jit(solution)/shard_map/pallas_call | solution.py:418
  1.9 0.2 collective-permute-start
  2.0 0.3 collective-permute-start.1
  2.3 0.1 fusion.16
  2.4 0.1 pad.9.clone
  2.4 0.1 pad.7.clone
  2.5 0.2 broadcast_multiply_fusion.1
  2.7 0.1 pad_maximum_fusion
  2.9 0.1 pad_maximum_fusion.1
  3.0 0.1 copy.24
  3.1 0.1 pad_add_fusion.place
  3.2 0.1 copy.22
  3.3 0.0 collective-permute-done.after_2_.own_1_
  3.3 0.2 collective-permute-done.2.own_in_1_
  3.5 1.6 %shard_map.92 = (f32[768,128]{1,0:T(8,128)S(1)}, f32[768,128]{1,0:T(8,128)S(1)}) custom-call(s32[3]{0:T(128)S(1)} %pad_add_fusion.place, f32[2304,128]{1,0:T(8,128)S(1)} %bitcast.28, f32[2304,128]{1,0:T(8,128)S(1)} %collective-permute-done.2.own_in_1_, f32[792,128]{1,0:T(8,128)S(1)} %get-tuple-element.33.after_0_, ...), custom_call_target="tpu_custom_call" | custom-call | bytes 5250000 | tf_op jit(solution)/shard_map/pallas_call | solution.py:433
  5.1 5.3 %shard_map.93.refs_1_.after.matrix = bf16[2,1152,1152]{2,1,0:T(8,128)(2,1)S(1)} custom-call(s32[3]{0:T(128)S(1)} %pad_add_fusion.place, f32[1,1152]{1,0:T(1,128)S(1)} %iota.18.names, f32[2,4,1152]{2,1,0:T(4,128)S(1)} %convert_bitcast_fusion.index, f32[2,4,1152]{2,1,0:T(4,128)S(1)} %maximum_bitcast_fusion.weight, f32[768,128]{1,0:T(8,128)S(1)} %get-tuple-element.34.after), custom_call_target="tpu_custom_call" | custom-call | bytes 21000000 | tf_op jit(solution)/shard_map/pallas_call | solution.py:463
  10.4 2.2 %collective-permute-done.1.refs_0_ = f32[792,128]{1,0:T(8,128)S(1)} collective-permute-done((f32[792,128]{1,0:T(8,128)S(1)}, f32[792,128]{1,0:T(8,128)S(1)}, u32[]{:S(2)}, u32[]{:S(2)}) %collective-permute-start.1) | collective-permute-done | bytes 405536 | tf_op jit(solution)/shard_map/ppermute | solution.py:442
  12.6 1.3 %collective-permute-start.3 = (f32[792,128]{1,0:T(8,128)S(1)}, f32[792,128]{1,0:T(8,128)S(1)}, u32[]{:S(2)}, u32[]{:S(2)}) collective-permute-start(f32[792,128]{1,0:T(8,128)S(1)} %shard_map.94.received_0__0_.lat_in_0__0_), channel_id=1, source_target_pairs={{0,1},{1,0},{2,3},{3,2},{4,5},{5,4},{6,7},{7,6},{8,9},{9,8},{10,11... | collective-permute-start | bytes 1216520 | tf_op jit(solution)/shard_map/ppermute | solution.py:415
  13.8 0.3 collective-permute-start.5
  14.2 0.1 maximum_maximum_fusion
  14.3 1.3 %collective-permute-start.4 = (f32[768,128]{1,0:T(8,128)S(1)}, f32[768,128]{1,0:T(8,128)S(1)}, u32[]{:S(2)}, u32[]{:S(2)}) collective-permute-start(f32[768,128]{1,0:T(8,128)S(1)} %get-tuple-element.34.after), channel_id=1, source_target_pairs={{0,2},{2,0},{1,3},{3,1},{4,6},{6,4},{5,7},{7,5},{8,10},{10,8},{9,1... | collective-permute-start | bytes 1179656 | tf_op jit(solution)/shard_map/ppermute | solution.py:442
  15.6 1.2 %shard_map.95 = (bf16[20,2,96,256]{3,2,1,0:T(8,128)(2,1)S(1)}, f32[20,3,256]{2,1,0:T(4,128)S(1)}) custom-call(s32[3]{0:T(128)S(1)} %pad_add_fusion.place, f32[24,128]{1,0:T(8,128)S(1)} %get-tuple-element.32.after_1_.own_0_, f32[24,128]{1,0:T(8,128)S(1)} %collective-permute-done.after_2_.own_1_, f32[792,128]{1,0:T(8,128)S(1)} %shard_map.94.received_0__0_.lat_in_0__0_, ...), custom_call_target="tpu_custom_call" | custom-call | bytes 7000000 | tf_op jit(solution)/shard_map/pallas_call | solution.py:479
  16.8 6.2 %shard_map.96 = (f32[2,2,48,128]{3,2,1,0:T(8,128)S(1)}, f32[2,2,48,128]{3,2,1,0:T(8,128)S(1)}, f32[2,2,48,128]{3,2,1,0:T(8,128)S(1)}, f32[2,2,48,128]{3,2,1,0:T(8,128)S(1)}) custom-call(s32[3]{0:T(128)S(1)} %pad_add_fusion.place, bf16[2,48,96]{2,1,0:T(8,128)(2,1)S(1)} %get-tuple-element.59.tables, bf16[20,2,96,256]{3,2,1,0:T(8,128)(2,1)S(1)} %get-tuple-element.35.faces, ...), custom_call_target="tpu_custom_call" | custom-call | bytes 23730000 | tf_op jit(solution)/shard_map/pallas_call | solution.py:523
  23.0 1.4 %collective-permute-start.6 = (f32[2,2,48,128]{3,2,1,0:T(8,128)S(1)}, f32[2,2,48,128]{3,2,1,0:T(8,128)S(1)}, u32[]{:S(2)}, u32[]{:S(2)}) collective-permute-start(f32[2,2,48,128]{3,2,1,0:T(8,128)S(1)} %get-tuple-element.41), channel_id=1, source_target_pairs={{0,4},{4,8},{8,12},{12,0},{1,5},{5,9},{9,13},{13,1},{2,6},{6,10},{... | collective-permute-start | bytes 294920 | tf_op jit(solution)/shard_map/ppermute | solution.py:557
  24.4 0.0 collective-permute-start.7
  24.4 0.3 collective-permute-done.5.lat_in_0__0_
  24.7 6.2 %shard_map.97 = (f32[2,2,48,128]{3,2,1,0:T(8,128)S(1)}, f32[2,2,48,128]{3,2,1,0:T(8,128)S(1)}, f32[2,2,48,128]{3,2,1,0:T(8,128)S(1)}, f32[2,2,48,128]{3,2,1,0:T(8,128)S(1)}) custom-call(s32[3]{0:T(128)S(1)} %pad_add_fusion.place, bf16[2,48,96]{2,1,0:T(8,128)(2,1)S(1)} %get-tuple-element.60.tables, bf16[20,2,96,256]{3,2,1,0:T(8,128)(2,1)S(1)} %get-tuple-element.35.faces, ...), custom_call_target="tpu_custom_call" | custom-call | bytes 23730000 | tf_op jit(solution)/shard_map/pallas_call | solution.py:523
  30.8 0.0 collective-permute-done.6.pieces_1_.refs_4_.refs_1_
  30.8 0.0 collective-permute-done.7.pieces_2_.refs_3_.refs_2_
  30.9 1.4 %collective-permute-start.10 = (f32[2,2,48,128]{3,2,1,0:T(8,128)S(1)}, f32[2,2,48,128]{3,2,1,0:T(8,128)S(1)}, u32[]{:S(2)}, u32[]{:S(2)}) collective-permute-start(f32[2,2,48,128]{3,2,1,0:T(8,128)S(1)} %get-tuple-element.47), channel_id=1, source_target_pairs={{0,4},{4,8},{8,12},{12,0},{1,5},{5,9},{9,13},{13,1},{2,6},{6,10},{... | collective-permute-start | bytes 294920 | tf_op jit(solution)/shard_map/ppermute | solution.py:557
  32.3 1.7 %collective-permute-start.11 = (f32[2,2,48,128]{3,2,1,0:T(8,128)S(1)}, f32[2,2,48,128]{3,2,1,0:T(8,128)S(1)}, u32[]{:S(2)}, u32[]{:S(2)}) collective-permute-start(f32[2,2,48,128]{3,2,1,0:T(8,128)S(1)} %get-tuple-element.48), channel_id=1, source_target_pairs={{0,8},{4,12},{8,0},{12,4},{1,9},{5,13},{9,1},{13,5},{2,10},{6,14},... | collective-permute-start | bytes 294920 | tf_op jit(solution)/shard_map/ppermute | solution.py:557
  33.9 2.4 %collective-permute-start.8 = (f32[2,2,48,128]{3,2,1,0:T(8,128)S(1)}, f32[2,2,48,128]{3,2,1,0:T(8,128)S(1)}, u32[]{:S(2)}, u32[]{:S(2)}) collective-permute-start(f32[2,2,48,128]{3,2,1,0:T(8,128)S(1)} %get-tuple-element.43), channel_id=1, source_target_pairs={{0,12},{4,0},{8,4},{12,8},{1,13},{5,1},{9,5},{13,9},{2,14},{6,2},{... | collective-permute-start | bytes 294920 | tf_op jit(solution)/shard_map/ppermute | solution.py:557
  36.3 0.0 collective-permute-done.4.lat_in_0__0_
  36.3 6.2 %shard_map.98 = (f32[2,2,48,128]{3,2,1,0:T(8,128)S(1)}, f32[2,2,48,128]{3,2,1,0:T(8,128)S(1)}, f32[2,2,48,128]{3,2,1,0:T(8,128)S(1)}, f32[2,2,48,128]{3,2,1,0:T(8,128)S(1)}) custom-call(s32[3]{0:T(128)S(1)} %pad_add_fusion.place, bf16[2,48,96]{2,1,0:T(8,128)(2,1)S(1)} %get-tuple-element.61.tables, bf16[20,2,96,256]{3,2,1,0:T(8,128)(2,1)S(1)} %get-tuple-element.35.faces, ...), custom_call_target="tpu_custom_call" | custom-call | bytes 23730000 | tf_op jit(solution)/shard_map/pallas_call | solution.py:523
  42.4 0.1 collective-permute-start.12
  42.5 1.8 %collective-permute-start.14 = (f32[2,2,48,128]{3,2,1,0:T(8,128)S(1)}, f32[2,2,48,128]{3,2,1,0:T(8,128)S(1)}, u32[]{:S(2)}, u32[]{:S(2)}) collective-permute-start(f32[2,2,48,128]{3,2,1,0:T(8,128)S(1)} %get-tuple-element.53), channel_id=1, source_target_pairs={{0,4},{4,8},{8,12},{12,0},{1,5},{5,9},{9,13},{13,1},{2,6},{6,10},{... | collective-permute-start | bytes 294920 | tf_op jit(solution)/shard_map/ppermute | solution.py:557
  44.3 0.6 collective-permute-start.15
  44.9 1.2 %collective-permute-start.16 = (f32[2,2,48,128]{3,2,1,0:T(8,128)S(1)}, f32[2,2,48,128]{3,2,1,0:T(8,128)S(1)}, u32[]{:S(2)}, u32[]{:S(2)}) collective-permute-start(f32[2,2,48,128]{3,2,1,0:T(8,128)S(1)} %get-tuple-element.55), channel_id=1, source_target_pairs={{0,12},{4,0},{8,4},{12,8},{1,13},{5,1},{9,5},{13,9},{2,14},{6,2},{... | collective-permute-start | bytes 294920 | tf_op jit(solution)/shard_map/ppermute | solution.py:557
  46.1 4.2 %shard_map.99.after_0_.matrix_t = bf16[2,1152,1152]{2,1,0:T(8,128)(2,1)S(1)} custom-call(s32[3]{0:T(128)S(1)} %pad_add_fusion.place, f32[2,4,1152]{2,1,0:T(4,128)S(1)} %convert_bitcast_fusion.index, f32[2,4,1152]{2,1,0:T(4,128)S(1)} %maximum_bitcast_fusion.weight, f32[2,2,48,128]{3,2,1,0:T(8,128)S(1)} %get-tuple-element.40.after.pieces_0_.refs_10_), custom_call_target="tpu_custom_call" | custom-call | bytes 14000000 | tf_op jit(solution)/shard_map/pallas_call | solution.py:565
  50.2 0.0 collective-permute-done.8.pieces_3_.refs_3_
  50.3 0.3 shard_map.100
  50.6 2.4 %collective-permute-start.9 = (f32[4,2,48,128]{3,2,1,0:T(8,128)S(1)}, f32[4,2,48,128]{3,2,1,0:T(8,128)S(1)}, u32[]{:S(2)}, u32[]{:S(2)}) collective-permute-start(f32[4,2,48,128]{3,2,1,0:T(8,128)S(1)} %shard_map.100), channel_id=1, source_target_pairs={{0,1},{1,0},{2,3},{3,2},{4,5},{5,4},{6,7},{7,6},{8,9},{9,8},{10,11... | collective-permute-start | bytes 589832 | tf_op jit(solution)/shard_map/ppermute | solution.py:587
  52.9 0.3 shard_map.102
  53.2 0.0 copy-start.4
  53.2 0.1 collective-permute-start.13
  53.3 0.0 collective-permute-done.14.pieces_1_.refs_11_
  53.3 0.0 collective-permute-done.15.pieces_2_.refs_12_
  53.3 0.2 collective-permute-done.16.pieces_3_.refs_13_
  53.6 0.3 shard_map.104
  53.9 1.1 %collective-permute-start.17 = (f32[4,2,48,128]{3,2,1,0:T(8,128)S(1)}, f32[4,2,48,128]{3,2,1,0:T(8,128)S(1)}, u32[]{:S(2)}, u32[]{:S(2)}) collective-permute-start(f32[4,2,48,128]{3,2,1,0:T(8,128)S(1)} %shard_map.104), channel_id=1, source_target_pairs={{0,1},{1,0},{2,3},{3,2},{4,5},{5,4},{6,7},{7,6},{8,9},{9,8},{10,11... | collective-permute-start | bytes 589832 | tf_op jit(solution)/shard_map/ppermute | solution.py:587
  55.0 0.2 reshape_broadcast_in_dim.4.coupling
  55.2 0.8 collective-permute-done.17.refs_14_
  56.0 2.5 %shard_map.105 = (f32[1152,256]{1,0:T(8,128)S(1)}, f32[1152,256]{1,0:T(8,128)S(1)}, bf16[1152,256]{1,0:T(8,128)(2,1)S(1)}) custom-call(s32[3]{0:T(128)S(1)} %pad_add_fusion.place, bf16[2,1152,1152]{2,1,0:T(8,128)(2,1)S(1)} %shard_map.93.refs_1_.after.matrix, f32[1152,1]{1,0:T(8,128)S(1)} %reshape_broadcast_in_dim.4.coupling, ...), custom_call_target="tpu_custom_call" | custom-call | bytes 14000000 | tf_op jit(solution)/shard_map/pallas_call | solution.py:591
  58.6 0.6 shard_map.109
  59.2 0.6 shard_map.108
  59.7 0.6 shard_map.107
  60.3 1.3 %collective-permute-start.18 = (f32[2,288,128]{2,1,0:T(8,128)S(1)}, f32[2,288,128]{2,1,0:T(8,128)S(1)}, u32[]{:S(2)}, u32[]{:S(2)}) collective-permute-start(f32[2,288,128]{2,1,0:T(8,128)S(1)} %shard_map.107), channel_id=1, source_target_pairs={{0,8},{4,12},{8,0},{12,4},{1,9},{5,13},{9,1},{13,5},{2,10},{6,14},... | collective-permute-start | bytes 884744 | tf_op jit(solution)/shard_map/ppermute | solution.py:621
  61.6 2.4 %collective-permute-start.19 = (f32[2,288,128]{2,1,0:T(8,128)S(1)}, f32[2,288,128]{2,1,0:T(8,128)S(1)}, u32[]{:S(2)}, u32[]{:S(2)}) collective-permute-start(f32[2,288,128]{2,1,0:T(8,128)S(1)} %shard_map.108), channel_id=1, source_target_pairs={{0,12},{4,0},{8,4},{12,8},{1,13},{5,1},{9,5},{13,9},{2,14},{6,2},{... | collective-permute-start | bytes 884744 | tf_op jit(solution)/shard_map/ppermute | solution.py:621
  64.0 0.6 shard_map.106.refs_0_
  64.6 9.4 %collective-permute-done.18.refs_1_ = f32[2,288,128]{2,1,0:T(8,128)S(1)} collective-permute-done((f32[2,288,128]{2,1,0:T(8,128)S(1)}, f32[2,288,128]{2,1,0:T(8,128)S(1)}, u32[]{:S(2)}, u32[]{:S(2)}) %collective-permute-start.18) | collective-permute-done | bytes 294944 | tf_op jit(solution)/shard_map/ppermute | solution.py:621
  73.9 12.6 %collective-permute-done.19.refs_2_ = f32[2,288,128]{2,1,0:T(8,128)S(1)} collective-permute-done((f32[2,288,128]{2,1,0:T(8,128)S(1)}, f32[2,288,128]{2,1,0:T(8,128)S(1)}, u32[]{:S(2)}, u32[]{:S(2)}) %collective-permute-start.19) | collective-permute-done | bytes 294944 | tf_op jit(solution)/shard_map/ppermute | solution.py:621
  86.6 2.7 %collective-permute-done.20.refs_3_ = f32[2,288,128]{2,1,0:T(8,128)S(1)} collective-permute-done((f32[2,288,128]{2,1,0:T(8,128)S(1)}, f32[2,288,128]{2,1,0:T(8,128)S(1)}, u32[]{:S(2)}, u32[]{:S(2)}) %collective-permute-start.20) | collective-permute-done | bytes 294944 | tf_op jit(solution)/shard_map/ppermute | solution.py:621
  89.2 1.8 %shard_map.110 = f32[2304,128]{1,0:T(8,128)} custom-call(s32[3]{0:T(128)S(1)} %pad_add_fusion.place, f32[2,288,128]{2,1,0:T(8,128)S(1)} %shard_map.106.refs_0_, f32[2,288,128]{2,1,0:T(8,128)S(1)} %collective-permute-done.18.refs_1_, f32[2,288,128]{2,1,0:T(8,128)S(1)} %collective-permute-done.19.refs_2_, f32[2,288,128]{2,1,0:T(8,128)S(1)} %collective-permute-done.20.refs_3_), custom_call_target="tpu_custom_call" | custom-call | bytes 7000000 | tf_op jit(solution)/shard_map/pallas_call | solution.py:623
  (29 shorter events, 0.2 us)
Async XLA Ops:
  0.0 2.5 %copy-start = (f32[16,32]{1,0:T(8,128)S(1)}, f32[16,32]{1,0:T(8,128)}, u32[]{:S(2)}) copy-start(f32[16,32]{1,0:T(8,128)} %param.13) | copy-start | bytes 6148
  0.0 3.5 %copy-start.1 = (f32[288,8,128]{2,1,0:T(8,128)S(1)}, f32[288,8,128]{2,1,0:T(8,128)}, u32[]{:S(2)}) copy-start(f32[288,8,128]{2,1,0:T(8,128)} %param.9) | copy-start | bytes 3538948
  0.0 2.3 %copy-start.5 = (f32[16,2]{0,1:T(2,128)S(1)}, f32[16,2]{0,1:T(2,128)}, u32[]{:S(2)}) copy-start(f32[16,2]{0,1:T(2,128)} %param.14) | copy-start | bytes 388
  0.0 2.5 %copy-start.2 = (s32[2,1152,4]{1,2,0:T(4,128)S(1)}, s32[2,1152,4]{1,2,0:T(4,128)}, u32[]{:S(2)}) copy-start(s32[2,1152,4]{1,2,0:T(4,128)} %param.16) | copy-start | bytes 110596
  0.0 2.9 %copy-start.3 = (f32[2,1152,4]{1,2,0:T(4,128)S(1)}, f32[2,1152,4]{1,2,0:T(4,128)}, u32[]{:S(2)}) copy-start(f32[2,1152,4]{1,2,0:T(4,128)} %param.17) | copy-start | bytes 110596
  0.0 3.4 %collective-permute-start.2 = (f32[2304,128]{1,0:T(8,128)}, f32[2304,128]{1,0:T(8,128)S(1)}, u32[]{:S(2)}, u32[]{:S(2)}) collective-permute-start(f32[2304,128]{1,0:T(8,128)} %bitcast.26), channel_id=1, source_target_pairs={{0,1},{1,0},{2,3},{3,2},{4,5},{5,4},{6,7},{7,6},{8,9},{9,8},{10,11... | collective-permute-start | bytes 3538952 | tf_op jit(solution)/shard_map/ppermute | solution.py:415
  1.9 1.4 %collective-permute-start = (f32[24,128]{1,0:T(8,128)S(1)}, f32[24,128]{1,0:T(8,128)S(1)}, u32[]{:S(2)}, u32[]{:S(2)}) collective-permute-start(f32[24,128]{1,0:T(8,128)S(1)} %get-tuple-element.32.after_1_.own_0_), channel_id=1, source_target_pairs={{0,1},{1,0},{2,3},{3,2},{4,5},{5,4},{6,7},{7,6},{8,9},{9,8},{10,11... | collective-permute-start | bytes 36872 | tf_op jit(solution)/shard_map/ppermute | solution.py:415
  2.0 10.5 %collective-permute-start.1 = (f32[792,128]{1,0:T(8,128)S(1)}, f32[792,128]{1,0:T(8,128)S(1)}, u32[]{:S(2)}, u32[]{:S(2)}) collective-permute-start(f32[792,128]{1,0:T(8,128)S(1)} %get-tuple-element.33.after_0_), channel_id=1, source_target_pairs={{0,2},{2,0},{1,3},{3,1},{4,6},{6,4},{5,7},{7,5},{8,10},{10,8},{9,1... | collective-permute-start | bytes 1216520 | tf_op jit(solution)/shard_map/ppermute | solution.py:442
  12.6 3.0 %collective-permute-start.3 = (f32[792,128]{1,0:T(8,128)S(1)}, f32[792,128]{1,0:T(8,128)S(1)}, u32[]{:S(2)}, u32[]{:S(2)}) collective-permute-start(f32[792,128]{1,0:T(8,128)S(1)} %shard_map.94.received_0__0_.lat_in_0__0_), channel_id=1, source_target_pairs={{0,1},{1,0},{2,3},{3,2},{4,5},{5,4},{6,7},{7,6},{8,9},{9,8},{10,11... | collective-permute-start | bytes 1216520 | tf_op jit(solution)/shard_map/ppermute | solution.py:415
  13.8 10.8 %collective-permute-start.5 = (f32[768,128]{1,0:T(8,128)S(1)}, f32[768,128]{1,0:T(8,128)S(1)}, u32[]{:S(2)}, u32[]{:S(2)}) collective-permute-start(f32[768,128]{1,0:T(8,128)S(1)} %get-tuple-element.37), channel_id=1, source_target_pairs={{0,2},{2,0},{1,3},{3,1},{4,6},{6,4},{5,7},{7,5},{8,10},{10,8},{9,1... | collective-permute-start | bytes 1179656 | tf_op jit(solution)/shard_map/ppermute | solution.py:442
  14.3 22.0 %collective-permute-start.4 = (f32[768,128]{1,0:T(8,128)S(1)}, f32[768,128]{1,0:T(8,128)S(1)}, u32[]{:S(2)}, u32[]{:S(2)}) collective-permute-start(f32[768,128]{1,0:T(8,128)S(1)} %get-tuple-element.34.after), channel_id=1, source_target_pairs={{0,2},{2,0},{1,3},{3,1},{4,6},{6,4},{5,7},{7,5},{8,10},{10,8},{9,1... | collective-permute-start | bytes 1179656 | tf_op jit(solution)/shard_map/ppermute | solution.py:442
  23.0 7.8 %collective-permute-start.6 = (f32[2,2,48,128]{3,2,1,0:T(8,128)S(1)}, f32[2,2,48,128]{3,2,1,0:T(8,128)S(1)}, u32[]{:S(2)}, u32[]{:S(2)}) collective-permute-start(f32[2,2,48,128]{3,2,1,0:T(8,128)S(1)} %get-tuple-element.41), channel_id=1, source_target_pairs={{0,4},{4,8},{8,12},{12,0},{1,5},{5,9},{9,13},{13,1},{2,6},{6,10},{... | collective-permute-start | bytes 294920 | tf_op jit(solution)/shard_map/ppermute | solution.py:557
  24.4 6.5 %collective-permute-start.7 = (f32[2,2,48,128]{3,2,1,0:T(8,128)S(1)}, f32[2,2,48,128]{3,2,1,0:T(8,128)S(1)}, u32[]{:S(2)}, u32[]{:S(2)}) collective-permute-start(f32[2,2,48,128]{3,2,1,0:T(8,128)S(1)} %get-tuple-element.42), channel_id=1, source_target_pairs={{0,8},{4,12},{8,0},{12,4},{1,9},{5,13},{9,1},{13,5},{2,10},{6,14},... | collective-permute-start | bytes 294920 | tf_op jit(solution)/shard_map/ppermute | solution.py:557
  30.9 11.7 %collective-permute-start.10 = (f32[2,2,48,128]{3,2,1,0:T(8,128)S(1)}, f32[2,2,48,128]{3,2,1,0:T(8,128)S(1)}, u32[]{:S(2)}, u32[]{:S(2)}) collective-permute-start(f32[2,2,48,128]{3,2,1,0:T(8,128)S(1)} %get-tuple-element.47), channel_id=1, source_target_pairs={{0,4},{4,8},{8,12},{12,0},{1,5},{5,9},{9,13},{13,1},{2,6},{6,10},{... | collective-permute-start | bytes 294920 | tf_op jit(solution)/shard_map/ppermute | solution.py:557
  32.3 10.3 %collective-permute-start.11 = (f32[2,2,48,128]{3,2,1,0:T(8,128)S(1)}, f32[2,2,48,128]{3,2,1,0:T(8,128)S(1)}, u32[]{:S(2)}, u32[]{:S(2)}) collective-permute-start(f32[2,2,48,128]{3,2,1,0:T(8,128)S(1)} %get-tuple-element.48), channel_id=1, source_target_pairs={{0,8},{4,12},{8,0},{12,4},{1,9},{5,13},{9,1},{13,5},{2,10},{6,14},... | collective-permute-start | bytes 294920 | tf_op jit(solution)/shard_map/ppermute | solution.py:557
  33.9 16.3 %collective-permute-start.8 = (f32[2,2,48,128]{3,2,1,0:T(8,128)S(1)}, f32[2,2,48,128]{3,2,1,0:T(8,128)S(1)}, u32[]{:S(2)}, u32[]{:S(2)}) collective-permute-start(f32[2,2,48,128]{3,2,1,0:T(8,128)S(1)} %get-tuple-element.43), channel_id=1, source_target_pairs={{0,12},{4,0},{8,4},{12,8},{1,13},{5,1},{9,5},{13,9},{2,14},{6,2},{... | collective-permute-start | bytes 294920 | tf_op jit(solution)/shard_map/ppermute | solution.py:557
  42.4 10.5 %collective-permute-start.12 = (f32[2,2,48,128]{3,2,1,0:T(8,128)S(1)}, f32[2,2,48,128]{3,2,1,0:T(8,128)S(1)}, u32[]{:S(2)}, u32[]{:S(2)}) collective-permute-start(f32[2,2,48,128]{3,2,1,0:T(8,128)S(1)} %get-tuple-element.49), channel_id=1, source_target_pairs={{0,12},{4,0},{8,4},{12,8},{1,13},{5,1},{9,5},{13,9},{2,14},{6,2},{... | collective-permute-start | bytes 294920 | tf_op jit(solution)/shard_map/ppermute | solution.py:557
  42.5 10.8 %collective-permute-start.14 = (f32[2,2,48,128]{3,2,1,0:T(8,128)S(1)}, f32[2,2,48,128]{3,2,1,0:T(8,128)S(1)}, u32[]{:S(2)}, u32[]{:S(2)}) collective-permute-start(f32[2,2,48,128]{3,2,1,0:T(8,128)S(1)} %get-tuple-element.53), channel_id=1, source_target_pairs={{0,4},{4,8},{8,12},{12,0},{1,5},{5,9},{9,13},{13,1},{2,6},{6,10},{... | collective-permute-start | bytes 294920 | tf_op jit(solution)/shard_map/ppermute | solution.py:557
  44.3 9.1 %collective-permute-start.15 = (f32[2,2,48,128]{3,2,1,0:T(8,128)S(1)}, f32[2,2,48,128]{3,2,1,0:T(8,128)S(1)}, u32[]{:S(2)}, u32[]{:S(2)}) collective-permute-start(f32[2,2,48,128]{3,2,1,0:T(8,128)S(1)} %get-tuple-element.54), channel_id=1, source_target_pairs={{0,8},{4,12},{8,0},{12,4},{1,9},{5,13},{9,1},{13,5},{2,10},{6,14},... | collective-permute-start | bytes 294920 | tf_op jit(solution)/shard_map/ppermute | solution.py:557
  44.9 8.7 %collective-permute-start.16 = (f32[2,2,48,128]{3,2,1,0:T(8,128)S(1)}, f32[2,2,48,128]{3,2,1,0:T(8,128)S(1)}, u32[]{:S(2)}, u32[]{:S(2)}) collective-permute-start(f32[2,2,48,128]{3,2,1,0:T(8,128)S(1)} %get-tuple-element.55), channel_id=1, source_target_pairs={{0,12},{4,0},{8,4},{12,8},{1,13},{5,1},{9,5},{13,9},{2,14},{6,2},{... | collective-permute-start | bytes 294920 | tf_op jit(solution)/shard_map/ppermute | solution.py:557
  50.6 4.6 %collective-permute-start.9 = (f32[4,2,48,128]{3,2,1,0:T(8,128)S(1)}, f32[4,2,48,128]{3,2,1,0:T(8,128)S(1)}, u32[]{:S(2)}, u32[]{:S(2)}) collective-permute-start(f32[4,2,48,128]{3,2,1,0:T(8,128)S(1)} %shard_map.100), channel_id=1, source_target_pairs={{0,1},{1,0},{2,3},{3,2},{4,5},{5,4},{6,7},{7,6},{8,9},{9,8},{10,11... | collective-permute-start | bytes 589832 | tf_op jit(solution)/shard_map/ppermute | solution.py:587
  53.2 1.8 %copy-start.4 = (f32[1152]{0:T(1024)S(1)}, f32[1152]{0:T(1024)}, u32[]{:S(2)}) copy-start(f32[1152]{0:T(1024)} %param.15) | copy-start | bytes 13828
  53.2 2.0 %collective-permute-start.13 = (f32[4,2,48,128]{3,2,1,0:T(8,128)S(1)}, f32[4,2,48,128]{3,2,1,0:T(8,128)S(1)}, u32[]{:S(2)}, u32[]{:S(2)}) collective-permute-start(f32[4,2,48,128]{3,2,1,0:T(8,128)S(1)} %shard_map.102), channel_id=1, source_target_pairs={{0,1},{1,0},{2,3},{3,2},{4,5},{5,4},{6,7},{7,6},{8,9},{9,8},{10,11... | collective-permute-start | bytes 589832 | tf_op jit(solution)/shard_map/ppermute | solution.py:587
  53.9 2.2 %collective-permute-start.17 = (f32[4,2,48,128]{3,2,1,0:T(8,128)S(1)}, f32[4,2,48,128]{3,2,1,0:T(8,128)S(1)}, u32[]{:S(2)}, u32[]{:S(2)}) collective-permute-start(f32[4,2,48,128]{3,2,1,0:T(8,128)S(1)} %shard_map.104), channel_id=1, source_target_pairs={{0,1},{1,0},{2,3},{3,2},{4,5},{5,4},{6,7},{7,6},{8,9},{9,8},{10,11... | collective-permute-start | bytes 589832 | tf_op jit(solution)/shard_map/ppermute | solution.py:587
  60.3 13.6 %collective-permute-start.18 = (f32[2,288,128]{2,1,0:T(8,128)S(1)}, f32[2,288,128]{2,1,0:T(8,128)S(1)}, u32[]{:S(2)}, u32[]{:S(2)}) collective-permute-start(f32[2,288,128]{2,1,0:T(8,128)S(1)} %shard_map.107), channel_id=1, source_target_pairs={{0,8},{4,12},{8,0},{12,4},{1,9},{5,13},{9,1},{13,5},{2,10},{6,14},... | collective-permute-start | bytes 884744 | tf_op jit(solution)/shard_map/ppermute | solution.py:621
  61.6 25.0 %collective-permute-start.19 = (f32[2,288,128]{2,1,0:T(8,128)S(1)}, f32[2,288,128]{2,1,0:T(8,128)S(1)}, u32[]{:S(2)}, u32[]{:S(2)}) collective-permute-start(f32[2,288,128]{2,1,0:T(8,128)S(1)} %shard_map.108), channel_id=1, source_target_pairs={{0,12},{4,0},{8,4},{12,8},{1,13},{5,1},{9,5},{13,9},{2,14},{6,2},{... | collective-permute-start | bytes 884744 | tf_op jit(solution)/shard_map/ppermute | solution.py:621
  64.0 25.2 %collective-permute-start.20 = (f32[2,288,128]{2,1,0:T(8,128)S(1)}, f32[2,288,128]{2,1,0:T(8,128)S(1)}, u32[]{:S(2)}, u32[]{:S(2)}) collective-permute-start(f32[2,288,128]{2,1,0:T(8,128)S(1)} %shard_map.109), channel_id=1, source_target_pairs={{0,4},{4,8},{8,12},{12,0},{1,5},{5,9},{9,13},{13,1},{2,6},{6,10},{... | collective-permute-start | bytes 884744 | tf_op jit(solution)/shard_map/ppermute | solution.py:621

commit v5 on v4

--- a/solution.py
+++ b/solution.py
@@ -302,10 +302,10 @@
 
     def step(i, _):
         at = pl.multiple_of(i * GROUP, GROUP)
-        row = base + at + lax.broadcasted_iota(jnp.int32, (GROUP, 1), 0)
+        row = base + at + lax.broadcasted_iota(jnp.int32, (GROUP, 128), 0)
         if half != half_own:
             row = jnp.where(row % half < half_own, row // half * half_own + row % half, -1)
-        row = jnp.broadcast_to(row.astype(jnp.float32), (GROUP, total))
+        row = jnp.concatenate([row.astype(jnp.float32)] * (-(-total // 128)), axis=1)[:, :total]
         made = jnp.zeros((GROUP, total), jnp.float32)
         for corner in range(4):
             made = jnp.where(row == index[0, corner : corner + 1, :], weight[0, corner : corner + 1, :], made)
@@ -362,14 +362,14 @@
         out[k] = result[:, k * lanes : (k + 1) * lanes]
 
 
-def gather_kernel(rows, order, place, *refs):
+def gather_kernel(rows, n_comp, order, place, held, *refs):
     pieces, out = refs[:-1], refs[-1]
-    comp = place[1]
-    n_comp = len(pieces)
     share = rows // n_comp
+    for ref in held:
+        out[...] = ref[...]
     for r, piece in zip(order, pieces):
         for k in range(share):
-            row = lax.rem(comp + r, n_comp) * share + k
+            row = lax.rem(place[1] + r, n_comp) * share + k
             for i in range(0, piece.shape[1], GROUP):
                 out[pl.ds(i * rows + row, GROUP, stride=rows), :] = piece[k, i : i + GROUP, :]
 
@@ -464,12 +464,12 @@
         functools.partial(matrix_kernel, home_of),
         grid=(2, n_comp),
         out_shape=pltpu.VMEM((2, total, total), jnp.bfloat16),
-        in_specs=[scalars, whole, by_cols, by_cols, anywhere],
+        in_specs=[scalars, whole, by_cols, by_cols, [anywhere] * 2],
         out_specs=by_block,
         scratch_shapes=[pltpu.VMEM((total, 8), jnp.float32)],
         compiler_params=params(),
         cost_estimate=cost(6),
-    )(place, names, index, weight, blocks[-1])
+    )(place, names, index, weight, [blocks[-1], strength])
 
     lat_in[0] = [on_all_columns(block) for block in gated(lat_in[0], [matrix])]
     lat_in[1:] = [[[block] for block in found] for found in lat_in[1:]]
@@ -513,6 +513,7 @@
         groups = n_comp // rows
         share, span = 1, lanes // groups
     far_first = sorted(range(1, n_comp), key=lambda r: abs(2 * r - n_comp))
+    order = [0] + far_first
     arrived = []
     for i, (start, size) in enumerate(zip(starts, sizes)):
         table = lax.slice_in_dim(tables, start, start + size, axis=1)
@@ -620,14 +621,19 @@
         for r in far_first:
             home[r] = lax.ppermute(back[r], "comp", [(a, (a - r) % n_comp) for a in range(n_comp)])
         if half == half_own:
-            out = pl.pallas_call(
-                functools.partial(gather_kernel, rows, [0] + far_first),
-                out_shape=jax.ShapeDtypeStruct((comps_local * rows, lanes), jnp.float32),
-                in_specs=[scalars] + [whole] * n_comp,
-                out_specs=whole,
-                compiler_params=params(),
-                cost_estimate=cost(2),
-            )(place, *[home[r] for r in [0] + far_first])
+            held = []
+            for some in (order[:2], order[2:]):
+                held = [
+                    pl.pallas_call(
+                        functools.partial(gather_kernel, rows, n_comp, some),
+                        out_shape=jax.ShapeDtypeStruct((comps_local * rows, lanes), jnp.float32),
+                        in_specs=[scalars, [whole] * len(held)] + [whole] * len(some),
+                        out_specs=whole,
+                        compiler_params=params(),
+                        cost_estimate=cost(1),
+                    )(place, held, *[home[r] for r in some])
+                ]
+            out = held[0]
             return out.reshape(comps_local, rows, lanes)
         home = jnp.stack(home).reshape(n_comp, share, n_lon, half, lanes)[:, :, :, :half_own]
         home = jnp.roll(home, comp, 0)

time: 91.2 us -> 90.6 us (level)
  waiting for transfers between devices: 28.3 us -> 27.2 us
    ppermute x3, waiting for transfers between devices: 24.7 us -> 23.4 us  [local(): lax.ppermute(back[r], 'comp', [(a, (a - r) % n_comp) for a in range(n_com...]
    pallas_call x1 -> x2, Pallas kernels: 1.76 us -> 2.36 us  [local(): pl.pallas_call(functools.partial(gather_kernel, rows, n_comp, some), out_...]
  transfers between devices with their start and end apart: 21 -> 21, of which waited for: 8 -> 7; matrix products, arithmetic and copies ran while one was open for 1% -> 1% of each run, Pallas kernels for 37% -> 38%
where the time goes in v5:
time: 90.6 us; the launch traced here: 90.5 us
  Pallas kernels  39.9 us (44%)
  waiting for transfers between devices  27.2 us (30%)
  starting transfers between devices  21.7 us (24%)
    ppermute x3, waiting for transfers between devices, local(): lax.ppermute(back[r], 'comp', [(a, (a - r) % n_comp) for a in range(n_com...  23.4 us
    pallas_call x3, Pallas kernels, local(): pl.pallas_call(functools.partial(propagate_kernel, window, n_lon, n_comp,...  18.5 us
    ppermute x9, starting transfers between devices, local(): moved[r] = lax.ppermute(sent[r - 1], 'comp', pairs)  10.4 us
    pallas_call x1, Pallas kernels, local(): pl.pallas_call(functools.partial(matrix_kernel, home_of), grid=(2, n_comp...  5.3 us
    pallas_call x1, Pallas kernels, local(): pl.pallas_call(functools.partial(transposed_kernel, home_of, half, half_o...  4.17 us
    ppermute x3, starting transfers between devices, local(): lax.ppermute(back[r], 'comp', [(a, (a - r) % n_comp) for a in range(n_com...  3.72 us
    ppermute x3, starting transfers between devices, local(): crossed.append(lax.ppermute(packed, 'lon', pairs))  3.61 us
    pallas_call x1, Pallas kernels, local(): pl.pallas_call(functools.partial(forward_kernel, sizes, n_lon, home_of),...  2.55 us
  transfers between devices with their start and end apart: 21, of which 7 were waited for; matrix products, arithmetic and copies ran while one was open for 1% of the time, Pallas kernels for 38%

profile of v5, /device:TPU:19, one launch (start us, length us, event | category | flops | bytes accessed | tf_op | source)
XLA Modules:
  0.0 90.5 jit_solution(17341705312535108348)
XLA Ops:
  0.0 0.7 collective-permute-start.2
  0.8 1.1 %shard_map.91 = (f32[792,128]{1,0:T(8,128)S(1)}, f32[24,128]{1,0:T(8,128)S(1)}) custom-call(f32[2304,128]{1,0:T(8,128)} %bitcast.27, s32[8,128]{1,0:T(8,128)} %sea.1, s32[8,128]{1,0:T(8,128)} %depth.1, s32[8,128]{1,0:T(8,128)} %current.1), custom_call_target="tpu_custom_call" | custom-call | bytes 3500000 | tf_op jit(solution)/shard_map/pallas_call | solution.py:418
  1.9 0.2 collective-permute-start
  2.1 0.3 collective-permute-start.1
  2.4 0.1 fusion.16
  2.4 0.1 pad.9.clone
  2.5 0.1 pad.7.clone
  2.6 0.2 broadcast_multiply_fusion.1
  2.8 0.1 pad_maximum_fusion
  3.0 0.1 pad_maximum_fusion.1
  3.1 0.1 copy.25
  3.2 0.1 pad_add_fusion.place
  3.3 0.1 copy.23
  3.4 0.2 reshape_broadcast_in_dim.4.after_1_.coupling
  3.6 0.0 collective-permute-done.2.own_in_1_
  3.6 1.6 %shard_map.92 = (f32[768,128]{1,0:T(8,128)S(1)}, f32[768,128]{1,0:T(8,128)S(1)}) custom-call(s32[3]{0:T(128)S(1)} %pad_add_fusion.place, f32[2304,128]{1,0:T(8,128)S(1)} %bitcast.28, f32[2304,128]{1,0:T(8,128)S(1)} %collective-permute-done.2.own_in_1_, f32[792,128]{1,0:T(8,128)S(1)} %get-tuple-element.33.after_0_, ...), custom_call_target="tpu_custom_call" | custom-call | bytes 5250000 | tf_op jit(solution)/shard_map/pallas_call | solution.py:433
  5.2 5.3 %shard_map.93.refs_1_.after.matrix = bf16[2,1152,1152]{2,1,0:T(8,128)(2,1)S(1)} custom-call(s32[3]{0:T(128)S(1)} %pad_add_fusion.place, f32[1,1152]{1,0:T(1,128)S(1)} %iota.18.names, f32[2,4,1152]{2,1,0:T(4,128)S(1)} %convert_bitcast_fusion.index, f32[2,4,1152]{2,1,0:T(4,128)S(1)} %maximum_bitcast_fusion.weight, f32[768,128]{1,0:T(8,128)S(1)} %get-tuple-element.34.after_0_, ...), custom_call_target="tpu_custom_call" | custom-call | bytes 21000000 | tf_op jit(solution)/shard_map/pallas_call | solution.py:463
  10.6 2.2 %collective-permute-done.1.refs_0_ = f32[792,128]{1,0:T(8,128)S(1)} collective-permute-done((f32[792,128]{1,0:T(8,128)S(1)}, f32[792,128]{1,0:T(8,128)S(1)}, u32[]{:S(2)}, u32[]{:S(2)}) %collective-permute-start.1) | collective-permute-done | bytes 405536 | tf_op jit(solution)/shard_map/ppermute | solution.py:442
  12.7 1.2 %collective-permute-start.3 = (f32[792,128]{1,0:T(8,128)S(1)}, f32[792,128]{1,0:T(8,128)S(1)}, u32[]{:S(2)}, u32[]{:S(2)}) collective-permute-start(f32[792,128]{1,0:T(8,128)S(1)} %shard_map.94.received_0__0_.lat_in_0__0_), channel_id=1, source_target_pairs={{0,1},{1,0},{2,3},{3,2},{4,5},{5,4},{6,7},{7,6},{8,9},{9,8},{10,11... | collective-permute-start | bytes 1216520 | tf_op jit(solution)/shard_map/ppermute | solution.py:415
  13.9 0.3 collective-permute-start.5
  14.2 0.1 maximum_maximum_fusion
  14.4 1.3 %collective-permute-start.4 = (f32[768,128]{1,0:T(8,128)S(1)}, f32[768,128]{1,0:T(8,128)S(1)}, u32[]{:S(2)}, u32[]{:S(2)}) collective-permute-start(f32[768,128]{1,0:T(8,128)S(1)} %get-tuple-element.34.after_0_), channel_id=1, source_target_pairs={{0,2},{2,0},{1,3},{3,1},{4,6},{6,4},{5,7},{7,5},{8,10},{10,8},{9,1... | collective-permute-start | bytes 1179656 | tf_op jit(solution)/shard_map/ppermute | solution.py:442
  15.6 0.0 collective-permute-done.3.received_0__1_.lat_in_0__1_
  15.6 1.2 %shard_map.95 = (bf16[20,2,96,256]{3,2,1,0:T(8,128)(2,1)S(1)}, f32[20,3,256]{2,1,0:T(4,128)S(1)}) custom-call(s32[3]{0:T(128)S(1)} %pad_add_fusion.place, f32[24,128]{1,0:T(8,128)S(1)} %get-tuple-element.32.after_1_.own_0_, f32[24,128]{1,0:T(8,128)S(1)} %collective-permute-done.after_2_.own_1_, f32[792,128]{1,0:T(8,128)S(1)} %shard_map.94.received_0__0_.lat_in_0__0_, ...), custom_call_target="tpu_custom_call" | custom-call | bytes 7000000 | tf_op jit(solution)/shard_map/pallas_call | solution.py:479
  16.9 6.2 %shard_map.96 = (f32[2,2,48,128]{3,2,1,0:T(8,128)S(1)}, f32[2,2,48,128]{3,2,1,0:T(8,128)S(1)}, f32[2,2,48,128]{3,2,1,0:T(8,128)S(1)}, f32[2,2,48,128]{3,2,1,0:T(8,128)S(1)}) custom-call(s32[3]{0:T(128)S(1)} %pad_add_fusion.place, bf16[2,48,96]{2,1,0:T(8,128)(2,1)S(1)} %get-tuple-element.59.tables, bf16[20,2,96,256]{3,2,1,0:T(8,128)(2,1)S(1)} %get-tuple-element.35.faces, ...), custom_call_target="tpu_custom_call" | custom-call | bytes 23730000 | tf_op jit(solution)/shard_map/pallas_call | solution.py:524
  23.1 1.4 %collective-permute-start.6 = (f32[2,2,48,128]{3,2,1,0:T(8,128)S(1)}, f32[2,2,48,128]{3,2,1,0:T(8,128)S(1)}, u32[]{:S(2)}, u32[]{:S(2)}) collective-permute-start(f32[2,2,48,128]{3,2,1,0:T(8,128)S(1)} %get-tuple-element.41), channel_id=1, source_target_pairs={{0,4},{4,8},{8,12},{12,0},{1,5},{5,9},{9,13},{13,1},{2,6},{6,10},{... | collective-permute-start | bytes 294920 | tf_op jit(solution)/shard_map/ppermute | solution.py:558
  24.4 0.0 collective-permute-start.7
  24.5 0.3 collective-permute-done.5.lat_in_0__0_
  24.7 6.2 %shard_map.97 = (f32[2,2,48,128]{3,2,1,0:T(8,128)S(1)}, f32[2,2,48,128]{3,2,1,0:T(8,128)S(1)}, f32[2,2,48,128]{3,2,1,0:T(8,128)S(1)}, f32[2,2,48,128]{3,2,1,0:T(8,128)S(1)}) custom-call(s32[3]{0:T(128)S(1)} %pad_add_fusion.place, bf16[2,48,96]{2,1,0:T(8,128)(2,1)S(1)} %get-tuple-element.60.tables, bf16[20,2,96,256]{3,2,1,0:T(8,128)(2,1)S(1)} %get-tuple-element.35.faces, ...), custom_call_target="tpu_custom_call" | custom-call | bytes 23730000 | tf_op jit(solution)/shard_map/pallas_call | solution.py:524
  30.9 0.0 collective-permute-done.6.pieces_1_.refs_4_.refs_1_
  30.9 0.0 collective-permute-done.7.pieces_2_.refs_3_.refs_2_
  30.9 1.4 %collective-permute-start.10 = (f32[2,2,48,128]{3,2,1,0:T(8,128)S(1)}, f32[2,2,48,128]{3,2,1,0:T(8,128)S(1)}, u32[]{:S(2)}, u32[]{:S(2)}) collective-permute-start(f32[2,2,48,128]{3,2,1,0:T(8,128)S(1)} %get-tuple-element.47), channel_id=1, source_target_pairs={{0,4},{4,8},{8,12},{12,0},{1,5},{5,9},{9,13},{13,1},{2,6},{6,10},{... | collective-permute-start | bytes 294920 | tf_op jit(solution)/shard_map/ppermute | solution.py:558
  32.3 1.7 %collective-permute-start.11 = (f32[2,2,48,128]{3,2,1,0:T(8,128)S(1)}, f32[2,2,48,128]{3,2,1,0:T(8,128)S(1)}, u32[]{:S(2)}, u32[]{:S(2)}) collective-permute-start(f32[2,2,48,128]{3,2,1,0:T(8,128)S(1)} %get-tuple-element.48), channel_id=1, source_target_pairs={{0,8},{4,12},{8,0},{12,4},{1,9},{5,13},{9,1},{13,5},{2,10},{6,14},... | collective-permute-start | bytes 294920 | tf_op jit(solution)/shard_map/ppermute | solution.py:558
  34.0 2.4 %collective-permute-start.8 = (f32[2,2,48,128]{3,2,1,0:T(8,128)S(1)}, f32[2,2,48,128]{3,2,1,0:T(8,128)S(1)}, u32[]{:S(2)}, u32[]{:S(2)}) collective-permute-start(f32[2,2,48,128]{3,2,1,0:T(8,128)S(1)} %get-tuple-element.43), channel_id=1, source_target_pairs={{0,12},{4,0},{8,4},{12,8},{1,13},{5,1},{9,5},{13,9},{2,14},{6,2},{... | collective-permute-start | bytes 294920 | tf_op jit(solution)/shard_map/ppermute | solution.py:558
  36.3 6.2 %shard_map.98 = (f32[2,2,48,128]{3,2,1,0:T(8,128)S(1)}, f32[2,2,48,128]{3,2,1,0:T(8,128)S(1)}, f32[2,2,48,128]{3,2,1,0:T(8,128)S(1)}, f32[2,2,48,128]{3,2,1,0:T(8,128)S(1)}) custom-call(s32[3]{0:T(128)S(1)} %pad_add_fusion.place, bf16[2,48,96]{2,1,0:T(8,128)(2,1)S(1)} %get-tuple-element.61.tables, bf16[20,2,96,256]{3,2,1,0:T(8,128)(2,1)S(1)} %get-tuple-element.35.faces, ...), custom_call_target="tpu_custom_call" | custom-call | bytes 23730000 | tf_op jit(solution)/shard_map/pallas_call | solution.py:524
  42.5 0.1 collective-permute-start.12
  42.6 0.0 collective-permute-done.10.pieces_1_.refs_4_.refs_6_
  42.6 1.8 %collective-permute-start.14 = (f32[2,2,48,128]{3,2,1,0:T(8,128)S(1)}, f32[2,2,48,128]{3,2,1,0:T(8,128)S(1)}, u32[]{:S(2)}, u32[]{:S(2)}) collective-permute-start(f32[2,2,48,128]{3,2,1,0:T(8,128)S(1)} %get-tuple-element.53), channel_id=1, source_target_pairs={{0,4},{4,8},{8,12},{12,0},{1,5},{5,9},{9,13},{13,1},{2,6},{6,10},{... | collective-permute-start | bytes 294920 | tf_op jit(solution)/shard_map/ppermute | solution.py:558
  44.4 0.6 collective-permute-start.15
  44.9 1.2 %collective-permute-start.16 = (f32[2,2,48,128]{3,2,1,0:T(8,128)S(1)}, f32[2,2,48,128]{3,2,1,0:T(8,128)S(1)}, u32[]{:S(2)}, u32[]{:S(2)}) collective-permute-start(f32[2,2,48,128]{3,2,1,0:T(8,128)S(1)} %get-tuple-element.55), channel_id=1, source_target_pairs={{0,12},{4,0},{8,4},{12,8},{1,13},{5,1},{9,5},{13,9},{2,14},{6,2},{... | collective-permute-start | bytes 294920 | tf_op jit(solution)/shard_map/ppermute | solution.py:558
  46.1 4.2 %shard_map.99.after_0_.matrix_t = bf16[2,1152,1152]{2,1,0:T(8,128)(2,1)S(1)} custom-call(s32[3]{0:T(128)S(1)} %pad_add_fusion.place, f32[2,4,1152]{2,1,0:T(4,128)S(1)} %convert_bitcast_fusion.index, f32[2,4,1152]{2,1,0:T(4,128)S(1)} %maximum_bitcast_fusion.weight, f32[2,2,48,128]{3,2,1,0:T(8,128)S(1)} %get-tuple-element.40.after.pieces_0_.refs_10_), custom_call_target="tpu_custom_call" | custom-call | bytes 14000000 | tf_op jit(solution)/shard_map/pallas_call | solution.py:566
  50.3 0.3 shard_map.100
  50.6 2.4 %collective-permute-start.9 = (f32[4,2,48,128]{3,2,1,0:T(8,128)S(1)}, f32[4,2,48,128]{3,2,1,0:T(8,128)S(1)}, u32[]{:S(2)}, u32[]{:S(2)}) collective-permute-start(f32[4,2,48,128]{3,2,1,0:T(8,128)S(1)} %shard_map.100), channel_id=1, source_target_pairs={{0,1},{1,0},{2,3},{3,2},{4,5},{5,4},{6,7},{7,6},{8,9},{9,8},{10,11... | collective-permute-start | bytes 589832 | tf_op jit(solution)/shard_map/ppermute | solution.py:588
  53.0 0.0 collective-permute-done.12.pieces_3_.refs_8_
  53.0 0.3 shard_map.102
  53.3 0.1 collective-permute-start.13
  53.4 0.0 collective-permute-done.15.pieces_2_.refs_12_
  53.4 0.2 collective-permute-done.16.pieces_3_.refs_13_
  53.7 0.3 shard_map.104
  53.9 1.1 %collective-permute-start.17 = (f32[4,2,48,128]{3,2,1,0:T(8,128)S(1)}, f32[4,2,48,128]{3,2,1,0:T(8,128)S(1)}, u32[]{:S(2)}, u32[]{:S(2)}) collective-permute-start(f32[4,2,48,128]{3,2,1,0:T(8,128)S(1)} %shard_map.104), channel_id=1, source_target_pairs={{0,1},{1,0},{2,3},{3,2},{4,5},{5,4},{6,7},{7,6},{8,9},{9,8},{10,11... | collective-permute-start | bytes 589832 | tf_op jit(solution)/shard_map/ppermute | solution.py:588
  55.1 0.0 collective-permute-done.9.refs_4_
  55.1 1.1 %collective-permute-done.17.refs_14_ = f32[4,2,48,128]{3,2,1,0:T(8,128)S(1)} collective-permute-done((f32[4,2,48,128]{3,2,1,0:T(8,128)S(1)}, f32[4,2,48,128]{3,2,1,0:T(8,128)S(1)}, u32[]{:S(2)}, u32[]{:S(2)}) %collective-permute-start.17) | collective-permute-done | bytes 196640 | tf_op jit(solution)/shard_map/ppermute | solution.py:588
  56.1 2.5 %shard_map.105 = (f32[1152,256]{1,0:T(8,128)S(1)}, f32[1152,256]{1,0:T(8,128)S(1)}, bf16[1152,256]{1,0:T(8,128)(2,1)S(1)}) custom-call(s32[3]{0:T(128)S(1)} %pad_add_fusion.place, bf16[2,1152,1152]{2,1,0:T(8,128)(2,1)S(1)} %shard_map.93.refs_1_.after.matrix, f32[1152,1]{1,0:T(8,128)S(1)} %reshape_broadcast_in_dim.4.after_1_.coupling, ...), custom_call_target="tpu_custom_call" | custom-call | bytes 14000000 | tf_op jit(solution)/shard_map/pallas_call | solution.py:592
  58.7 0.6 shard_map.110
  59.3 0.6 shard_map.107
  59.8 1.3 %collective-permute-start.18 = (f32[2,288,128]{2,1,0:T(8,128)S(1)}, f32[2,288,128]{2,1,0:T(8,128)S(1)}, u32[]{:S(2)}, u32[]{:S(2)}) collective-permute-start(f32[2,288,128]{2,1,0:T(8,128)S(1)} %shard_map.107), channel_id=1, source_target_pairs={{0,8},{4,12},{8,0},{12,4},{1,9},{5,13},{9,1},{13,5},{2,10},{6,14},... | collective-permute-start | bytes 884744 | tf_op jit(solution)/shard_map/ppermute | solution.py:622
  61.1 0.6 shard_map.109
  61.7 2.5 %collective-permute-start.19 = (f32[2,288,128]{2,1,0:T(8,128)S(1)}, f32[2,288,128]{2,1,0:T(8,128)S(1)}, u32[]{:S(2)}, u32[]{:S(2)}) collective-permute-start(f32[2,288,128]{2,1,0:T(8,128)S(1)} %shard_map.109), channel_id=1, source_target_pairs={{0,12},{4,0},{8,4},{12,8},{1,13},{5,1},{9,5},{13,9},{2,14},{6,2},{... | collective-permute-start | bytes 884744 | tf_op jit(solution)/shard_map/ppermute | solution.py:622
  64.1 0.6 shard_map.106.refs_0_
  64.7 8.8 %collective-permute-done.18.refs_1_ = f32[2,288,128]{2,1,0:T(8,128)S(1)} collective-permute-done((f32[2,288,128]{2,1,0:T(8,128)S(1)}, f32[2,288,128]{2,1,0:T(8,128)S(1)}, u32[]{:S(2)}, u32[]{:S(2)}) %collective-permute-start.18) | collective-permute-done | bytes 294944 | tf_op jit(solution)/shard_map/ppermute | solution.py:622
  73.5 0.6 shard_map.108.held_0_
  74.1 12.0 %collective-permute-done.19.refs_0_ = f32[2,288,128]{2,1,0:T(8,128)S(1)} collective-permute-done((f32[2,288,128]{2,1,0:T(8,128)S(1)}, f32[2,288,128]{2,1,0:T(8,128)S(1)}, u32[]{:S(2)}, u32[]{:S(2)}) %collective-permute-start.19) | collective-permute-done | bytes 294944 | tf_op jit(solution)/shard_map/ppermute | solution.py:622
  86.1 2.7 %collective-permute-done.20.refs_1_ = f32[2,288,128]{2,1,0:T(8,128)S(1)} collective-permute-done((f32[2,288,128]{2,1,0:T(8,128)S(1)}, f32[2,288,128]{2,1,0:T(8,128)S(1)}, u32[]{:S(2)}, u32[]{:S(2)}) %collective-permute-start.20) | collective-permute-done | bytes 294944 | tf_op jit(solution)/shard_map/ppermute | solution.py:622
  88.8 1.7 %shard_map.111 = f32[2304,128]{1,0:T(8,128)} custom-call(s32[3]{0:T(128)S(1)} %pad_add_fusion.place, f32[2304,128]{1,0:T(8,128)S(1)} %shard_map.108.held_0_, f32[2,288,128]{2,1,0:T(8,128)S(1)} %collective-permute-done.19.refs_0_, f32[2,288,128]{2,1,0:T(8,128)S(1)} %collective-permute-done.20.refs_1_), custom_call_target="tpu_custom_call" | custom-call | bytes 3500000 | tf_op jit(solution)/shard_map/pallas_call | solution.py:627
  (30 shorter events, 0.2 us)
Async XLA Ops:
  0.0 2.6 %copy-start = (f32[16,32]{1,0:T(8,128)S(1)}, f32[16,32]{1,0:T(8,128)}, u32[]{:S(2)}) copy-start(f32[16,32]{1,0:T(8,128)} %param.13) | copy-start | bytes 6148
  0.0 2.4 %copy-start.5 = (f32[16,2]{0,1:T(2,128)S(1)}, f32[16,2]{0,1:T(2,128)}, u32[]{:S(2)}) copy-start(f32[16,2]{0,1:T(2,128)} %param.14) | copy-start | bytes 388
  0.0 2.6 %copy-start.2 = (s32[2,1152,4]{1,2,0:T(4,128)S(1)}, s32[2,1152,4]{1,2,0:T(4,128)}, u32[]{:S(2)}) copy-start(s32[2,1152,4]{1,2,0:T(4,128)} %param.16) | copy-start | bytes 110596
  0.0 2.9 %copy-start.3 = (f32[2,1152,4]{1,2,0:T(4,128)S(1)}, f32[2,1152,4]{1,2,0:T(4,128)}, u32[]{:S(2)}) copy-start(f32[2,1152,4]{1,2,0:T(4,128)} %param.17) | copy-start | bytes 110596
  0.0 3.3 %copy-start.4 = (f32[1152]{0:T(1024)S(1)}, f32[1152]{0:T(1024)}, u32[]{:S(2)}) copy-start(f32[1152]{0:T(1024)} %param.15) | copy-start | bytes 13828
  0.0 3.6 %copy-start.1 = (f32[288,8,128]{2,1,0:T(8,128)S(1)}, f32[288,8,128]{2,1,0:T(8,128)}, u32[]{:S(2)}) copy-start(f32[288,8,128]{2,1,0:T(8,128)} %param.9) | copy-start | bytes 3538948
  0.0 3.6 %collective-permute-start.2 = (f32[2304,128]{1,0:T(8,128)}, f32[2304,128]{1,0:T(8,128)S(1)}, u32[]{:S(2)}, u32[]{:S(2)}) collective-permute-start(f32[2304,128]{1,0:T(8,128)} %bitcast.26), channel_id=1, source_target_pairs={{0,1},{1,0},{2,3},{3,2},{4,5},{5,4},{6,7},{7,6},{8,9},{9,8},{10,11... | collective-permute-start | bytes 3538952 | tf_op jit(solution)/shard_map/ppermute | solution.py:415
  1.9 1.7 %collective-permute-start = (f32[24,128]{1,0:T(8,128)S(1)}, f32[24,128]{1,0:T(8,128)S(1)}, u32[]{:S(2)}, u32[]{:S(2)}) collective-permute-start(f32[24,128]{1,0:T(8,128)S(1)} %get-tuple-element.32.after_1_.own_0_), channel_id=1, source_target_pairs={{0,1},{1,0},{2,3},{3,2},{4,5},{5,4},{6,7},{7,6},{8,9},{9,8},{10,11... | collective-permute-start | bytes 36872 | tf_op jit(solution)/shard_map/ppermute | solution.py:415
  2.1 10.6 %collective-permute-start.1 = (f32[792,128]{1,0:T(8,128)S(1)}, f32[792,128]{1,0:T(8,128)S(1)}, u32[]{:S(2)}, u32[]{:S(2)}) collective-permute-start(f32[792,128]{1,0:T(8,128)S(1)} %get-tuple-element.33.after_0_), channel_id=1, source_target_pairs={{0,2},{2,0},{1,3},{3,1},{4,6},{6,4},{5,7},{7,5},{8,10},{10,8},{9,1... | collective-permute-start | bytes 1216520 | tf_op jit(solution)/shard_map/ppermute | solution.py:442
  12.7 2.9 %collective-permute-start.3 = (f32[792,128]{1,0:T(8,128)S(1)}, f32[792,128]{1,0:T(8,128)S(1)}, u32[]{:S(2)}, u32[]{:S(2)}) collective-permute-start(f32[792,128]{1,0:T(8,128)S(1)} %shard_map.94.received_0__0_.lat_in_0__0_), channel_id=1, source_target_pairs={{0,1},{1,0},{2,3},{3,2},{4,5},{5,4},{6,7},{7,6},{8,9},{9,8},{10,11... | collective-permute-start | bytes 1216520 | tf_op jit(solution)/shard_map/ppermute | solution.py:415
  13.9 10.8 %collective-permute-start.5 = (f32[768,128]{1,0:T(8,128)S(1)}, f32[768,128]{1,0:T(8,128)S(1)}, u32[]{:S(2)}, u32[]{:S(2)}) collective-permute-start(f32[768,128]{1,0:T(8,128)S(1)} %get-tuple-element.37), channel_id=1, source_target_pairs={{0,2},{2,0},{1,3},{3,1},{4,6},{6,4},{5,7},{7,5},{8,10},{10,8},{9,1... | collective-permute-start | bytes 1179656 | tf_op jit(solution)/shard_map/ppermute | solution.py:442
  14.4 22.0 %collective-permute-start.4 = (f32[768,128]{1,0:T(8,128)S(1)}, f32[768,128]{1,0:T(8,128)S(1)}, u32[]{:S(2)}, u32[]{:S(2)}) collective-permute-start(f32[768,128]{1,0:T(8,128)S(1)} %get-tuple-element.34.after_0_), channel_id=1, source_target_pairs={{0,2},{2,0},{1,3},{3,1},{4,6},{6,4},{5,7},{7,5},{8,10},{10,8},{9,1... | collective-permute-start | bytes 1179656 | tf_op jit(solution)/shard_map/ppermute | solution.py:442
  23.1 7.8 %collective-permute-start.6 = (f32[2,2,48,128]{3,2,1,0:T(8,128)S(1)}, f32[2,2,48,128]{3,2,1,0:T(8,128)S(1)}, u32[]{:S(2)}, u32[]{:S(2)}) collective-permute-start(f32[2,2,48,128]{3,2,1,0:T(8,128)S(1)} %get-tuple-element.41), channel_id=1, source_target_pairs={{0,4},{4,8},{8,12},{12,0},{1,5},{5,9},{9,13},{13,1},{2,6},{6,10},{... | collective-permute-start | bytes 294920 | tf_op jit(solution)/shard_map/ppermute | solution.py:558
  24.4 6.5 %collective-permute-start.7 = (f32[2,2,48,128]{3,2,1,0:T(8,128)S(1)}, f32[2,2,48,128]{3,2,1,0:T(8,128)S(1)}, u32[]{:S(2)}, u32[]{:S(2)}) collective-permute-start(f32[2,2,48,128]{3,2,1,0:T(8,128)S(1)} %get-tuple-element.42), channel_id=1, source_target_pairs={{0,8},{4,12},{8,0},{12,4},{1,9},{5,13},{9,1},{13,5},{2,10},{6,14},... | collective-permute-start | bytes 294920 | tf_op jit(solution)/shard_map/ppermute | solution.py:558
  30.9 11.6 %collective-permute-start.10 = (f32[2,2,48,128]{3,2,1,0:T(8,128)S(1)}, f32[2,2,48,128]{3,2,1,0:T(8,128)S(1)}, u32[]{:S(2)}, u32[]{:S(2)}) collective-permute-start(f32[2,2,48,128]{3,2,1,0:T(8,128)S(1)} %get-tuple-element.47), channel_id=1, source_target_pairs={{0,4},{4,8},{8,12},{12,0},{1,5},{5,9},{9,13},{13,1},{2,6},{6,10},{... | collective-permute-start | bytes 294920 | tf_op jit(solution)/shard_map/ppermute | solution.py:558
  32.3 10.3 %collective-permute-start.11 = (f32[2,2,48,128]{3,2,1,0:T(8,128)S(1)}, f32[2,2,48,128]{3,2,1,0:T(8,128)S(1)}, u32[]{:S(2)}, u32[]{:S(2)}) collective-permute-start(f32[2,2,48,128]{3,2,1,0:T(8,128)S(1)} %get-tuple-element.48), channel_id=1, source_target_pairs={{0,8},{4,12},{8,0},{12,4},{1,9},{5,13},{9,1},{13,5},{2,10},{6,14},... | collective-permute-start | bytes 294920 | tf_op jit(solution)/shard_map/ppermute | solution.py:558
  34.0 16.3 %collective-permute-start.8 = (f32[2,2,48,128]{3,2,1,0:T(8,128)S(1)}, f32[2,2,48,128]{3,2,1,0:T(8,128)S(1)}, u32[]{:S(2)}, u32[]{:S(2)}) collective-permute-start(f32[2,2,48,128]{3,2,1,0:T(8,128)S(1)} %get-tuple-element.43), channel_id=1, source_target_pairs={{0,12},{4,0},{8,4},{12,8},{1,13},{5,1},{9,5},{13,9},{2,14},{6,2},{... | collective-permute-start | bytes 294920 | tf_op jit(solution)/shard_map/ppermute | solution.py:558
  42.5 10.5 %collective-permute-start.12 = (f32[2,2,48,128]{3,2,1,0:T(8,128)S(1)}, f32[2,2,48,128]{3,2,1,0:T(8,128)S(1)}, u32[]{:S(2)}, u32[]{:S(2)}) collective-permute-start(f32[2,2,48,128]{3,2,1,0:T(8,128)S(1)} %get-tuple-element.49), channel_id=1, source_target_pairs={{0,12},{4,0},{8,4},{12,8},{1,13},{5,1},{9,5},{13,9},{2,14},{6,2},{... | collective-permute-start | bytes 294920 | tf_op jit(solution)/shard_map/ppermute | solution.py:558
  42.6 10.8 %collective-permute-start.14 = (f32[2,2,48,128]{3,2,1,0:T(8,128)S(1)}, f32[2,2,48,128]{3,2,1,0:T(8,128)S(1)}, u32[]{:S(2)}, u32[]{:S(2)}) collective-permute-start(f32[2,2,48,128]{3,2,1,0:T(8,128)S(1)} %get-tuple-element.53), channel_id=1, source_target_pairs={{0,4},{4,8},{8,12},{12,0},{1,5},{5,9},{9,13},{13,1},{2,6},{6,10},{... | collective-permute-start | bytes 294920 | tf_op jit(solution)/shard_map/ppermute | solution.py:558
  44.4 9.0 %collective-permute-start.15 = (f32[2,2,48,128]{3,2,1,0:T(8,128)S(1)}, f32[2,2,48,128]{3,2,1,0:T(8,128)S(1)}, u32[]{:S(2)}, u32[]{:S(2)}) collective-permute-start(f32[2,2,48,128]{3,2,1,0:T(8,128)S(1)} %get-tuple-element.54), channel_id=1, source_target_pairs={{0,8},{4,12},{8,0},{12,4},{1,9},{5,13},{9,1},{13,5},{2,10},{6,14},... | collective-permute-start | bytes 294920 | tf_op jit(solution)/shard_map/ppermute | solution.py:558
  44.9 8.7 %collective-permute-start.16 = (f32[2,2,48,128]{3,2,1,0:T(8,128)S(1)}, f32[2,2,48,128]{3,2,1,0:T(8,128)S(1)}, u32[]{:S(2)}, u32[]{:S(2)}) collective-permute-start(f32[2,2,48,128]{3,2,1,0:T(8,128)S(1)} %get-tuple-element.55), channel_id=1, source_target_pairs={{0,12},{4,0},{8,4},{12,8},{1,13},{5,1},{9,5},{13,9},{2,14},{6,2},{... | collective-permute-start | bytes 294920 | tf_op jit(solution)/shard_map/ppermute | solution.py:558
  50.6 4.4 %collective-permute-start.9 = (f32[4,2,48,128]{3,2,1,0:T(8,128)S(1)}, f32[4,2,48,128]{3,2,1,0:T(8,128)S(1)}, u32[]{:S(2)}, u32[]{:S(2)}) collective-permute-start(f32[4,2,48,128]{3,2,1,0:T(8,128)S(1)} %shard_map.100), channel_id=1, source_target_pairs={{0,1},{1,0},{2,3},{3,2},{4,5},{5,4},{6,7},{7,6},{8,9},{9,8},{10,11... | collective-permute-start | bytes 589832 | tf_op jit(solution)/shard_map/ppermute | solution.py:588
  53.3 1.8 %collective-permute-start.13 = (f32[4,2,48,128]{3,2,1,0:T(8,128)S(1)}, f32[4,2,48,128]{3,2,1,0:T(8,128)S(1)}, u32[]{:S(2)}, u32[]{:S(2)}) collective-permute-start(f32[4,2,48,128]{3,2,1,0:T(8,128)S(1)} %shard_map.102), channel_id=1, source_target_pairs={{0,1},{1,0},{2,3},{3,2},{4,5},{5,4},{6,7},{7,6},{8,9},{9,8},{10,11... | collective-permute-start | bytes 589832 | tf_op jit(solution)/shard_map/ppermute | solution.py:588
  53.9 2.2 %collective-permute-start.17 = (f32[4,2,48,128]{3,2,1,0:T(8,128)S(1)}, f32[4,2,48,128]{3,2,1,0:T(8,128)S(1)}, u32[]{:S(2)}, u32[]{:S(2)}) collective-permute-start(f32[4,2,48,128]{3,2,1,0:T(8,128)S(1)} %shard_map.104), channel_id=1, source_target_pairs={{0,1},{1,0},{2,3},{3,2},{4,5},{5,4},{6,7},{7,6},{8,9},{9,8},{10,11... | collective-permute-start | bytes 589832 | tf_op jit(solution)/shard_map/ppermute | solution.py:588
  59.8 13.6 %collective-permute-start.18 = (f32[2,288,128]{2,1,0:T(8,128)S(1)}, f32[2,288,128]{2,1,0:T(8,128)S(1)}, u32[]{:S(2)}, u32[]{:S(2)}) collective-permute-start(f32[2,288,128]{2,1,0:T(8,128)S(1)} %shard_map.107), channel_id=1, source_target_pairs={{0,8},{4,12},{8,0},{12,4},{1,9},{5,13},{9,1},{13,5},{2,10},{6,14},... | collective-permute-start | bytes 884744 | tf_op jit(solution)/shard_map/ppermute | solution.py:622
  61.7 24.4 %collective-permute-start.19 = (f32[2,288,128]{2,1,0:T(8,128)S(1)}, f32[2,288,128]{2,1,0:T(8,128)S(1)}, u32[]{:S(2)}, u32[]{:S(2)}) collective-permute-start(f32[2,288,128]{2,1,0:T(8,128)S(1)} %shard_map.109), channel_id=1, source_target_pairs={{0,12},{4,0},{8,4},{12,8},{1,13},{5,1},{9,5},{13,9},{2,14},{6,2},{... | collective-permute-start | bytes 884744 | tf_op jit(solution)/shard_map/ppermute | solution.py:622
  64.1 24.6 %collective-permute-start.20 = (f32[2,288,128]{2,1,0:T(8,128)S(1)}, f32[2,288,128]{2,1,0:T(8,128)S(1)}, u32[]{:S(2)}, u32[]{:S(2)}) collective-permute-start(f32[2,288,128]{2,1,0:T(8,128)S(1)} %shard_map.110), channel_id=1, source_target_pairs={{0,4},{4,8},{8,12},{12,0},{1,5},{5,9},{9,13},{13,1},{2,6},{6,10},{... | collective-permute-start | bytes 884744 | tf_op jit(solution)/shard_map/ppermute | solution.py:622

commit v6 on v5

--- a/solution.py
+++ b/solution.py
@@ -98,7 +98,7 @@
             out[row, 1, copy * span : (copy + 1) * span, :] = north
         return 0
 
-    lax.fori_loop(0, window.size - 1, step, 0, unroll=4)
+    lax.fori_loop(0, window.size - 1, step, 0, unroll=True)
     out[window.size - 1] = jnp.zeros(out.shape[1:], jnp.bfloat16)
 
 

time: 90.6 us -> 90.2 us (level)
  no operation moved by 1% of the time
where the time goes in v6:
time: 90.2 us; the launch traced here: 90.1 us
  Pallas kernels  39.5 us (44%)
  waiting for transfers between devices  27.6 us (31%)
  starting transfers between devices  21.3 us (24%)
    ppermute x3, waiting for transfers between devices, local(): lax.ppermute(back[r], 'comp', [(a, (a - r) % n_comp) for a in range(n_com...  23.4 us
    pallas_call x3, Pallas kernels, local(): pl.pallas_call(functools.partial(propagate_kernel, window, n_lon, n_comp,...  18.5 us
    ppermute x9, starting transfers between devices, local(): moved[r] = lax.ppermute(sent[r - 1], 'comp', pairs)  9.98 us
    pallas_call x1, Pallas kernels, local(): pl.pallas_call(functools.partial(matrix_kernel, home_of), grid=(2, n_comp...  5.3 us
    pallas_call x1, Pallas kernels, local(): pl.pallas_call(functools.partial(transposed_kernel, home_of, half, half_o...  4.17 us
    ppermute x3, starting transfers between devices, local(): lax.ppermute(back[r], 'comp', [(a, (a - r) % n_comp) for a in range(n_com...  3.73 us
    ppermute x3, starting transfers between devices, local(): crossed.append(lax.ppermute(packed, 'lon', pairs))  3.61 us
    ppermute x3, waiting for transfers between devices, local(): lax.ppermute(block, 'lat', move)  2.82 us
  transfers between devices with their start and end apart: 21, of which 7 were waited for; matrix products, arithmetic and copies ran while one was open for 1% of the time, Pallas kernels for 38%

profile of v6, /device:TPU:19, one launch (start us, length us, event | category | flops | bytes accessed | tf_op | source)
XLA Modules:
  0.0 90.1 jit_solution(9846284593729647270)
XLA Ops:
  0.0 0.7 collective-permute-start.2
  0.8 1.1 %shard_map.91 = (f32[792,128]{1,0:T(8,128)S(1)}, f32[24,128]{1,0:T(8,128)S(1)}) custom-call(f32[2304,128]{1,0:T(8,128)} %bitcast.27, s32[8,128]{1,0:T(8,128)} %sea.1, s32[8,128]{1,0:T(8,128)} %depth.1, s32[8,128]{1,0:T(8,128)} %current.1), custom_call_target="tpu_custom_call" | custom-call | bytes 3500000 | tf_op jit(solution)/shard_map/pallas_call | solution.py:418
  1.9 0.2 collective-permute-start
  2.1 0.3 collective-permute-start.1
  2.4 0.1 fusion.16
  2.4 0.1 pad.9.clone
  2.5 0.1 pad.7.clone
  2.6 0.2 broadcast_multiply_fusion.1
  2.8 0.1 pad_maximum_fusion
  3.0 0.1 pad_maximum_fusion.1
  3.1 0.1 copy.25
  3.2 0.1 pad_add_fusion.place
  3.3 0.1 copy.23
  3.4 0.2 reshape_broadcast_in_dim.4.after_1_.coupling
  3.6 0.0 collective-permute-done.after_2_.own_1_
  3.6 0.0 collective-permute-done.2.own_in_1_
  3.6 1.6 %shard_map.92 = (f32[768,128]{1,0:T(8,128)S(1)}, f32[768,128]{1,0:T(8,128)S(1)}) custom-call(s32[3]{0:T(128)S(1)} %pad_add_fusion.place, f32[2304,128]{1,0:T(8,128)S(1)} %bitcast.28, f32[2304,128]{1,0:T(8,128)S(1)} %collective-permute-done.2.own_in_1_, f32[792,128]{1,0:T(8,128)S(1)} %get-tuple-element.33.after_0_, ...), custom_call_target="tpu_custom_call" | custom-call | bytes 5250000 | tf_op jit(solution)/shard_map/pallas_call | solution.py:433
  5.2 5.3 %shard_map.93.refs_1_.after.matrix = bf16[2,1152,1152]{2,1,0:T(8,128)(2,1)S(1)} custom-call(s32[3]{0:T(128)S(1)} %pad_add_fusion.place, f32[1,1152]{1,0:T(1,128)S(1)} %iota.18.names, f32[2,4,1152]{2,1,0:T(4,128)S(1)} %convert_bitcast_fusion.index, f32[2,4,1152]{2,1,0:T(4,128)S(1)} %maximum_bitcast_fusion.weight, f32[768,128]{1,0:T(8,128)S(1)} %get-tuple-element.34.after_0_, ...), custom_call_target="tpu_custom_call" | custom-call | bytes 21000000 | tf_op jit(solution)/shard_map/pallas_call | solution.py:463
  10.6 2.2 %collective-permute-done.1.refs_0_ = f32[792,128]{1,0:T(8,128)S(1)} collective-permute-done((f32[792,128]{1,0:T(8,128)S(1)}, f32[792,128]{1,0:T(8,128)S(1)}, u32[]{:S(2)}, u32[]{:S(2)}) %collective-permute-start.1) | collective-permute-done | bytes 405536 | tf_op jit(solution)/shard_map/ppermute | solution.py:442
  12.7 1.2 %collective-permute-start.3 = (f32[792,128]{1,0:T(8,128)S(1)}, f32[792,128]{1,0:T(8,128)S(1)}, u32[]{:S(2)}, u32[]{:S(2)}) collective-permute-start(f32[792,128]{1,0:T(8,128)S(1)} %shard_map.94.received_0__0_.lat_in_0__0_), channel_id=1, source_target_pairs={{0,1},{1,0},{2,3},{3,2},{4,5},{5,4},{6,7},{7,6},{8,9},{9,8},{10,11... | collective-permute-start | bytes 1216520 | tf_op jit(solution)/shard_map/ppermute | solution.py:415
  13.9 0.3 collective-permute-start.5
  14.2 0.1 maximum_maximum_fusion
  14.4 1.3 %collective-permute-start.4 = (f32[768,128]{1,0:T(8,128)S(1)}, f32[768,128]{1,0:T(8,128)S(1)}, u32[]{:S(2)}, u32[]{:S(2)}) collective-permute-start(f32[768,128]{1,0:T(8,128)S(1)} %get-tuple-element.34.after_0_), channel_id=1, source_target_pairs={{0,2},{2,0},{1,3},{3,1},{4,6},{6,4},{5,7},{7,5},{8,10},{10,8},{9,1... | collective-permute-start | bytes 1179656 | tf_op jit(solution)/shard_map/ppermute | solution.py:442
  15.6 0.0 collective-permute-done.3.received_0__1_.lat_in_0__1_
  15.6 0.8 shard_map.95
  16.5 6.2 %shard_map.96 = (f32[2,2,48,128]{3,2,1,0:T(8,128)S(1)}, f32[2,2,48,128]{3,2,1,0:T(8,128)S(1)}, f32[2,2,48,128]{3,2,1,0:T(8,128)S(1)}, f32[2,2,48,128]{3,2,1,0:T(8,128)S(1)}) custom-call(s32[3]{0:T(128)S(1)} %pad_add_fusion.place, bf16[2,48,96]{2,1,0:T(8,128)(2,1)S(1)} %get-tuple-element.59.tables, bf16[20,2,96,256]{3,2,1,0:T(8,128)(2,1)S(1)} %get-tuple-element.35.faces, ...), custom_call_target="tpu_custom_call" | custom-call | bytes 23730000 | tf_op jit(solution)/shard_map/pallas_call | solution.py:524
  22.7 1.4 %collective-permute-start.6 = (f32[2,2,48,128]{3,2,1,0:T(8,128)S(1)}, f32[2,2,48,128]{3,2,1,0:T(8,128)S(1)}, u32[]{:S(2)}, u32[]{:S(2)}) collective-permute-start(f32[2,2,48,128]{3,2,1,0:T(8,128)S(1)} %get-tuple-element.41), channel_id=1, source_target_pairs={{0,4},{4,8},{8,12},{12,0},{1,5},{5,9},{9,13},{13,1},{2,6},{6,10},{... | collective-permute-start | bytes 294920 | tf_op jit(solution)/shard_map/ppermute | solution.py:558
  24.0 0.0 collective-permute-start.7
  24.1 0.7 collective-permute-done.5.lat_in_0__0_
  24.7 6.2 %shard_map.97 = (f32[2,2,48,128]{3,2,1,0:T(8,128)S(1)}, f32[2,2,48,128]{3,2,1,0:T(8,128)S(1)}, f32[2,2,48,128]{3,2,1,0:T(8,128)S(1)}, f32[2,2,48,128]{3,2,1,0:T(8,128)S(1)}) custom-call(s32[3]{0:T(128)S(1)} %pad_add_fusion.place, bf16[2,48,96]{2,1,0:T(8,128)(2,1)S(1)} %get-tuple-element.60.tables, bf16[20,2,96,256]{3,2,1,0:T(8,128)(2,1)S(1)} %get-tuple-element.35.faces, ...), custom_call_target="tpu_custom_call" | custom-call | bytes 23730000 | tf_op jit(solution)/shard_map/pallas_call | solution.py:524
  30.9 0.0 collective-permute-done.6.pieces_1_.refs_4_.refs_1_
  30.9 0.0 collective-permute-done.7.pieces_2_.refs_3_.refs_2_
  30.9 1.3 %collective-permute-start.10 = (f32[2,2,48,128]{3,2,1,0:T(8,128)S(1)}, f32[2,2,48,128]{3,2,1,0:T(8,128)S(1)}, u32[]{:S(2)}, u32[]{:S(2)}) collective-permute-start(f32[2,2,48,128]{3,2,1,0:T(8,128)S(1)} %get-tuple-element.47), channel_id=1, source_target_pairs={{0,4},{4,8},{8,12},{12,0},{1,5},{5,9},{9,13},{13,1},{2,6},{6,10},{... | collective-permute-start | bytes 294920 | tf_op jit(solution)/shard_map/ppermute | solution.py:558
  32.3 1.3 %collective-permute-start.11 = (f32[2,2,48,128]{3,2,1,0:T(8,128)S(1)}, f32[2,2,48,128]{3,2,1,0:T(8,128)S(1)}, u32[]{:S(2)}, u32[]{:S(2)}) collective-permute-start(f32[2,2,48,128]{3,2,1,0:T(8,128)S(1)} %get-tuple-element.48), channel_id=1, source_target_pairs={{0,8},{4,12},{8,0},{12,4},{1,9},{5,13},{9,1},{13,5},{2,10},{6,14},... | collective-permute-start | bytes 294920 | tf_op jit(solution)/shard_map/ppermute | solution.py:558
  33.6 2.4 %collective-permute-start.8 = (f32[2,2,48,128]{3,2,1,0:T(8,128)S(1)}, f32[2,2,48,128]{3,2,1,0:T(8,128)S(1)}, u32[]{:S(2)}, u32[]{:S(2)}) collective-permute-start(f32[2,2,48,128]{3,2,1,0:T(8,128)S(1)} %get-tuple-element.43), channel_id=1, source_target_pairs={{0,12},{4,0},{8,4},{12,8},{1,13},{5,1},{9,5},{13,9},{2,14},{6,2},{... | collective-permute-start | bytes 294920 | tf_op jit(solution)/shard_map/ppermute | solution.py:558
  35.9 0.0 collective-permute-done.4.lat_in_0__0_
  35.9 6.2 %shard_map.98 = (f32[2,2,48,128]{3,2,1,0:T(8,128)S(1)}, f32[2,2,48,128]{3,2,1,0:T(8,128)S(1)}, f32[2,2,48,128]{3,2,1,0:T(8,128)S(1)}, f32[2,2,48,128]{3,2,1,0:T(8,128)S(1)}) custom-call(s32[3]{0:T(128)S(1)} %pad_add_fusion.place, bf16[2,48,96]{2,1,0:T(8,128)(2,1)S(1)} %get-tuple-element.61.tables, bf16[20,2,96,256]{3,2,1,0:T(8,128)(2,1)S(1)} %get-tuple-element.35.faces, ...), custom_call_target="tpu_custom_call" | custom-call | bytes 23730000 | tf_op jit(solution)/shard_map/pallas_call | solution.py:524
  42.1 0.1 collective-permute-start.12
  42.2 0.0 collective-permute-done.11.pieces_2_.refs_3_.refs_7_
  42.2 1.8 %collective-permute-start.14 = (f32[2,2,48,128]{3,2,1,0:T(8,128)S(1)}, f32[2,2,48,128]{3,2,1,0:T(8,128)S(1)}, u32[]{:S(2)}, u32[]{:S(2)}) collective-permute-start(f32[2,2,48,128]{3,2,1,0:T(8,128)S(1)} %get-tuple-element.53), channel_id=1, source_target_pairs={{0,4},{4,8},{8,12},{12,0},{1,5},{5,9},{9,13},{13,1},{2,6},{6,10},{... | collective-permute-start | bytes 294920 | tf_op jit(solution)/shard_map/ppermute | solution.py:558
  44.0 0.6 collective-permute-start.15
  44.5 1.2 %collective-permute-start.16 = (f32[2,2,48,128]{3,2,1,0:T(8,128)S(1)}, f32[2,2,48,128]{3,2,1,0:T(8,128)S(1)}, u32[]{:S(2)}, u32[]{:S(2)}) collective-permute-start(f32[2,2,48,128]{3,2,1,0:T(8,128)S(1)} %get-tuple-element.55), channel_id=1, source_target_pairs={{0,12},{4,0},{8,4},{12,8},{1,13},{5,1},{9,5},{13,9},{2,14},{6,2},{... | collective-permute-start | bytes 294920 | tf_op jit(solution)/shard_map/ppermute | solution.py:558
  45.7 4.2 %shard_map.99.after_0_.matrix_t = bf16[2,1152,1152]{2,1,0:T(8,128)(2,1)S(1)} custom-call(s32[3]{0:T(128)S(1)} %pad_add_fusion.place, f32[2,4,1152]{2,1,0:T(4,128)S(1)} %convert_bitcast_fusion.index, f32[2,4,1152]{2,1,0:T(4,128)S(1)} %maximum_bitcast_fusion.weight, f32[2,2,48,128]{3,2,1,0:T(8,128)S(1)} %get-tuple-element.40.after.pieces_0_.refs_10_), custom_call_target="tpu_custom_call" | custom-call | bytes 14000000 | tf_op jit(solution)/shard_map/pallas_call | solution.py:566
  49.9 0.3 shard_map.100
  50.2 2.4 %collective-permute-start.9 = (f32[4,2,48,128]{3,2,1,0:T(8,128)S(1)}, f32[4,2,48,128]{3,2,1,0:T(8,128)S(1)}, u32[]{:S(2)}, u32[]{:S(2)}) collective-permute-start(f32[4,2,48,128]{3,2,1,0:T(8,128)S(1)} %shard_map.100), channel_id=1, source_target_pairs={{0,1},{1,0},{2,3},{3,2},{4,5},{5,4},{6,7},{7,6},{8,9},{9,8},{10,11... | collective-permute-start | bytes 589832 | tf_op jit(solution)/shard_map/ppermute | solution.py:588
  52.6 0.3 shard_map.102
  52.9 0.1 collective-permute-start.13
  53.0 0.2 collective-permute-done.16.pieces_3_.refs_13_
  53.2 0.3 shard_map.104
  53.5 1.1 %collective-permute-start.17 = (f32[4,2,48,128]{3,2,1,0:T(8,128)S(1)}, f32[4,2,48,128]{3,2,1,0:T(8,128)S(1)}, u32[]{:S(2)}, u32[]{:S(2)}) collective-permute-start(f32[4,2,48,128]{3,2,1,0:T(8,128)S(1)} %shard_map.104), channel_id=1, source_target_pairs={{0,1},{1,0},{2,3},{3,2},{4,5},{5,4},{6,7},{7,6},{8,9},{9,8},{10,11... | collective-permute-start | bytes 589832 | tf_op jit(solution)/shard_map/ppermute | solution.py:588
  54.7 1.1 %collective-permute-done.17.refs_14_ = f32[4,2,48,128]{3,2,1,0:T(8,128)S(1)} collective-permute-done((f32[4,2,48,128]{3,2,1,0:T(8,128)S(1)}, f32[4,2,48,128]{3,2,1,0:T(8,128)S(1)}, u32[]{:S(2)}, u32[]{:S(2)}) %collective-permute-start.17) | collective-permute-done | bytes 196640 | tf_op jit(solution)/shard_map/ppermute | solution.py:588
  55.7 2.5 %shard_map.105 = (f32[1152,256]{1,0:T(8,128)S(1)}, f32[1152,256]{1,0:T(8,128)S(1)}, bf16[1152,256]{1,0:T(8,128)(2,1)S(1)}) custom-call(s32[3]{0:T(128)S(1)} %pad_add_fusion.place, bf16[2,1152,1152]{2,1,0:T(8,128)(2,1)S(1)} %shard_map.93.refs_1_.after.matrix, f32[1152,1]{1,0:T(8,128)S(1)} %reshape_broadcast_in_dim.4.after_1_.coupling, ...), custom_call_target="tpu_custom_call" | custom-call | bytes 14000000 | tf_op jit(solution)/shard_map/pallas_call | solution.py:592
  58.3 0.6 shard_map.110
  58.8 0.6 shard_map.107
  59.4 1.3 %collective-permute-start.18 = (f32[2,288,128]{2,1,0:T(8,128)S(1)}, f32[2,288,128]{2,1,0:T(8,128)S(1)}, u32[]{:S(2)}, u32[]{:S(2)}) collective-permute-start(f32[2,288,128]{2,1,0:T(8,128)S(1)} %shard_map.107), channel_id=1, source_target_pairs={{0,8},{4,12},{8,0},{12,4},{1,9},{5,13},{9,1},{13,5},{2,10},{6,14},... | collective-permute-start | bytes 884744 | tf_op jit(solution)/shard_map/ppermute | solution.py:622
  60.7 0.6 shard_map.109
  61.3 2.5 %collective-permute-start.19 = (f32[2,288,128]{2,1,0:T(8,128)S(1)}, f32[2,288,128]{2,1,0:T(8,128)S(1)}, u32[]{:S(2)}, u32[]{:S(2)}) collective-permute-start(f32[2,288,128]{2,1,0:T(8,128)S(1)} %shard_map.109), channel_id=1, source_target_pairs={{0,12},{4,0},{8,4},{12,8},{1,13},{5,1},{9,5},{13,9},{2,14},{6,2},{... | collective-permute-start | bytes 884744 | tf_op jit(solution)/shard_map/ppermute | solution.py:622
  63.7 0.0 collective-permute-start.20
  63.7 0.6 shard_map.106.refs_0_
  64.3 8.8 %collective-permute-done.18.refs_1_ = f32[2,288,128]{2,1,0:T(8,128)S(1)} collective-permute-done((f32[2,288,128]{2,1,0:T(8,128)S(1)}, f32[2,288,128]{2,1,0:T(8,128)S(1)}, u32[]{:S(2)}, u32[]{:S(2)}) %collective-permute-start.18) | collective-permute-done | bytes 294944 | tf_op jit(solution)/shard_map/ppermute | solution.py:622
  73.1 0.6 shard_map.108.held_0_
  73.7 12.0 %collective-permute-done.19.refs_0_ = f32[2,288,128]{2,1,0:T(8,128)S(1)} collective-permute-done((f32[2,288,128]{2,1,0:T(8,128)S(1)}, f32[2,288,128]{2,1,0:T(8,128)S(1)}, u32[]{:S(2)}, u32[]{:S(2)}) %collective-permute-start.19) | collective-permute-done | bytes 294944 | tf_op jit(solution)/shard_map/ppermute | solution.py:622
  85.7 2.6 %collective-permute-done.20.refs_1_ = f32[2,288,128]{2,1,0:T(8,128)S(1)} collective-permute-done((f32[2,288,128]{2,1,0:T(8,128)S(1)}, f32[2,288,128]{2,1,0:T(8,128)S(1)}, u32[]{:S(2)}, u32[]{:S(2)}) %collective-permute-start.20) | collective-permute-done | bytes 294944 | tf_op jit(solution)/shard_map/ppermute | solution.py:622
  88.3 1.7 %shard_map.111 = f32[2304,128]{1,0:T(8,128)} custom-call(s32[3]{0:T(128)S(1)} %pad_add_fusion.place, f32[2304,128]{1,0:T(8,128)S(1)} %shard_map.108.held_0_, f32[2,288,128]{2,1,0:T(8,128)S(1)} %collective-permute-done.19.refs_0_, f32[2,288,128]{2,1,0:T(8,128)S(1)} %collective-permute-done.20.refs_1_), custom_call_target="tpu_custom_call" | custom-call | bytes 3500000 | tf_op jit(solution)/shard_map/pallas_call | solution.py:627
  (30 shorter events, 0.2 us)
Async XLA Ops:
  0.0 2.6 %copy-start = (f32[16,32]{1,0:T(8,128)S(1)}, f32[16,32]{1,0:T(8,128)}, u32[]{:S(2)}) copy-start(f32[16,32]{1,0:T(8,128)} %param.13) | copy-start | bytes 6148
  0.0 2.4 %copy-start.5 = (f32[16,2]{0,1:T(2,128)S(1)}, f32[16,2]{0,1:T(2,128)}, u32[]{:S(2)}) copy-start(f32[16,2]{0,1:T(2,128)} %param.14) | copy-start | bytes 388
  0.0 2.6 %copy-start.2 = (s32[2,1152,4]{1,2,0:T(4,128)S(1)}, s32[2,1152,4]{1,2,0:T(4,128)}, u32[]{:S(2)}) copy-start(s32[2,1152,4]{1,2,0:T(4,128)} %param.16) | copy-start | bytes 110596
  0.0 2.9 %copy-start.3 = (f32[2,1152,4]{1,2,0:T(4,128)S(1)}, f32[2,1152,4]{1,2,0:T(4,128)}, u32[]{:S(2)}) copy-start(f32[2,1152,4]{1,2,0:T(4,128)} %param.17) | copy-start | bytes 110596
  0.0 3.3 %copy-start.4 = (f32[1152]{0:T(1024)S(1)}, f32[1152]{0:T(1024)}, u32[]{:S(2)}) copy-start(f32[1152]{0:T(1024)} %param.15) | copy-start | bytes 13828
  0.0 3.6 %copy-start.1 = (f32[288,8,128]{2,1,0:T(8,128)S(1)}, f32[288,8,128]{2,1,0:T(8,128)}, u32[]{:S(2)}) copy-start(f32[288,8,128]{2,1,0:T(8,128)} %param.9) | copy-start | bytes 3538948
  0.0 3.6 %collective-permute-start.2 = (f32[2304,128]{1,0:T(8,128)}, f32[2304,128]{1,0:T(8,128)S(1)}, u32[]{:S(2)}, u32[]{:S(2)}) collective-permute-start(f32[2304,128]{1,0:T(8,128)} %bitcast.26), channel_id=1, source_target_pairs={{0,1},{1,0},{2,3},{3,2},{4,5},{5,4},{6,7},{7,6},{8,9},{9,8},{10,11... | collective-permute-start | bytes 3538952 | tf_op jit(solution)/shard_map/ppermute | solution.py:415
  1.9 1.7 %collective-permute-start = (f32[24,128]{1,0:T(8,128)S(1)}, f32[24,128]{1,0:T(8,128)S(1)}, u32[]{:S(2)}, u32[]{:S(2)}) collective-permute-start(f32[24,128]{1,0:T(8,128)S(1)} %get-tuple-element.32.after_1_.own_0_), channel_id=1, source_target_pairs={{0,1},{1,0},{2,3},{3,2},{4,5},{5,4},{6,7},{7,6},{8,9},{9,8},{10,11... | collective-permute-start | bytes 36872 | tf_op jit(solution)/shard_map/ppermute | solution.py:415
  2.1 10.6 %collective-permute-start.1 = (f32[792,128]{1,0:T(8,128)S(1)}, f32[792,128]{1,0:T(8,128)S(1)}, u32[]{:S(2)}, u32[]{:S(2)}) collective-permute-start(f32[792,128]{1,0:T(8,128)S(1)} %get-tuple-element.33.after_0_), channel_id=1, source_target_pairs={{0,2},{2,0},{1,3},{3,1},{4,6},{6,4},{5,7},{7,5},{8,10},{10,8},{9,1... | collective-permute-start | bytes 1216520 | tf_op jit(solution)/shard_map/ppermute | solution.py:442
  12.7 2.9 %collective-permute-start.3 = (f32[792,128]{1,0:T(8,128)S(1)}, f32[792,128]{1,0:T(8,128)S(1)}, u32[]{:S(2)}, u32[]{:S(2)}) collective-permute-start(f32[792,128]{1,0:T(8,128)S(1)} %shard_map.94.received_0__0_.lat_in_0__0_), channel_id=1, source_target_pairs={{0,1},{1,0},{2,3},{3,2},{4,5},{5,4},{6,7},{7,6},{8,9},{9,8},{10,11... | collective-permute-start | bytes 1216520 | tf_op jit(solution)/shard_map/ppermute | solution.py:415
  13.9 10.8 %collective-permute-start.5 = (f32[768,128]{1,0:T(8,128)S(1)}, f32[768,128]{1,0:T(8,128)S(1)}, u32[]{:S(2)}, u32[]{:S(2)}) collective-permute-start(f32[768,128]{1,0:T(8,128)S(1)} %get-tuple-element.37), channel_id=1, source_target_pairs={{0,2},{2,0},{1,3},{3,1},{4,6},{6,4},{5,7},{7,5},{8,10},{10,8},{9,1... | collective-permute-start | bytes 1179656 | tf_op jit(solution)/shard_map/ppermute | solution.py:442
  14.4 21.6 %collective-permute-start.4 = (f32[768,128]{1,0:T(8,128)S(1)}, f32[768,128]{1,0:T(8,128)S(1)}, u32[]{:S(2)}, u32[]{:S(2)}) collective-permute-start(f32[768,128]{1,0:T(8,128)S(1)} %get-tuple-element.34.after_0_), channel_id=1, source_target_pairs={{0,2},{2,0},{1,3},{3,1},{4,6},{6,4},{5,7},{7,5},{8,10},{10,8},{9,1... | collective-permute-start | bytes 1179656 | tf_op jit(solution)/shard_map/ppermute | solution.py:442
  22.7 8.2 %collective-permute-start.6 = (f32[2,2,48,128]{3,2,1,0:T(8,128)S(1)}, f32[2,2,48,128]{3,2,1,0:T(8,128)S(1)}, u32[]{:S(2)}, u32[]{:S(2)}) collective-permute-start(f32[2,2,48,128]{3,2,1,0:T(8,128)S(1)} %get-tuple-element.41), channel_id=1, source_target_pairs={{0,4},{4,8},{8,12},{12,0},{1,5},{5,9},{9,13},{13,1},{2,6},{6,10},{... | collective-permute-start | bytes 294920 | tf_op jit(solution)/shard_map/ppermute | solution.py:558
  24.0 6.9 %collective-permute-start.7 = (f32[2,2,48,128]{3,2,1,0:T(8,128)S(1)}, f32[2,2,48,128]{3,2,1,0:T(8,128)S(1)}, u32[]{:S(2)}, u32[]{:S(2)}) collective-permute-start(f32[2,2,48,128]{3,2,1,0:T(8,128)S(1)} %get-tuple-element.42), channel_id=1, source_target_pairs={{0,8},{4,12},{8,0},{12,4},{1,9},{5,13},{9,1},{13,5},{2,10},{6,14},... | collective-permute-start | bytes 294920 | tf_op jit(solution)/shard_map/ppermute | solution.py:558
  30.9 11.2 %collective-permute-start.10 = (f32[2,2,48,128]{3,2,1,0:T(8,128)S(1)}, f32[2,2,48,128]{3,2,1,0:T(8,128)S(1)}, u32[]{:S(2)}, u32[]{:S(2)}) collective-permute-start(f32[2,2,48,128]{3,2,1,0:T(8,128)S(1)} %get-tuple-element.47), channel_id=1, source_target_pairs={{0,4},{4,8},{8,12},{12,0},{1,5},{5,9},{9,13},{13,1},{2,6},{6,10},{... | collective-permute-start | bytes 294920 | tf_op jit(solution)/shard_map/ppermute | solution.py:558
  32.3 9.9 %collective-permute-start.11 = (f32[2,2,48,128]{3,2,1,0:T(8,128)S(1)}, f32[2,2,48,128]{3,2,1,0:T(8,128)S(1)}, u32[]{:S(2)}, u32[]{:S(2)}) collective-permute-start(f32[2,2,48,128]{3,2,1,0:T(8,128)S(1)} %get-tuple-element.48), channel_id=1, source_target_pairs={{0,8},{4,12},{8,0},{12,4},{1,9},{5,13},{9,1},{13,5},{2,10},{6,14},... | collective-permute-start | bytes 294920 | tf_op jit(solution)/shard_map/ppermute | solution.py:558
  33.6 16.3 %collective-permute-start.8 = (f32[2,2,48,128]{3,2,1,0:T(8,128)S(1)}, f32[2,2,48,128]{3,2,1,0:T(8,128)S(1)}, u32[]{:S(2)}, u32[]{:S(2)}) collective-permute-start(f32[2,2,48,128]{3,2,1,0:T(8,128)S(1)} %get-tuple-element.43), channel_id=1, source_target_pairs={{0,12},{4,0},{8,4},{12,8},{1,13},{5,1},{9,5},{13,9},{2,14},{6,2},{... | collective-permute-start | bytes 294920 | tf_op jit(solution)/shard_map/ppermute | solution.py:558
  42.1 10.5 %collective-permute-start.12 = (f32[2,2,48,128]{3,2,1,0:T(8,128)S(1)}, f32[2,2,48,128]{3,2,1,0:T(8,128)S(1)}, u32[]{:S(2)}, u32[]{:S(2)}) collective-permute-start(f32[2,2,48,128]{3,2,1,0:T(8,128)S(1)} %get-tuple-element.49), channel_id=1, source_target_pairs={{0,12},{4,0},{8,4},{12,8},{1,13},{5,1},{9,5},{13,9},{2,14},{6,2},{... | collective-permute-start | bytes 294920 | tf_op jit(solution)/shard_map/ppermute | solution.py:558
  42.2 10.8 %collective-permute-start.14 = (f32[2,2,48,128]{3,2,1,0:T(8,128)S(1)}, f32[2,2,48,128]{3,2,1,0:T(8,128)S(1)}, u32[]{:S(2)}, u32[]{:S(2)}) collective-permute-start(f32[2,2,48,128]{3,2,1,0:T(8,128)S(1)} %get-tuple-element.53), channel_id=1, source_target_pairs={{0,4},{4,8},{8,12},{12,0},{1,5},{5,9},{9,13},{13,1},{2,6},{6,10},{... | collective-permute-start | bytes 294920 | tf_op jit(solution)/shard_map/ppermute | solution.py:558
  44.0 9.0 %collective-permute-start.15 = (f32[2,2,48,128]{3,2,1,0:T(8,128)S(1)}, f32[2,2,48,128]{3,2,1,0:T(8,128)S(1)}, u32[]{:S(2)}, u32[]{:S(2)}) collective-permute-start(f32[2,2,48,128]{3,2,1,0:T(8,128)S(1)} %get-tuple-element.54), channel_id=1, source_target_pairs={{0,8},{4,12},{8,0},{12,4},{1,9},{5,13},{9,1},{13,5},{2,10},{6,14},... | collective-permute-start | bytes 294920 | tf_op jit(solution)/shard_map/ppermute | solution.py:558
  44.5 8.7 %collective-permute-start.16 = (f32[2,2,48,128]{3,2,1,0:T(8,128)S(1)}, f32[2,2,48,128]{3,2,1,0:T(8,128)S(1)}, u32[]{:S(2)}, u32[]{:S(2)}) collective-permute-start(f32[2,2,48,128]{3,2,1,0:T(8,128)S(1)} %get-tuple-element.55), channel_id=1, source_target_pairs={{0,12},{4,0},{8,4},{12,8},{1,13},{5,1},{9,5},{13,9},{2,14},{6,2},{... | collective-permute-start | bytes 294920 | tf_op jit(solution)/shard_map/ppermute | solution.py:558
  50.2 4.4 %collective-permute-start.9 = (f32[4,2,48,128]{3,2,1,0:T(8,128)S(1)}, f32[4,2,48,128]{3,2,1,0:T(8,128)S(1)}, u32[]{:S(2)}, u32[]{:S(2)}) collective-permute-start(f32[4,2,48,128]{3,2,1,0:T(8,128)S(1)} %shard_map.100), channel_id=1, source_target_pairs={{0,1},{1,0},{2,3},{3,2},{4,5},{5,4},{6,7},{7,6},{8,9},{9,8},{10,11... | collective-permute-start | bytes 589832 | tf_op jit(solution)/shard_map/ppermute | solution.py:588
  52.9 1.8 %collective-permute-start.13 = (f32[4,2,48,128]{3,2,1,0:T(8,128)S(1)}, f32[4,2,48,128]{3,2,1,0:T(8,128)S(1)}, u32[]{:S(2)}, u32[]{:S(2)}) collective-permute-start(f32[4,2,48,128]{3,2,1,0:T(8,128)S(1)} %shard_map.102), channel_id=1, source_target_pairs={{0,1},{1,0},{2,3},{3,2},{4,5},{5,4},{6,7},{7,6},{8,9},{9,8},{10,11... | collective-permute-start | bytes 589832 | tf_op jit(solution)/shard_map/ppermute | solution.py:588
  53.5 2.2 %collective-permute-start.17 = (f32[4,2,48,128]{3,2,1,0:T(8,128)S(1)}, f32[4,2,48,128]{3,2,1,0:T(8,128)S(1)}, u32[]{:S(2)}, u32[]{:S(2)}) collective-permute-start(f32[4,2,48,128]{3,2,1,0:T(8,128)S(1)} %shard_map.104), channel_id=1, source_target_pairs={{0,1},{1,0},{2,3},{3,2},{4,5},{5,4},{6,7},{7,6},{8,9},{9,8},{10,11... | collective-permute-start | bytes 589832 | tf_op jit(solution)/shard_map/ppermute | solution.py:588
  59.4 13.6 %collective-permute-start.18 = (f32[2,288,128]{2,1,0:T(8,128)S(1)}, f32[2,288,128]{2,1,0:T(8,128)S(1)}, u32[]{:S(2)}, u32[]{:S(2)}) collective-permute-start(f32[2,288,128]{2,1,0:T(8,128)S(1)} %shard_map.107), channel_id=1, source_target_pairs={{0,8},{4,12},{8,0},{12,4},{1,9},{5,13},{9,1},{13,5},{2,10},{6,14},... | collective-permute-start | bytes 884744 | tf_op jit(solution)/shard_map/ppermute | solution.py:622
  61.3 24.4 %collective-permute-start.19 = (f32[2,288,128]{2,1,0:T(8,128)S(1)}, f32[2,288,128]{2,1,0:T(8,128)S(1)}, u32[]{:S(2)}, u32[]{:S(2)}) collective-permute-start(f32[2,288,128]{2,1,0:T(8,128)S(1)} %shard_map.109), channel_id=1, source_target_pairs={{0,12},{4,0},{8,4},{12,8},{1,13},{5,1},{9,5},{13,9},{2,14},{6,2},{... | collective-permute-start | bytes 884744 | tf_op jit(solution)/shard_map/ppermute | solution.py:622
  63.7 24.6 %collective-permute-start.20 = (f32[2,288,128]{2,1,0:T(8,128)S(1)}, f32[2,288,128]{2,1,0:T(8,128)S(1)}, u32[]{:S(2)}, u32[]{:S(2)}) collective-permute-start(f32[2,288,128]{2,1,0:T(8,128)S(1)} %shard_map.110), channel_id=1, source_target_pairs={{0,4},{4,8},{8,12},{12,0},{1,5},{5,9},{9,13},{13,1},{2,6},{6,10},{... | collective-permute-start | bytes 884744 | tf_op jit(solution)/shard_map/ppermute | solution.py:622

commit v7 on v6

--- a/solution.py
+++ b/solution.py
@@ -176,26 +176,18 @@
     width = n_lon * lanes
     energy = pltpu.VMEM((window.size, GROUP, width), jnp.float32)
     speed = pltpu.VMEM((window.size, size, width), jnp.float32)
-    block = pltpu.VMEM((size * window.rows, lanes), jnp.float32)
-    return [energy, energy, speed, speed, speed, speed] + [block] * n_lon + [pltpu.SemaphoreType.DMA((n_lon,))]
+    return [energy, energy, speed, speed, speed, speed]
 
 
 def propagate_kernel(
     window, n_lon, n_comp, split, start, half, head, place, tables, faces, wet, own_in, lat_in, after, *refs
 ):
-    outs, scratch = refs[: -7 - n_lon], refs[-7 - n_lon :]
-    energy, other, east_u, east_c, north_u, north_c = scratch[:6]
-    own_blocks, sems = scratch[6:-1], scratch[-1]
+    outs = refs[:-6]
+    energy, other, east_u, east_c, north_u, north_c = refs[-6:]
     lat, comp, lon = place[0], place[1], place[2]
     rows, lanes = window.rows, wet.shape[2] // n_lon
     width = n_lon * lanes
     count = east_u.shape[1]
-    copies = []
-    for d in range(n_lon):
-        first = pl.multiple_of((lon * half + start) * rows, 8)
-        copies.append(pltpu.make_async_copy(own_in[d].at[pl.ds(first, count * rows)], own_blocks[d], sems.at[d]))
-        copies[-1].start()
-
     def speeds(row, _):
         for which, u_ref, c_ref in ((0, east_u, east_c), (1, north_u, north_c)):
             u = jnp.dot(tables[which], faces[row, which], preferred_element_type=jnp.float32)
@@ -206,8 +198,6 @@
 
     lax.fori_loop(0, window.size, speeds, 0, unroll=True)
 
-    for copy in copies:
-        copy.wait()
     own = window.own(lat)
 
     def group(g, _):
@@ -216,7 +206,7 @@
         for row in window.zeros(lat):
             energy[row] = jnp.zeros((GROUP, width), jnp.float32)
             other[row] = jnp.zeros((GROUP, width), jnp.float32)
-        sources = [(own, [(ref, 0) for ref in own_blocks])]
+        sources = [(own, [(ref, lon * half + start) for ref in own_in])]
         for offset, blocks in zip(window.received(lat), lat_in):
             if head:
                 sources.append((offset, [(ref, head + lon * count) for ref in blocks]))
@@ -531,7 +521,7 @@
                 whole,
                 whole,
                 whole,
-                [anywhere] * n_lon,
+                [whole] * n_lon,
                 [[whole] * len(found) for found in lat_in[i]],
                 anywhere,
             ],

time: 90.2 us -> 89.1 us (0.988)
  Pallas kernels: 39.5 us -> 37.9 us
    pallas_call x3, Pallas kernels: 18.5 us -> 16.9 us  [local(): pl.pallas_call(functools.partial(propagate_kernel, window, n_lon, n_comp,...]
  transfers between devices with their start and end apart: 21 -> 21, of which waited for: 7 -> 7; matrix products, arithmetic and copies ran while one was open for 1% -> 1% of each run, Pallas kernels for 38% -> 37%
where the time goes in v7:
time: 89.1 us; the launch traced here: 89 us
  Pallas kernels  37.9 us (43%)
  waiting for transfers between devices  27.9 us (31%)
  starting transfers between devices  21.5 us (24%)
    ppermute x3, waiting for transfers between devices, local(): lax.ppermute(back[r], 'comp', [(a, (a - r) % n_comp) for a in range(n_com...  23.4 us
    pallas_call x3, Pallas kernels, local(): pl.pallas_call(functools.partial(propagate_kernel, window, n_lon, n_comp,...  16.9 us
    ppermute x9, starting transfers between devices, local(): moved[r] = lax.ppermute(sent[r - 1], 'comp', pairs)  9.99 us
    pallas_call x1, Pallas kernels, local(): pl.pallas_call(functools.partial(matrix_kernel, home_of), grid=(2, n_comp...  5.3 us
    pallas_call x1, Pallas kernels, local(): pl.pallas_call(functools.partial(transposed_kernel, home_of, half, half_o...  4.17 us
    ppermute x3, starting transfers between devices, local(): crossed.append(lax.ppermute(packed, 'lon', pairs))  3.81 us
    ppermute x3, starting transfers between devices, local(): lax.ppermute(back[r], 'comp', [(a, (a - r) % n_comp) for a in range(n_com...  3.72 us
    ppermute x3, waiting for transfers between devices, local(): lax.ppermute(block, 'lat', move)  3.35 us
  transfers between devices with their start and end apart: 21, of which 7 were waited for; matrix products, arithmetic and copies ran while one was open for 1% of the time, Pallas kernels for 37%

profile of v7, /device:TPU:19, one launch (start us, length us, event | category | flops | bytes accessed | tf_op | source)
XLA Modules:
  0.0 89.0 jit_solution(9782938219725298165)
XLA Ops:
  0.0 0.7 collective-permute-start.2
  0.8 1.1 %shard_map.91 = (f32[792,128]{1,0:T(8,128)S(1)}, f32[24,128]{1,0:T(8,128)S(1)}) custom-call(f32[2304,128]{1,0:T(8,128)} %bitcast.27, s32[8,128]{1,0:T(8,128)} %sea.1, s32[8,128]{1,0:T(8,128)} %depth.1, s32[8,128]{1,0:T(8,128)} %current.1), custom_call_target="tpu_custom_call" | custom-call | bytes 3500000 | tf_op jit(solution)/shard_map/pallas_call | solution.py:408
  1.9 0.2 collective-permute-start
  2.1 0.3 collective-permute-start.1
  2.4 0.1 fusion.16
  2.4 0.1 pad.9.clone
  2.5 0.1 pad.7.clone
  2.6 0.2 broadcast_multiply_fusion.1
  2.8 0.1 pad_maximum_fusion
  3.0 0.1 pad_maximum_fusion.1
  3.1 0.1 copy.25
  3.2 0.1 pad_add_fusion.place
  3.3 0.1 copy.23
  3.4 0.2 reshape_broadcast_in_dim.4.after_1_.coupling
  3.6 0.0 collective-permute-done.after_2_.own_1_
  3.6 0.0 collective-permute-done.2.own_in_1_
  3.6 1.6 %shard_map.92 = (f32[768,128]{1,0:T(8,128)S(1)}, f32[768,128]{1,0:T(8,128)S(1)}) custom-call(s32[3]{0:T(128)S(1)} %pad_add_fusion.place, f32[2304,128]{1,0:T(8,128)S(1)} %bitcast.28, f32[2304,128]{1,0:T(8,128)S(1)} %collective-permute-done.2.own_in_1_, f32[792,128]{1,0:T(8,128)S(1)} %get-tuple-element.33.after_0_, ...), custom_call_target="tpu_custom_call" | custom-call | bytes 5250000 | tf_op jit(solution)/shard_map/pallas_call | solution.py:423
  5.2 5.3 %shard_map.93.refs_1_.after.matrix = bf16[2,1152,1152]{2,1,0:T(8,128)(2,1)S(1)} custom-call(s32[3]{0:T(128)S(1)} %pad_add_fusion.place, f32[1,1152]{1,0:T(1,128)S(1)} %iota.18.names, f32[2,4,1152]{2,1,0:T(4,128)S(1)} %convert_bitcast_fusion.index, f32[2,4,1152]{2,1,0:T(4,128)S(1)} %maximum_bitcast_fusion.weight, f32[768,128]{1,0:T(8,128)S(1)} %get-tuple-element.34.after_0_, ...), custom_call_target="tpu_custom_call" | custom-call | bytes 21000000 | tf_op jit(solution)/shard_map/pallas_call | solution.py:453
  10.6 2.2 %collective-permute-done.1.refs_0_ = f32[792,128]{1,0:T(8,128)S(1)} collective-permute-done((f32[792,128]{1,0:T(8,128)S(1)}, f32[792,128]{1,0:T(8,128)S(1)}, u32[]{:S(2)}, u32[]{:S(2)}) %collective-permute-start.1) | collective-permute-done | bytes 405536 | tf_op jit(solution)/shard_map/ppermute | solution.py:432
  12.7 1.2 %collective-permute-start.3 = (f32[792,128]{1,0:T(8,128)S(1)}, f32[792,128]{1,0:T(8,128)S(1)}, u32[]{:S(2)}, u32[]{:S(2)}) collective-permute-start(f32[792,128]{1,0:T(8,128)S(1)} %shard_map.94.received_0__0_.lat_in_0__0_), channel_id=1, source_target_pairs={{0,1},{1,0},{2,3},{3,2},{4,5},{5,4},{6,7},{7,6},{8,9},{9,8},{10,11... | collective-permute-start | bytes 1216520 | tf_op jit(solution)/shard_map/ppermute | solution.py:405
  13.9 0.3 collective-permute-start.5
  14.2 0.1 maximum_maximum_fusion
  14.4 1.3 %collective-permute-start.4 = (f32[768,128]{1,0:T(8,128)S(1)}, f32[768,128]{1,0:T(8,128)S(1)}, u32[]{:S(2)}, u32[]{:S(2)}) collective-permute-start(f32[768,128]{1,0:T(8,128)S(1)} %get-tuple-element.34.after_0_), channel_id=1, source_target_pairs={{0,2},{2,0},{1,3},{3,1},{4,6},{6,4},{5,7},{7,5},{8,10},{10,8},{9,1... | collective-permute-start | bytes 1179656 | tf_op jit(solution)/shard_map/ppermute | solution.py:432
  15.6 0.0 collective-permute-done.3.received_0__1_.lat_in_0__1_
  15.6 0.8 shard_map.95
  16.5 5.6 %shard_map.96 = (f32[2,2,48,128]{3,2,1,0:T(8,128)S(1)}, f32[2,2,48,128]{3,2,1,0:T(8,128)S(1)}, f32[2,2,48,128]{3,2,1,0:T(8,128)S(1)}, f32[2,2,48,128]{3,2,1,0:T(8,128)S(1)}) custom-call(s32[3]{0:T(128)S(1)} %pad_add_fusion.place, bf16[2,48,96]{2,1,0:T(8,128)(2,1)S(1)} %get-tuple-element.59.tables, bf16[20,2,96,256]{3,2,1,0:T(8,128)(2,1)S(1)} %get-tuple-element.35.faces, ...), custom_call_target="tpu_custom_call" | custom-call | bytes 23730000 | tf_op jit(solution)/shard_map/pallas_call | solution.py:514
  22.1 1.4 %collective-permute-start.6 = (f32[2,2,48,128]{3,2,1,0:T(8,128)S(1)}, f32[2,2,48,128]{3,2,1,0:T(8,128)S(1)}, u32[]{:S(2)}, u32[]{:S(2)}) collective-permute-start(f32[2,2,48,128]{3,2,1,0:T(8,128)S(1)} %get-tuple-element.41), channel_id=1, source_target_pairs={{0,4},{4,8},{8,12},{12,0},{1,5},{5,9},{9,13},{13,1},{2,6},{6,10},{... | collective-permute-start | bytes 294920 | tf_op jit(solution)/shard_map/ppermute | solution.py:548
  23.5 0.0 collective-permute-start.7
  23.5 1.2 %collective-permute-done.5.lat_in_0__0_ = f32[768,128]{1,0:T(8,128)S(1)} collective-permute-done((f32[768,128]{1,0:T(8,128)S(1)}, f32[768,128]{1,0:T(8,128)S(1)}, u32[]{:S(2)}, u32[]{:S(2)}) %collective-permute-start.5) | collective-permute-done | bytes 393248 | tf_op jit(solution)/shard_map/ppermute | solution.py:432
  24.7 5.6 %shard_map.97 = (f32[2,2,48,128]{3,2,1,0:T(8,128)S(1)}, f32[2,2,48,128]{3,2,1,0:T(8,128)S(1)}, f32[2,2,48,128]{3,2,1,0:T(8,128)S(1)}, f32[2,2,48,128]{3,2,1,0:T(8,128)S(1)}) custom-call(s32[3]{0:T(128)S(1)} %pad_add_fusion.place, bf16[2,48,96]{2,1,0:T(8,128)(2,1)S(1)} %get-tuple-element.60.tables, bf16[20,2,96,256]{3,2,1,0:T(8,128)(2,1)S(1)} %get-tuple-element.35.faces, ...), custom_call_target="tpu_custom_call" | custom-call | bytes 23730000 | tf_op jit(solution)/shard_map/pallas_call | solution.py:514
  30.4 0.0 collective-permute-done.7.pieces_2_.refs_3_.refs_2_
  30.4 1.4 %collective-permute-start.10 = (f32[2,2,48,128]{3,2,1,0:T(8,128)S(1)}, f32[2,2,48,128]{3,2,1,0:T(8,128)S(1)}, u32[]{:S(2)}, u32[]{:S(2)}) collective-permute-start(f32[2,2,48,128]{3,2,1,0:T(8,128)S(1)} %get-tuple-element.47), channel_id=1, source_target_pairs={{0,4},{4,8},{8,12},{12,0},{1,5},{5,9},{9,13},{13,1},{2,6},{6,10},{... | collective-permute-start | bytes 294920 | tf_op jit(solution)/shard_map/ppermute | solution.py:548
  31.8 1.3 %collective-permute-start.11 = (f32[2,2,48,128]{3,2,1,0:T(8,128)S(1)}, f32[2,2,48,128]{3,2,1,0:T(8,128)S(1)}, u32[]{:S(2)}, u32[]{:S(2)}) collective-permute-start(f32[2,2,48,128]{3,2,1,0:T(8,128)S(1)} %get-tuple-element.48), channel_id=1, source_target_pairs={{0,8},{4,12},{8,0},{12,4},{1,9},{5,13},{9,1},{13,5},{2,10},{6,14},... | collective-permute-start | bytes 294920 | tf_op jit(solution)/shard_map/ppermute | solution.py:548
  33.0 2.4 %collective-permute-start.8 = (f32[2,2,48,128]{3,2,1,0:T(8,128)S(1)}, f32[2,2,48,128]{3,2,1,0:T(8,128)S(1)}, u32[]{:S(2)}, u32[]{:S(2)}) collective-permute-start(f32[2,2,48,128]{3,2,1,0:T(8,128)S(1)} %get-tuple-element.43), channel_id=1, source_target_pairs={{0,12},{4,0},{8,4},{12,8},{1,13},{5,1},{9,5},{13,9},{2,14},{6,2},{... | collective-permute-start | bytes 294920 | tf_op jit(solution)/shard_map/ppermute | solution.py:548
  35.4 0.0 collective-permute-done.4.lat_in_0__0_
  35.4 5.6 %shard_map.98 = (f32[2,2,48,128]{3,2,1,0:T(8,128)S(1)}, f32[2,2,48,128]{3,2,1,0:T(8,128)S(1)}, f32[2,2,48,128]{3,2,1,0:T(8,128)S(1)}, f32[2,2,48,128]{3,2,1,0:T(8,128)S(1)}) custom-call(s32[3]{0:T(128)S(1)} %pad_add_fusion.place, bf16[2,48,96]{2,1,0:T(8,128)(2,1)S(1)} %get-tuple-element.61.tables, bf16[20,2,96,256]{3,2,1,0:T(8,128)(2,1)S(1)} %get-tuple-element.35.faces, ...), custom_call_target="tpu_custom_call" | custom-call | bytes 23730000 | tf_op jit(solution)/shard_map/pallas_call | solution.py:514
  41.0 0.1 collective-permute-start.12
  41.1 0.0 collective-permute-done.11.pieces_2_.refs_3_.refs_7_
  41.1 2.3 %collective-permute-start.14 = (f32[2,2,48,128]{3,2,1,0:T(8,128)S(1)}, f32[2,2,48,128]{3,2,1,0:T(8,128)S(1)}, u32[]{:S(2)}, u32[]{:S(2)}) collective-permute-start(f32[2,2,48,128]{3,2,1,0:T(8,128)S(1)} %get-tuple-element.53), channel_id=1, source_target_pairs={{0,4},{4,8},{8,12},{12,0},{1,5},{5,9},{9,13},{13,1},{2,6},{6,10},{... | collective-permute-start | bytes 294920 | tf_op jit(solution)/shard_map/ppermute | solution.py:548
  43.4 0.0 collective-permute-start.15
  43.5 1.2 %collective-permute-start.16 = (f32[2,2,48,128]{3,2,1,0:T(8,128)S(1)}, f32[2,2,48,128]{3,2,1,0:T(8,128)S(1)}, u32[]{:S(2)}, u32[]{:S(2)}) collective-permute-start(f32[2,2,48,128]{3,2,1,0:T(8,128)S(1)} %get-tuple-element.55), channel_id=1, source_target_pairs={{0,12},{4,0},{8,4},{12,8},{1,13},{5,1},{9,5},{13,9},{2,14},{6,2},{... | collective-permute-start | bytes 294920 | tf_op jit(solution)/shard_map/ppermute | solution.py:548
  44.7 4.2 %shard_map.99.after_0_.matrix_t = bf16[2,1152,1152]{2,1,0:T(8,128)(2,1)S(1)} custom-call(s32[3]{0:T(128)S(1)} %pad_add_fusion.place, f32[2,4,1152]{2,1,0:T(4,128)S(1)} %convert_bitcast_fusion.index, f32[2,4,1152]{2,1,0:T(4,128)S(1)} %maximum_bitcast_fusion.weight, f32[2,2,48,128]{3,2,1,0:T(8,128)S(1)} %get-tuple-element.40.after.pieces_0_.refs_10_), custom_call_target="tpu_custom_call" | custom-call | bytes 14000000 | tf_op jit(solution)/shard_map/pallas_call | solution.py:556
  48.8 0.0 collective-permute-done.8.pieces_3_.refs_3_
  48.9 0.3 shard_map.100
  49.2 2.9 %collective-permute-start.9 = (f32[4,2,48,128]{3,2,1,0:T(8,128)S(1)}, f32[4,2,48,128]{3,2,1,0:T(8,128)S(1)}, u32[]{:S(2)}, u32[]{:S(2)}) collective-permute-start(f32[4,2,48,128]{3,2,1,0:T(8,128)S(1)} %shard_map.100), channel_id=1, source_target_pairs={{0,1},{1,0},{2,3},{3,2},{4,5},{5,4},{6,7},{7,6},{8,9},{9,8},{10,11... | collective-permute-start | bytes 589832 | tf_op jit(solution)/shard_map/ppermute | solution.py:578
  52.1 0.3 shard_map.102
  52.4 0.1 collective-permute-start.13
  52.5 0.3 shard_map.104
  52.8 0.8 collective-permute-start.17
  53.6 0.0 collective-permute-done.9.refs_4_
  53.6 0.3 collective-permute-done.13.refs_9_
  53.9 0.8 collective-permute-done.17.refs_14_
  54.6 2.5 %shard_map.105 = (f32[1152,256]{1,0:T(8,128)S(1)}, f32[1152,256]{1,0:T(8,128)S(1)}, bf16[1152,256]{1,0:T(8,128)(2,1)S(1)}) custom-call(s32[3]{0:T(128)S(1)} %pad_add_fusion.place, bf16[2,1152,1152]{2,1,0:T(8,128)(2,1)S(1)} %shard_map.93.refs_1_.after.matrix, f32[1152,1]{1,0:T(8,128)S(1)} %reshape_broadcast_in_dim.4.after_1_.coupling, ...), custom_call_target="tpu_custom_call" | custom-call | bytes 14000000 | tf_op jit(solution)/shard_map/pallas_call | solution.py:582
  57.2 0.6 shard_map.110
  57.8 0.6 shard_map.107
  58.4 1.3 %collective-permute-start.18 = (f32[2,288,128]{2,1,0:T(8,128)S(1)}, f32[2,288,128]{2,1,0:T(8,128)S(1)}, u32[]{:S(2)}, u32[]{:S(2)}) collective-permute-start(f32[2,288,128]{2,1,0:T(8,128)S(1)} %shard_map.107), channel_id=1, source_target_pairs={{0,8},{4,12},{8,0},{12,4},{1,9},{5,13},{9,1},{13,5},{2,10},{6,14},... | collective-permute-start | bytes 884744 | tf_op jit(solution)/shard_map/ppermute | solution.py:612
  59.6 0.6 shard_map.109
  60.2 2.5 %collective-permute-start.19 = (f32[2,288,128]{2,1,0:T(8,128)S(1)}, f32[2,288,128]{2,1,0:T(8,128)S(1)}, u32[]{:S(2)}, u32[]{:S(2)}) collective-permute-start(f32[2,288,128]{2,1,0:T(8,128)S(1)} %shard_map.109), channel_id=1, source_target_pairs={{0,12},{4,0},{8,4},{12,8},{1,13},{5,1},{9,5},{13,9},{2,14},{6,2},{... | collective-permute-start | bytes 884744 | tf_op jit(solution)/shard_map/ppermute | solution.py:612
  62.6 0.6 shard_map.106.refs_0_
  63.2 8.8 %collective-permute-done.18.refs_1_ = f32[2,288,128]{2,1,0:T(8,128)S(1)} collective-permute-done((f32[2,288,128]{2,1,0:T(8,128)S(1)}, f32[2,288,128]{2,1,0:T(8,128)S(1)}, u32[]{:S(2)}, u32[]{:S(2)}) %collective-permute-start.18) | collective-permute-done | bytes 294944 | tf_op jit(solution)/shard_map/ppermute | solution.py:612
  72.0 0.6 shard_map.108.held_0_
  72.6 12.0 %collective-permute-done.19.refs_0_ = f32[2,288,128]{2,1,0:T(8,128)S(1)} collective-permute-done((f32[2,288,128]{2,1,0:T(8,128)S(1)}, f32[2,288,128]{2,1,0:T(8,128)S(1)}, u32[]{:S(2)}, u32[]{:S(2)}) %collective-permute-start.19) | collective-permute-done | bytes 294944 | tf_op jit(solution)/shard_map/ppermute | solution.py:612
  84.6 2.6 %collective-permute-done.20.refs_1_ = f32[2,288,128]{2,1,0:T(8,128)S(1)} collective-permute-done((f32[2,288,128]{2,1,0:T(8,128)S(1)}, f32[2,288,128]{2,1,0:T(8,128)S(1)}, u32[]{:S(2)}, u32[]{:S(2)}) %collective-permute-start.20) | collective-permute-done | bytes 294944 | tf_op jit(solution)/shard_map/ppermute | solution.py:612
  87.3 1.7 %shard_map.111 = f32[2304,128]{1,0:T(8,128)} custom-call(s32[3]{0:T(128)S(1)} %pad_add_fusion.place, f32[2304,128]{1,0:T(8,128)S(1)} %shard_map.108.held_0_, f32[2,288,128]{2,1,0:T(8,128)S(1)} %collective-permute-done.19.refs_0_, f32[2,288,128]{2,1,0:T(8,128)S(1)} %collective-permute-done.20.refs_1_), custom_call_target="tpu_custom_call" | custom-call | bytes 3500000 | tf_op jit(solution)/shard_map/pallas_call | solution.py:617
  (30 shorter events, 0.2 us)
Async XLA Ops:
  0.0 2.6 %copy-start = (f32[16,32]{1,0:T(8,128)S(1)}, f32[16,32]{1,0:T(8,128)}, u32[]{:S(2)}) copy-start(f32[16,32]{1,0:T(8,128)} %param.13) | copy-start | bytes 6148
  0.0 2.4 %copy-start.5 = (f32[16,2]{0,1:T(2,128)S(1)}, f32[16,2]{0,1:T(2,128)}, u32[]{:S(2)}) copy-start(f32[16,2]{0,1:T(2,128)} %param.14) | copy-start | bytes 388
  0.0 2.6 %copy-start.2 = (s32[2,1152,4]{1,2,0:T(4,128)S(1)}, s32[2,1152,4]{1,2,0:T(4,128)}, u32[]{:S(2)}) copy-start(s32[2,1152,4]{1,2,0:T(4,128)} %param.16) | copy-start | bytes 110596
  0.0 2.9 %copy-start.3 = (f32[2,1152,4]{1,2,0:T(4,128)S(1)}, f32[2,1152,4]{1,2,0:T(4,128)}, u32[]{:S(2)}) copy-start(f32[2,1152,4]{1,2,0:T(4,128)} %param.17) | copy-start | bytes 110596
  0.0 3.3 %copy-start.4 = (f32[1152]{0:T(1024)S(1)}, f32[1152]{0:T(1024)}, u32[]{:S(2)}) copy-start(f32[1152]{0:T(1024)} %param.15) | copy-start | bytes 13828
  0.0 3.6 %copy-start.1 = (f32[288,8,128]{2,1,0:T(8,128)S(1)}, f32[288,8,128]{2,1,0:T(8,128)}, u32[]{:S(2)}) copy-start(f32[288,8,128]{2,1,0:T(8,128)} %param.9) | copy-start | bytes 3538948
  0.0 3.6 %collective-permute-start.2 = (f32[2304,128]{1,0:T(8,128)}, f32[2304,128]{1,0:T(8,128)S(1)}, u32[]{:S(2)}, u32[]{:S(2)}) collective-permute-start(f32[2304,128]{1,0:T(8,128)} %bitcast.26), channel_id=1, source_target_pairs={{0,1},{1,0},{2,3},{3,2},{4,5},{5,4},{6,7},{7,6},{8,9},{9,8},{10,11... | collective-permute-start | bytes 3538952 | tf_op jit(solution)/shard_map/ppermute | solution.py:405
  1.9 1.7 %collective-permute-start = (f32[24,128]{1,0:T(8,128)S(1)}, f32[24,128]{1,0:T(8,128)S(1)}, u32[]{:S(2)}, u32[]{:S(2)}) collective-permute-start(f32[24,128]{1,0:T(8,128)S(1)} %get-tuple-element.32.after_1_.own_0_), channel_id=1, source_target_pairs={{0,1},{1,0},{2,3},{3,2},{4,5},{5,4},{6,7},{7,6},{8,9},{9,8},{10,11... | collective-permute-start | bytes 36872 | tf_op jit(solution)/shard_map/ppermute | solution.py:405
  2.1 10.6 %collective-permute-start.1 = (f32[792,128]{1,0:T(8,128)S(1)}, f32[792,128]{1,0:T(8,128)S(1)}, u32[]{:S(2)}, u32[]{:S(2)}) collective-permute-start(f32[792,128]{1,0:T(8,128)S(1)} %get-tuple-element.33.after_0_), channel_id=1, source_target_pairs={{0,2},{2,0},{1,3},{3,1},{4,6},{6,4},{5,7},{7,5},{8,10},{10,8},{9,1... | collective-permute-start | bytes 1216520 | tf_op jit(solution)/shard_map/ppermute | solution.py:432
  12.7 2.9 %collective-permute-start.3 = (f32[792,128]{1,0:T(8,128)S(1)}, f32[792,128]{1,0:T(8,128)S(1)}, u32[]{:S(2)}, u32[]{:S(2)}) collective-permute-start(f32[792,128]{1,0:T(8,128)S(1)} %shard_map.94.received_0__0_.lat_in_0__0_), channel_id=1, source_target_pairs={{0,1},{1,0},{2,3},{3,2},{4,5},{5,4},{6,7},{7,6},{8,9},{9,8},{10,11... | collective-permute-start | bytes 1216520 | tf_op jit(solution)/shard_map/ppermute | solution.py:405
  13.9 10.8 %collective-permute-start.5 = (f32[768,128]{1,0:T(8,128)S(1)}, f32[768,128]{1,0:T(8,128)S(1)}, u32[]{:S(2)}, u32[]{:S(2)}) collective-permute-start(f32[768,128]{1,0:T(8,128)S(1)} %get-tuple-element.37), channel_id=1, source_target_pairs={{0,2},{2,0},{1,3},{3,1},{4,6},{6,4},{5,7},{7,5},{8,10},{10,8},{9,1... | collective-permute-start | bytes 1179656 | tf_op jit(solution)/shard_map/ppermute | solution.py:432
  14.4 21.1 %collective-permute-start.4 = (f32[768,128]{1,0:T(8,128)S(1)}, f32[768,128]{1,0:T(8,128)S(1)}, u32[]{:S(2)}, u32[]{:S(2)}) collective-permute-start(f32[768,128]{1,0:T(8,128)S(1)} %get-tuple-element.34.after_0_), channel_id=1, source_target_pairs={{0,2},{2,0},{1,3},{3,1},{4,6},{6,4},{5,7},{7,5},{8,10},{10,8},{9,1... | collective-permute-start | bytes 1179656 | tf_op jit(solution)/shard_map/ppermute | solution.py:432
  22.1 8.2 %collective-permute-start.6 = (f32[2,2,48,128]{3,2,1,0:T(8,128)S(1)}, f32[2,2,48,128]{3,2,1,0:T(8,128)S(1)}, u32[]{:S(2)}, u32[]{:S(2)}) collective-permute-start(f32[2,2,48,128]{3,2,1,0:T(8,128)S(1)} %get-tuple-element.41), channel_id=1, source_target_pairs={{0,4},{4,8},{8,12},{12,0},{1,5},{5,9},{9,13},{13,1},{2,6},{6,10},{... | collective-permute-start | bytes 294920 | tf_op jit(solution)/shard_map/ppermute | solution.py:548
  23.5 6.9 %collective-permute-start.7 = (f32[2,2,48,128]{3,2,1,0:T(8,128)S(1)}, f32[2,2,48,128]{3,2,1,0:T(8,128)S(1)}, u32[]{:S(2)}, u32[]{:S(2)}) collective-permute-start(f32[2,2,48,128]{3,2,1,0:T(8,128)S(1)} %get-tuple-element.42), channel_id=1, source_target_pairs={{0,8},{4,12},{8,0},{12,4},{1,9},{5,13},{9,1},{13,5},{2,10},{6,14},... | collective-permute-start | bytes 294920 | tf_op jit(solution)/shard_map/ppermute | solution.py:548
  30.4 10.7 %collective-permute-start.10 = (f32[2,2,48,128]{3,2,1,0:T(8,128)S(1)}, f32[2,2,48,128]{3,2,1,0:T(8,128)S(1)}, u32[]{:S(2)}, u32[]{:S(2)}) collective-permute-start(f32[2,2,48,128]{3,2,1,0:T(8,128)S(1)} %get-tuple-element.47), channel_id=1, source_target_pairs={{0,4},{4,8},{8,12},{12,0},{1,5},{5,9},{9,13},{13,1},{2,6},{6,10},{... | collective-permute-start | bytes 294920 | tf_op jit(solution)/shard_map/ppermute | solution.py:548
  31.8 9.4 %collective-permute-start.11 = (f32[2,2,48,128]{3,2,1,0:T(8,128)S(1)}, f32[2,2,48,128]{3,2,1,0:T(8,128)S(1)}, u32[]{:S(2)}, u32[]{:S(2)}) collective-permute-start(f32[2,2,48,128]{3,2,1,0:T(8,128)S(1)} %get-tuple-element.48), channel_id=1, source_target_pairs={{0,8},{4,12},{8,0},{12,4},{1,9},{5,13},{9,1},{13,5},{2,10},{6,14},... | collective-permute-start | bytes 294920 | tf_op jit(solution)/shard_map/ppermute | solution.py:548
  33.0 15.8 %collective-permute-start.8 = (f32[2,2,48,128]{3,2,1,0:T(8,128)S(1)}, f32[2,2,48,128]{3,2,1,0:T(8,128)S(1)}, u32[]{:S(2)}, u32[]{:S(2)}) collective-permute-start(f32[2,2,48,128]{3,2,1,0:T(8,128)S(1)} %get-tuple-element.43), channel_id=1, source_target_pairs={{0,12},{4,0},{8,4},{12,8},{1,13},{5,1},{9,5},{13,9},{2,14},{6,2},{... | collective-permute-start | bytes 294920 | tf_op jit(solution)/shard_map/ppermute | solution.py:548
  41.0 11.0 %collective-permute-start.12 = (f32[2,2,48,128]{3,2,1,0:T(8,128)S(1)}, f32[2,2,48,128]{3,2,1,0:T(8,128)S(1)}, u32[]{:S(2)}, u32[]{:S(2)}) collective-permute-start(f32[2,2,48,128]{3,2,1,0:T(8,128)S(1)} %get-tuple-element.49), channel_id=1, source_target_pairs={{0,12},{4,0},{8,4},{12,8},{1,13},{5,1},{9,5},{13,9},{2,14},{6,2},{... | collective-permute-start | bytes 294920 | tf_op jit(solution)/shard_map/ppermute | solution.py:548
  41.1 11.3 %collective-permute-start.14 = (f32[2,2,48,128]{3,2,1,0:T(8,128)S(1)}, f32[2,2,48,128]{3,2,1,0:T(8,128)S(1)}, u32[]{:S(2)}, u32[]{:S(2)}) collective-permute-start(f32[2,2,48,128]{3,2,1,0:T(8,128)S(1)} %get-tuple-element.53), channel_id=1, source_target_pairs={{0,4},{4,8},{8,12},{12,0},{1,5},{5,9},{9,13},{13,1},{2,6},{6,10},{... | collective-permute-start | bytes 294920 | tf_op jit(solution)/shard_map/ppermute | solution.py:548
  43.4 9.0 %collective-permute-start.15 = (f32[2,2,48,128]{3,2,1,0:T(8,128)S(1)}, f32[2,2,48,128]{3,2,1,0:T(8,128)S(1)}, u32[]{:S(2)}, u32[]{:S(2)}) collective-permute-start(f32[2,2,48,128]{3,2,1,0:T(8,128)S(1)} %get-tuple-element.54), channel_id=1, source_target_pairs={{0,8},{4,12},{8,0},{12,4},{1,9},{5,13},{9,1},{13,5},{2,10},{6,14},... | collective-permute-start | bytes 294920 | tf_op jit(solution)/shard_map/ppermute | solution.py:548
  43.5 9.0 %collective-permute-start.16 = (f32[2,2,48,128]{3,2,1,0:T(8,128)S(1)}, f32[2,2,48,128]{3,2,1,0:T(8,128)S(1)}, u32[]{:S(2)}, u32[]{:S(2)}) collective-permute-start(f32[2,2,48,128]{3,2,1,0:T(8,128)S(1)} %get-tuple-element.55), channel_id=1, source_target_pairs={{0,12},{4,0},{8,4},{12,8},{1,13},{5,1},{9,5},{13,9},{2,14},{6,2},{... | collective-permute-start | bytes 294920 | tf_op jit(solution)/shard_map/ppermute | solution.py:548
  49.2 4.4 %collective-permute-start.9 = (f32[4,2,48,128]{3,2,1,0:T(8,128)S(1)}, f32[4,2,48,128]{3,2,1,0:T(8,128)S(1)}, u32[]{:S(2)}, u32[]{:S(2)}) collective-permute-start(f32[4,2,48,128]{3,2,1,0:T(8,128)S(1)} %shard_map.100), channel_id=1, source_target_pairs={{0,1},{1,0},{2,3},{3,2},{4,5},{5,4},{6,7},{7,6},{8,9},{9,8},{10,11... | collective-permute-start | bytes 589832 | tf_op jit(solution)/shard_map/ppermute | solution.py:578
  52.4 1.5 %collective-permute-start.13 = (f32[4,2,48,128]{3,2,1,0:T(8,128)S(1)}, f32[4,2,48,128]{3,2,1,0:T(8,128)S(1)}, u32[]{:S(2)}, u32[]{:S(2)}) collective-permute-start(f32[4,2,48,128]{3,2,1,0:T(8,128)S(1)} %shard_map.102), channel_id=1, source_target_pairs={{0,1},{1,0},{2,3},{3,2},{4,5},{5,4},{6,7},{7,6},{8,9},{9,8},{10,11... | collective-permute-start | bytes 589832 | tf_op jit(solution)/shard_map/ppermute | solution.py:578
  52.8 1.9 %collective-permute-start.17 = (f32[4,2,48,128]{3,2,1,0:T(8,128)S(1)}, f32[4,2,48,128]{3,2,1,0:T(8,128)S(1)}, u32[]{:S(2)}, u32[]{:S(2)}) collective-permute-start(f32[4,2,48,128]{3,2,1,0:T(8,128)S(1)} %shard_map.104), channel_id=1, source_target_pairs={{0,1},{1,0},{2,3},{3,2},{4,5},{5,4},{6,7},{7,6},{8,9},{9,8},{10,11... | collective-permute-start | bytes 589832 | tf_op jit(solution)/shard_map/ppermute | solution.py:578
  58.4 13.6 %collective-permute-start.18 = (f32[2,288,128]{2,1,0:T(8,128)S(1)}, f32[2,288,128]{2,1,0:T(8,128)S(1)}, u32[]{:S(2)}, u32[]{:S(2)}) collective-permute-start(f32[2,288,128]{2,1,0:T(8,128)S(1)} %shard_map.107), channel_id=1, source_target_pairs={{0,8},{4,12},{8,0},{12,4},{1,9},{5,13},{9,1},{13,5},{2,10},{6,14},... | collective-permute-start | bytes 884744 | tf_op jit(solution)/shard_map/ppermute | solution.py:612
  60.2 24.4 %collective-permute-start.19 = (f32[2,288,128]{2,1,0:T(8,128)S(1)}, f32[2,288,128]{2,1,0:T(8,128)S(1)}, u32[]{:S(2)}, u32[]{:S(2)}) collective-permute-start(f32[2,288,128]{2,1,0:T(8,128)S(1)} %shard_map.109), channel_id=1, source_target_pairs={{0,12},{4,0},{8,4},{12,8},{1,13},{5,1},{9,5},{13,9},{2,14},{6,2},{... | collective-permute-start | bytes 884744 | tf_op jit(solution)/shard_map/ppermute | solution.py:612
  62.6 24.6 %collective-permute-start.20 = (f32[2,288,128]{2,1,0:T(8,128)S(1)}, f32[2,288,128]{2,1,0:T(8,128)S(1)}, u32[]{:S(2)}, u32[]{:S(2)}) collective-permute-start(f32[2,288,128]{2,1,0:T(8,128)S(1)} %shard_map.110), channel_id=1, source_target_pairs={{0,4},{4,8},{8,12},{12,0},{1,5},{5,9},{9,13},{13,1},{2,6},{6,10},{... | collective-permute-start | bytes 884744 | tf_op jit(solution)/shard_map/ppermute | solution.py:612
